TPU v7x, 32 devices: a whole 2x2x4 slice. The times are simulated.
32 devices in a mesh: groups: 2 (over x), ctx: 8 (over z, y), head: 2 (over core).
Axes of the slice: x: 2, y: 2, z: 4, core: 2. Of those that a mesh axis runs over, the one named last changes fastest.
Arguments:
- queries: bfloat16 [2048, 12288], P(('groups', 'ctx'), 'head'), parts along dimension 0, may hold values from -32 to 32
- span_latents: bfloat16 [2048, 576], P(('groups', 'ctx')), parts along dimension 0, may hold values from -600 to 600
- cache_latents: bfloat16 [256, 576], P(('groups', 'ctx')), parts along dimension 0, may hold values from -32 to 32
- latent_gain: float32 [512], replicated, may hold values from 0.1 to 1.9
- key_weight: bfloat16 [512, 8192], P(None, 'head'), may hold values from -0.25 to 0.25
- value_weight: bfloat16 [512, 8192], P(None, 'head'), may hold values from -0.25 to 0.25
- prefix_length: int32 [2], P('groups'), parts along dimension 0, may hold values from 64 to 128
- block_order: int32 [16], P('groups'), parts along dimension 0, may hold values from 0 to 7, each once
Outputs:
- attended: bfloat16 [2048, 8192], P(('groups', 'ctx'), 'head'), parts along dimension 0
There are 2 independent parts, one for each index of `groups`. A program takes and returns all parts, laid end to end along the dimension named above; an argument that names none is the same for every part. Nothing has to cross between parts.
Inputs may be any that keep to these rules, and one draw needn't show every extreme that they name: Cache slots 0 to prefix_length[0] - 1 hold the prefix. A permutation; shard c of ctx holds span positions block_order[c] * 128 to block_order[c] * 128 + 127.
All inputs are finite; a program needn't handle non-finite values.
Results may differ from a plain program's by a relative error of at most 0.0076.
Values may be sent and summed in bfloat16 or wider, within the bound.
No kernel may reach another device: no remote copies, remote signals or barrier semaphores. Data moves between devices by JAX's collectives and lax.ppermute only.
A program may use at most 64 MiB of HBM per device.

v0:
```python
import math

import jax
import jax.numpy as jnp
from jax import lax
from jax.sharding import PartitionSpec as P

LATENT = 512
ROPE = 64
NOPE = 128
VDIM = 128


def span_rows(span_latents, latent_gain):
    raw_rows = span_latents.astype(jnp.float32)
    latent = raw_rows[:, :LATENT]
    mean_square = jnp.mean(latent * latent, axis=1, keepdims=True)
    normed = latent * lax.rsqrt(mean_square + 1e-06) * latent_gain[None, :]
    return jnp.concatenate([normed, raw_rows[:, LATENT:]], axis=1).astype(jnp.bfloat16)


def block_lookup(source, block_order):
    shard_ids = jnp.arange(block_order.shape[0], dtype=jnp.int32)
    picked = jnp.where(source[:, None] == shard_ids[None, :], block_order[None, :], 0)
    return jnp.sum(picked, axis=1)


def attend(query_head, key_full, values, query_pos, key_pos):
    query_count = query_head.shape[0]
    row_block = 512
    score_scale = 1.0 / math.sqrt(query_head.shape[1])

    def one_block(block_index):
        first_row = block_index * row_block
        query_part = lax.dynamic_slice_in_dim(query_head, first_row, row_block, 0)
        pos_part = lax.dynamic_slice_in_dim(query_pos, first_row, row_block, 0)
        scores = (
            lax.dot_general(
                query_part, key_full, (((1,), (1,)), ((), ())), preferred_element_type=jnp.float32
            )
            * score_scale
        )
        scores = jnp.where(key_pos[None, :] <= pos_part[:, None], scores, -1e30)
        row_max = jnp.max(scores, axis=1, keepdims=True)
        exponent = jnp.exp(scores - row_max)
        weight_sum = jnp.sum(exponent, axis=1, keepdims=True)
        weights = exponent.astype(jnp.bfloat16)
        head_mixed = jnp.dot(weights, values, preferred_element_type=jnp.float32) / weight_sum
        return head_mixed.astype(jnp.bfloat16)

    blocks = lax.map(one_block, jnp.arange(query_count // row_block, dtype=jnp.int32))
    return blocks.reshape(query_count, values.shape[1])


def per_device(
    queries,
    span_latents,
    cache_latents,
    latent_gain,
    key_weight,
    value_weight,
    prefix_length,
    block_order,
):
    shard_count = lax.axis_size("ctx")
    position = lax.axis_index("ctx")
    tok_rows = queries.shape[0]
    cache_rows = cache_latents.shape[0]
    own_count = tok_rows + cache_rows
    qk_width = NOPE + ROPE
    group_heads = key_weight.shape[1] // NOPE
    my_heads = group_heads // shard_count
    own_rows = jnp.concatenate([span_rows(span_latents, latent_gain), cache_latents], axis=0)
    query_split = queries.reshape(tok_rows, shard_count, my_heads * qk_width)
    w_key = lax.dynamic_slice_in_dim(key_weight, position * (my_heads * NOPE), my_heads * NOPE, 1)
    w_value = lax.dynamic_slice_in_dim(
        value_weight, position * (my_heads * VDIM), my_heads * VDIM, 1
    )
    query_here = lax.all_to_all(query_split, "ctx", split_axis=1, concat_axis=0, tiled=True)
    piece = lax.all_gather(own_rows, "ctx", axis=0, tiled=True)
    latent_piece = piece[:, :LATENT]
    key_part = jnp.dot(latent_piece, w_key, preferred_element_type=jnp.float32).astype(jnp.bfloat16)
    value_part = jnp.dot(latent_piece, w_value, preferred_element_type=jnp.float32).astype(
        jnp.bfloat16
    )
    gathered = jnp.concatenate([key_part, value_part, piece[:, LATENT:]], axis=1)
    key_nope = gathered[:, : my_heads * NOPE]
    values = gathered[:, my_heads * NOPE : my_heads * (NOPE + VDIM)]
    rotary = gathered[:, my_heads * (NOPE + VDIM) :]
    query_here = query_here.reshape(shard_count * tok_rows, my_heads * qk_width)
    row_index = jnp.arange(shard_count * tok_rows, dtype=jnp.int32)
    query_pos = block_lookup(row_index // tok_rows, block_order) * tok_rows + row_index % tok_rows
    key_index = jnp.arange(shard_count * own_count, dtype=jnp.int32)
    source = key_index // own_count
    local_row = key_index % own_count
    span_pos = block_lookup(source, block_order) * tok_rows + local_row
    slot_index = source * cache_rows + local_row - tok_rows
    cache_pos = jnp.where(slot_index < prefix_length[0], -1, tok_rows * shard_count)
    key_pos = jnp.where(local_row < tok_rows, span_pos, cache_pos)
    results = []
    for head_number in range(my_heads):
        query_head = query_here[:, head_number * qk_width : (head_number + 1) * qk_width]
        key_full = jnp.concatenate(
            [key_nope[:, head_number * NOPE : (head_number + 1) * NOPE], rotary], axis=1
        )
        head_values = values[:, head_number * VDIM : (head_number + 1) * VDIM]
        results.append(attend(query_head, key_full, head_values, query_pos, key_pos))
    mixed_heads = jnp.concatenate(results, axis=1)
    returned = lax.all_to_all(
        mixed_heads.reshape(shard_count * tok_rows, 1, my_heads * VDIM),
        "ctx",
        split_axis=0,
        concat_axis=1,
        tiled=True,
    )
    return returned.reshape(tok_rows, group_heads * VDIM)


def solution(mesh):
    return jax.shard_map(
        per_device,
        mesh=mesh,
        in_specs=(
            P(("groups", "ctx"), "head"),
            P(("groups", "ctx"), None),
            P(("groups", "ctx"), None),
            P(),
            P(None, "head"),
            P(None, "head"),
            P("groups"),
            P("groups"),
        ),
        out_specs=P(("groups", "ctx"), "head"),
        check_vma=False,
    )
```

profile of v0, /device:TPU:0, one launch (start us, length us, event | category | flops | bytes accessed | tf_op | source)
XLA Modules:
  0.0 159.3 jit_solution(15011479043573403967)
XLA Ops:
  6.5 0.9 slice.53
  7.5 0.7 slice.55
  8.4 0.1 copy.63
  8.5 0.8 fusion.86
  9.3 1.4 pad_maximum_fusion.4
  10.8 2.7 %copy.67 = bf16[16,8,8,768]{3,2,0,1:T(8,128)(2,1)} copy(bf16[16,8,8,768]{3,2,1,0:T(8,128)(2,1)} %bitcast.84) | data formatting | bytes 3145728 | tf_op jit(solution)/shard_map/reshape | solution.py:74
  13.5 7.4 %all-to-all-start = ((bf16[128,8,768]{2,0,1:T(8,128)(2,1)}), bf16[128,8,768]{2,0,1:T(8,128)(2,1)S(1)}, u32[]{:S(2)}, u32[]{:S(2)}) async-start(bf16[128,8,768]{2,0,1:T(8,128)(2,1)} %bitcast.47), calls=%async_computation | async-start | bytes 3145728 | tf_op jit(solution)/shard_map/all_to_all | solution.py:79
  21.8 55.2 %all-gather.2.cloned.1.call-done = bf16[1152,576]{1,0:T(8,128)(2,1)} async-done(((bf16[144,576]{1,0:T(8,128)(2,1)}), bf16[1152,576]{1,0:T(8,128)(2,1)}) %all-gather.2.cloned.1.call-update) | async-done | bytes 1327120 | tf_op jit(solution)/shard_map/all_gather | solution.py:80
  77.0 1.0 slice.72
  78.0 0.2 copy.64
  78.1 2.3 %convolution_convert_fusion.1 = bf16[1152,512]{0,1:T(8,128)(2,1)S(1)} fusion(bf16[1152,576]{1,0:T(8,128)(2,1)} %all-gather.2.cloned.1.call-done, bf16[512,4096]{1,0:T(8,128)(2,1)} %param.20, s32[]{:T(128)S(6)} %select_n.94), kind=kOutput, calls=%fused_computation.53 | convolution fusion | flops 604569600 | bytes 2883588 | tf_op jit(solution)/shard_map/dot_general | solution.py:82
  80.5 0.1 pad_maximum_fusion.3
  80.7 1.1 copy.54
  81.7 1.1 copy.55
  82.8 0.2 copy.56
  83.0 0.2 copy.57
  83.3 2.2 %convolution_convert_fusion = bf16[1152,512]{1,0:T(8,128)(2,1)S(1)} fusion(bf16[1152,576]{1,0:T(8,128)(2,1)} %all-gather.2.cloned.1.call-done, bf16[512,4096]{1,0:T(8,128)(2,1)} %param.21, s32[]{:T(128)S(6)} %select_n.94), kind=kOutput, calls=%fused_computation.52 | convolution fusion | flops 604569600 | bytes 2883588 | tf_op jit(solution)/shard_map/dot_general | solution.py:83
  85.5 1.1 fusion.108
  86.6 1.5 fusion.107
  88.2 8.7 %while.40 = (s32[]{:T(128)}, bf16[2,512,128]{2,1,0:T(8,128)(2,1)S(1)}, s32[1152]{0:T(1024)S(1)}, s32[2]{0:T(128)S(1)}, s32[1024]{0:T(1024)S(1)}, /*index=5*/bf16...) while((s32[]{:T(128)}, ...), condition=%wide.region_6.7_spmd, body=%wide.region_3.6_spmd.sunk | while | flops 382336000 | bytes 9412823 | solution.py:51
  88.2 0.7 dynamic_slice.78
  89.6 1.8 %fusion.145 = (f32[512]{0:T(512)S(1)}, f32[512,1152]{1,0:T(8,128)S(1)}) fusion(bf16[1152,192]{1,0:T(8,128)(2,1)} %get-tuple-element.807, bf16[1024,192]{1,0:T(8,128)(2,1)S(1)} %get-tuple-element.806, s32[]{:T(128)S(6)} %select_n.125, s32[512]{0:T(512)S(1)} %dynamic_slice.79, s32[1152]{0:T(1024)S(1)} %get-tuple-element.803), kind=kOutput, calls=%fused_computation.102.clone.1 | convolution fusion | flops 228851200 | bytes 3076100 | tf_op jit(solution)/shard_map/while/body/eval_jaxpr/dot_general | solution.py:38
  91.4 0.5 fusion.146
  92.0 0.6 fusion.147
  92.6 0.7 dynamic_slice.78
  94.0 1.8 %fusion.145 = (f32[512]{0:T(512)S(1)}, f32[512,1152]{1,0:T(8,128)S(1)}) fusion(bf16[1152,192]{1,0:T(8,128)(2,1)} %get-tuple-element.807, bf16[1024,192]{1,0:T(8,128)(2,1)S(1)} %get-tuple-element.806, s32[]{:T(128)S(6)} %select_n.125, s32[512]{0:T(512)S(1)} %dynamic_slice.79, s32[1152]{0:T(1024)S(1)} %get-tuple-element.803), kind=kOutput, calls=%fused_computation.102.clone.1 | convolution fusion | flops 228851200 | bytes 3076100 | tf_op jit(solution)/shard_map/while/body/eval_jaxpr/dot_general | solution.py:38
  95.8 0.5 fusion.146
  96.3 0.6 fusion.147
  97.0 8.3 %while.41 = (s32[]{:T(128)}, bf16[2,512,128]{2,1,0:T(8,128)(2,1)S(1)}, s32[1152]{0:T(1024)S(1)}, s32[2]{0:T(128)S(1)}, s32[1024]{0:T(1024)S(1)}, /*index=5*/bf16...) while((s32[]{:T(128)}, ...), condition=%wide.region_10.11_spmd, body=%wide.region_7.10_spmd.sunk | while | flops 382336000 | bytes 9409239 | solution.py:51
  97.0 0.6 dynamic_slice.81
  98.3 1.7 %fusion.151 = (f32[512]{0:T(512)S(1)}, f32[512,1152]{1,0:T(8,128)S(1)}) fusion(bf16[1152,192]{1,0:T(8,128)(2,1)S(1)} %get-tuple-element.771, bf16[1024,192]{1,0:T(8,128)(2,1)} %get-tuple-element.770, s32[]{:T(128)S(6)} %select_n.126, s32[512]{0:T(512)S(1)} %dynamic_slice.82, s32[1152]{0:T(1024)S(1)} %get-tuple-element.767), kind=kOutput, calls=%fused_computation.103.clone.1 | convolution fusion | flops 228851200 | bytes 3072516 | tf_op jit(solution)/shard_map/while/body/eval_jaxpr/dot_general | solution.py:38
  100.0 0.5 fusion.152
  100.5 0.6 fusion.153
  101.1 0.6 dynamic_slice.81
  102.4 1.7 %fusion.151 = (f32[512]{0:T(512)S(1)}, f32[512,1152]{1,0:T(8,128)S(1)}) fusion(bf16[1152,192]{1,0:T(8,128)(2,1)S(1)} %get-tuple-element.771, bf16[1024,192]{1,0:T(8,128)(2,1)} %get-tuple-element.770, s32[]{:T(128)S(6)} %select_n.126, s32[512]{0:T(512)S(1)} %dynamic_slice.82, s32[1152]{0:T(1024)S(1)} %get-tuple-element.767), kind=kOutput, calls=%fused_computation.103.clone.1 | convolution fusion | flops 228851200 | bytes 3072516 | tf_op jit(solution)/shard_map/while/body/eval_jaxpr/dot_general | solution.py:38
  104.1 0.5 fusion.152
  104.7 0.6 fusion.153
  105.3 6.3 %while.42 = (s32[]{:T(128)}, bf16[2,512,128]{2,1,0:T(8,128)(2,1)S(1)}, s32[1152]{0:T(1024)S(1)}, s32[2]{0:T(128)S(1)}, s32[1024]{0:T(1024)S(1)}, /*index=5*/bf16...) while((s32[]{:T(128)}, ...), condition=%wide.region_14.15_spmd, body=%wide.region_11.14_spmd.sunk | while | flops 382336000 | bytes 9560279 | solution.py:51
  105.3 0.6 dynamic_slice.84
  106.6 0.7 fusion.157
  107.3 0.5 fusion.158
  107.9 0.6 fusion.159
  108.5 0.6 dynamic_slice.84
  109.8 0.7 fusion.157
  110.5 0.5 fusion.158
  111.0 0.6 fusion.159
  111.6 6.3 %while.43 = (s32[]{:T(128)}, bf16[2,512,128]{2,1,0:T(8,128)(2,1)S(1)}, s32[1152]{0:T(1024)S(1)}, s32[2]{0:T(128)S(1)}, s32[1024]{0:T(1024)S(1)}, /*index=5*/bf16...) while((s32[]{:T(128)}, ...), condition=%wide.region_18.19_spmd, body=%wide.region_15.18_spmd.sunk | while | flops 382336000 | bytes 9560279 | solution.py:51
  111.7 0.6 dynamic_slice.87
  113.0 0.7 fusion.163
  113.7 0.5 fusion.164
  114.2 0.6 fusion.165
  114.8 0.6 dynamic_slice.87
  116.1 0.7 fusion.163
  116.8 0.5 fusion.164
  117.3 0.6 fusion.165
  117.9 0.1 maximum_bitcast_fusion
  118.0 0.5 broadcast.116
  118.6 1.5 reduce
  120.0 0.8 reshape.94
  120.8 28.3 %all_to_all.30 = bf16[8,2,32768]{2,1,0:T(2,128)(2,1)S(1)} all-to-all(bf16[8,2,32768]{2,1,0:T(2,128)(2,1)S(1)} %reshape.94), channel_id=1, replica_groups=mesh['groups'=2,'ctx'=8,'head'=2] {'ctx'}, dimensions={0} | all-to-all | bytes 2097152 | tf_op jit(solution)/shard_map/all_to_all | solution.py:109
  149.1 1.0 reshape.95
  150.2 0.3 copy.61
  150.5 0.7 copy.59
  151.1 1.3 copy.60
  (53 shorter events, 1.4 us)
Async XLA Ops:
  6.5 70.4 %all-gather.2.cloned.1.call-start = ((), (), s32[]{:S(2)}) async-start(), calls=%async_computation.2 | async-start | bytes 1658880 | tf_op jit(solution)/shard_map/all_gather | solution.py:80
  13.5 8.1 %copy-start.7 = (s32[8]{0:T(128)S(1)}, s32[8]{0:T(128)}, u32[]{:S(2)}) copy-start(s32[8]{0:T(128)} %param.23) | copy-start | bytes 100
  13.5 73.2 %all-to-all-start = ((bf16[128,8,768]{2,0,1:T(8,128)(2,1)}), bf16[128,8,768]{2,0,1:T(8,128)(2,1)S(1)}, u32[]{:S(2)}, u32[]{:S(2)}) async-start(bf16[128,8,768]{2,0,1:T(8,128)(2,1)} %bitcast.47), calls=%async_computation | async-start | bytes 3145728 | tf_op jit(solution)/shard_map/all_to_all | solution.py:79
  88.2 8.7 %copy-start = (bf16[1152,192]{1,0:T(8,128)(2,1)S(1)}, bf16[1152,192]{1,0:T(8,128)(2,1)}, u32[]{:S(2)}) copy-start(bf16[1152,192]{1,0:T(8,128)(2,1)} %copy.55) | copy-start | bytes 1327108
  89.6 2.3 %copy-start.6 = (bf16[1152,128]{1,0:T(8,128)(2,1)S(1)}, bf16[1152,128]{1,0:T(8,128)(2,1)}, u32[]{:S(2)}) copy-start(bf16[1152,128]{1,0:T(8,128)(2,1)} %get-tuple-element.808) | copy-start | bytes 884740 | tf_op jit(solution)/shard_map/while
  94.0 2.3 %copy-start.6 = (bf16[1152,128]{1,0:T(8,128)(2,1)S(1)}, bf16[1152,128]{1,0:T(8,128)(2,1)}, u32[]{:S(2)}) copy-start(bf16[1152,128]{1,0:T(8,128)(2,1)} %get-tuple-element.808) | copy-start | bytes 884740 | tf_op jit(solution)/shard_map/while
  97.0 8.3 %copy-start.2 = (bf16[1024,192]{1,0:T(8,128)(2,1)S(1)}, bf16[1024,192]{1,0:T(8,128)(2,1)}, u32[]{:S(2)}) copy-start(bf16[1024,192]{1,0:T(8,128)(2,1)} %get-tuple-element.710) | copy-start | bytes 1179652
  98.3 2.2 %copy-start.5 = (bf16[1152,128]{1,0:T(8,128)(2,1)S(1)}, bf16[1152,128]{1,0:T(8,128)(2,1)}, u32[]{:S(2)}) copy-start(bf16[1152,128]{1,0:T(8,128)(2,1)} %get-tuple-element.772) | copy-start | bytes 884740 | tf_op jit(solution)/shard_map/while
  102.4 2.2 %copy-start.5 = (bf16[1152,128]{1,0:T(8,128)(2,1)S(1)}, bf16[1152,128]{1,0:T(8,128)(2,1)}, u32[]{:S(2)}) copy-start(bf16[1152,128]{1,0:T(8,128)(2,1)} %get-tuple-element.772) | copy-start | bytes 884740 | tf_op jit(solution)/shard_map/while
  105.3 6.3 %copy-start.1 = (bf16[1024,192]{1,0:T(8,128)(2,1)S(1)}, bf16[1024,192]{1,0:T(8,128)(2,1)}, u32[]{:S(2)}) copy-start(bf16[1024,192]{1,0:T(8,128)(2,1)} %get-tuple-element.674) | copy-start | bytes 1179652
  106.6 1.2 copy-start.4
  109.8 1.2 copy-start.4
  113.0 1.2 copy-start.3
  116.1 1.2 copy-start.3
Sparse Core Ops, SparseCore 0:
  10.9 66.0 all-gather.1
where the time goes:
time: 160 us; the launch traced here: 159 us
  waiting for transfers between devices  55.2 us (34%)
  blocking collectives  28.3 us (18%)
  local copies, waits for them, and re-layouts  21.3 us (13%)
  matrix products  18.7 us (12%)
  between operations  14.3 us (9%)
  other arithmetic  8.5 us (5%)
  starting transfers between devices  7.41 us (5%)
  loops' own time  5.5 us (3%)
    all_gather x1, waiting for transfers between devices, per_device(): piece = lax.all_gather(own_rows, 'ctx', axis=0, tiled=True)  55.2 us
    all_to_all x1, blocking collectives, per_device(): lax.all_to_all(mixed_heads.reshape(shard_count * tok_rows, 1, my_heads *...  28.3 us
    dot_general x8, matrix products, one_block(): lax.dot_general(query_part, key_full, (((1,), (1,)), ((), ())), preferred...  9.69 us
    all_to_all x1, starting transfers between devices, per_device(): lax.all_to_all(query_split, 'ctx', split_axis=1, concat_axis=0, tiled=True)  7.41 us
    another operation x4, loops' own time, attend(): lax.map(one_block, jnp.arange(query_count // row_block, dtype=jnp.int32))  5.5 us
    dynamic_slice x8, local copies, waits for them, and re-layouts, attend(): lax.map(one_block, jnp.arange(query_count // row_block, dtype=jnp.int32))  4.82 us
    dot_general x8, matrix products, one_block(): jnp.dot(weights, values, preferred_element_type=jnp.float32) / weight_sum  4.53 us
    reduce_sum x8, other arithmetic, one_block(): weight_sum = jnp.sum(exponent, axis=1, keepdims=True)  4.28 us
  transfers between devices with their start and end apart: 2, of which 1 were waited for; matrix products, arithmetic and copies ran while one was open for 8% of the time, Pallas kernels for 0%

commit v1 on v0

v1 whole, which is shorter than its diff:
```python
import functools
import math

import jax
import jax.numpy as jnp
from jax import lax
from jax.experimental import pallas as pl
from jax.experimental.pallas import tpu as pltpu
from jax.sharding import PartitionSpec as P

LATENT = 512
ROPE = 64
NOPE = 128
VDIM = 128
PACKED = 640
QK = 256
NEG = -1e30
AXES = ("ctx", "head")
BF = jnp.bfloat16
F32 = jnp.float32


def vmem_spec():
    return pl.BlockSpec(memory_space=pltpu.VMEM)


def smem_spec():
    return pl.BlockSpec(memory_space=pltpu.SMEM)


def any_spec():
    return pl.BlockSpec(memory_space=pl.ANY)


def pack_kernel(shard_count, order_ref, prefix_ref, span_ref, cache_ref, gain_ref, out_ref):
    tok_rows = span_ref.shape[0]
    cache_rows = cache_ref.shape[0]
    me = lax.axis_index("ctx")
    latent = span_ref[:, :LATENT].astype(F32)
    mean_square = jnp.mean(latent * latent, axis=1, keepdims=True)
    normed = latent * lax.rsqrt(mean_square + 1e-06) * gain_ref[...]
    out_ref[:tok_rows, :LATENT] = normed.astype(BF)
    out_ref[tok_rows:, :LATENT] = cache_ref[:, :LATENT]
    lanes = lax.broadcasted_iota(jnp.int32, (tok_rows, 128), 1)
    out_ref[:tok_rows, LATENT:] = jnp.where(lanes == ROPE + order_ref[me], 1.0, 0.0).astype(BF)
    out_ref[:tok_rows, LATENT : LATENT + ROPE] = span_ref[:, LATENT:]
    lanes = lax.broadcasted_iota(jnp.int32, (cache_rows, 128), 1)
    slots = me * cache_rows + lax.broadcasted_iota(jnp.int32, (cache_rows, 128), 0)
    hidden = jnp.logical_and(lanes == ROPE + shard_count, slots >= prefix_ref[0])
    out_ref[tok_rows:, LATENT:] = jnp.where(hidden, 1.0, 0.0).astype(BF)
    out_ref[tok_rows:, LATENT : LATENT + ROPE] = cache_ref[:, LATENT:]


def pack(span_latents, cache_latents, gain, prefix_length, block_order):
    rows = span_latents.shape[0] + cache_latents.shape[0]
    return pl.pallas_call(
        functools.partial(pack_kernel, block_order.shape[0]),
        out_shape=jax.ShapeDtypeStruct((rows, PACKED), BF),
        in_specs=[smem_spec(), smem_spec(), vmem_spec(), vmem_spec(), vmem_spec()],
        out_specs=vmem_spec(),
        name="pack_rows",
    )(block_order, prefix_length, span_latents, cache_latents, gain.reshape(1, LATENT))


def query_kernel(order_ref, q_ref, out_ref):
    me = lax.axis_index("ctx")
    rows = q_ref.shape[0]
    lanes = lax.broadcasted_iota(jnp.int32, (rows, 128), 1)
    low = lanes < ROPE
    hide = jnp.where(lanes - ROPE > order_ref[me], NEG, 0.0)
    for pair in range(q_ref.shape[1] // 384):
        base = pair * 384
        second = q_ref[:, base + 128 : base + 256].astype(F32)
        third = q_ref[:, base + 256 : base + 384].astype(F32)
        second_turned = pltpu.roll(second, 64, 1)
        third_turned = pltpu.roll(third, 64, 1)
        to = pair * 2 * QK
        out_ref[:, to : to + 128] = q_ref[:, base : base + 128]
        out_ref[:, to + 128 : to + 256] = jnp.where(low, second, hide).astype(BF)
        out_ref[:, to + 256 : to + 384] = jnp.where(low, second_turned, third_turned).astype(BF)
        out_ref[:, to + 384 : to + 512] = jnp.where(low, third_turned, hide).astype(BF)


def arrange_queries(queries, block_order):
    rows, width = queries.shape
    heads = width // (NOPE + ROPE)
    return pl.pallas_call(
        query_kernel,
        out_shape=jax.ShapeDtypeStruct((rows, heads * QK), BF),
        grid=(4,),
        in_specs=[smem_spec(), pl.BlockSpec((rows, width // 4), lambda i: (0, i))],
        out_specs=pl.BlockSpec((rows, heads * QK // 4), lambda i: (0, i)),
        cost_estimate=pl.CostEstimate(flops=rows * width * 4, bytes_accessed=rows * width * 4, transcendentals=0),
        name="arrange_queries",
    )(block_order, queries)


def attend_kernel(pairs, own_rows, tok_rows, heads, q_ref, wk_ref, wv_ref, *rest):
    sources = rest[: 1 + sum(len(p) for p in pairs)]
    out_ref, rows_ref, keys_ref, sems = rest[1 + sum(len(p) for p in pairs) :]
    core = lax.axis_index("head")

    def target(slot):
        return rows_ref.at[pl.ds(slot * own_rows, own_rows), :]

    @pl.when(pl.program_id(0) == 0)
    def _():
        at = 0
        slot = 0
        for group in [(0,)] + list(pairs):
            if len(group) == 1:
                pltpu.make_async_copy(sources[at], target(slot), sems.at[slot]).start()
            else:
                for which in range(2):

                    @pl.when(core == which)
                    def _():
                        pltpu.make_async_copy(sources[at + which], target(slot), sems.at[slot]).start()

            at += len(group)
            slot += 1
        for index in range(slot):
            pltpu.make_async_copy(sources[0], target(index), sems.at[index]).wait()
        for head in range(heads):
            keys_ref[head, :, NOPE:] = rows_ref[:, LATENT:]

    scale = math.log2(math.e) / math.sqrt(NOPE + ROPE)
    latent = rows_ref[:, :LATENT]
    row_ids = lax.broadcasted_iota(jnp.int32, (tok_rows, tok_rows), 0)
    col_ids = lax.broadcasted_iota(jnp.int32, (tok_rows, tok_rows), 1)
    causal = jnp.where(col_ids <= row_ids, 0.0, NEG)
    for pair in range(heads // 2):
        keys = jnp.dot(latent, wk_ref[:, pair * 256 : pair * 256 + 256], preferred_element_type=F32).astype(BF)
        keys_ref[2 * pair, :, :NOPE] = keys[:, :NOPE]
        keys_ref[2 * pair + 1, :, :NOPE] = keys[:, NOPE:]
    for head in range(heads):
        scores = lax.dot_general(
            q_ref[:, head * QK : head * QK + QK],
            keys_ref[head],
            (((1,), (1,)), ((), ())),
            preferred_element_type=F32,
        )
        scores = jnp.concatenate([scores[:, :tok_rows] + causal, scores[:, tok_rows:]], axis=1)
        row_max = jnp.max(scores, axis=1, keepdims=True)
        exponent = jnp.exp2((scores - row_max) * scale)
        weight_sum = jnp.sum(exponent, axis=1, keepdims=True)
        mixed = jnp.dot(exponent.astype(BF), latent, preferred_element_type=F32).astype(BF)
        wv = wv_ref[:, head * VDIM : head * VDIM + VDIM]
        out = jnp.dot(mixed, wv, preferred_element_type=F32) / weight_sum
        out_ref[:, head * VDIM : head * VDIM + VDIM] = out.astype(BF)


def attend(arranged, key_weight, value_weight, own, pairs):
    tok_rows = arranged.shape[0]
    own_rows = own.shape[0]
    all_heads = key_weight.shape[1] // NOPE
    slots = 1 + len(pairs)
    heads = 4 if slots * own_rows <= 2048 else 2
    flat = [own] + [entry for group in pairs for entry in group]
    keys = slots * own_rows
    return pl.pallas_call(
        functools.partial(attend_kernel, pairs, own_rows, tok_rows, heads),
        out_shape=jax.ShapeDtypeStruct((tok_rows, all_heads * VDIM), BF),
        grid=(all_heads // heads,),
        in_specs=[
            pl.BlockSpec((tok_rows, heads * QK), lambda i: (0, i)),
            pl.BlockSpec((LATENT, heads * NOPE), lambda i: (0, i)),
            pl.BlockSpec((LATENT, heads * VDIM), lambda i: (0, i)),
        ]
        + [any_spec()] * len(flat),
        out_specs=pl.BlockSpec((tok_rows, heads * VDIM), lambda i: (0, i)),
        scratch_shapes=[
            pltpu.VMEM((keys, PACKED), BF),
            pltpu.VMEM((heads, keys, QK), BF),
            pltpu.SemaphoreType.DMA((slots,)),
        ],
        compiler_params=pltpu.CompilerParams(vmem_limit_bytes=56 * 1024 * 1024),
        cost_estimate=pl.CostEstimate(
            flops=2 * keys * all_heads * (LATENT * NOPE + tok_rows * (QK + LATENT)),
            bytes_accessed=LATENT * all_heads * 512,
            transcendentals=keys * tok_rows * all_heads,
        ),
        name="attend",
    )(arranged, key_weight, value_weight, *flat)


def exchange(own, shard_count):
    line = shard_count // 2

    def dev(place, side, core):
        return ((place % line) * 2 + side) * 2 + core

    def move(value, route):
        return lax.ppermute(
            value, AXES, [route(place, side) for place in range(line) for side in range(2)]
        )

    both = [
        (dev(place, side, core), dev(place, 1 - side, core))
        for place in range(line)
        for side in range(2)
        for core in range(2)
    ]
    steps = range(1, line)
    along = [move(own, lambda p, s, k=k: (dev(p, s, 0), dev(p + k, s, 0))) for k in steps]
    across = lax.ppermute(own, AXES, both)
    crossed = [move(a, lambda p, s: (dev(p, s, 0), dev(p, 1 - s, 1))) for a in along]
    shared = [move(a, lambda p, s: (dev(p, s, 0), dev(p, s, 1))) for a in along]
    back = [move(c, lambda p, s: (dev(p, s, 1), dev(p, s, 0))) for c in crossed]
    pairs = [(across,)]
    pairs += [(a, w) for a, w in zip(along, shared)]
    pairs += [(b, c) for b, c in zip(back, crossed)]
    return pairs


def per_device(
    queries,
    span_latents,
    cache_latents,
    latent_gain,
    key_weight,
    value_weight,
    prefix_length,
    block_order,
):
    shard_count = lax.axis_size("ctx")
    own = pack(span_latents, cache_latents, latent_gain, prefix_length, block_order)
    pairs = exchange(own, shard_count)
    arranged = arrange_queries(queries, block_order)
    return attend(arranged, key_weight, value_weight, own, pairs)


def solution(mesh):
    return jax.shard_map(
        per_device,
        mesh=mesh,
        in_specs=(
            P(("groups", "ctx"), "head"),
            P(("groups", "ctx"), None),
            P(("groups", "ctx"), None),
            P(),
            P(None, "head"),
            P(None, "head"),
            P("groups"),
            P("groups"),
        ),
        out_specs=P(("groups", "ctx"), "head"),
        check_vma=False,
    )
```

time: 160 us -> 70.8 us (0.44)
  waiting for transfers between devices: 55.2 us -> 1.03 us
  Pallas kernels: 0 us -> 39.4 us
  blocking collectives: 28.3 us -> 0 us
  matrix products: 18.7 us -> 0 us
  local copies, waits for them, and re-layouts: 21.3 us -> 3.12 us
  starting transfers between devices: 7.41 us -> 25 us
  between operations: 14.3 us -> 0.96 us
  other arithmetic: 8.5 us -> 0 us
  loops' own time: 5.5 us -> 0 us
    all_gather x1 -> x0, waiting for transfers between devices: 55.2 us -> none  [per_device(): piece = lax.all_gather(own_rows, 'ctx', axis=0, tiled=True)]
    pallas_call x0 -> x3, Pallas kernels: none -> 39.4 us  [the longest x1 33.7 us: attend(): pl.pallas_call(functools.partial(attend_kernel, pairs, own_rows, tok_rows...]
    all_to_all x1 -> x0, blocking collectives: 28.3 us -> none  [per_device(): lax.all_to_all(mixed_heads.reshape(shard_count * tok_rows, 1, my_heads *...]
    ppermute x0 -> x13, starting transfers between devices: none -> 25 us  [the longest x12 23.4 us: move(): lax.ppermute(value, AXES, [route(place, side) for place in range(line) fo...]
    dot_general x18 -> x0, matrix products: 18.7 us -> none  [the longest x8 9.69 us: one_block(): lax.dot_general(query_part, key_full, (((1,), (1,)), ((), ())), preferred...]
    all_to_all x1 -> x0, starting transfers between devices: 7.41 us -> none  [per_device(): lax.all_to_all(query_split, 'ctx', split_axis=1, concat_axis=0, tiled=True)]
    another operation x4 -> x0, loops' own time: 5.5 us -> none  [attend(): lax.map(one_block, jnp.arange(query_count // row_block, dtype=jnp.int32))]
    dynamic_slice x16 -> x0, local copies, waits for them, and re-layouts: 5.43 us -> none  [the longest x8 4.82 us: attend(): lax.map(one_block, jnp.arange(query_count // row_block, dtype=jnp.int32))]
  transfers between devices with their start and end apart: 2 -> 13, of which waited for: 1 -> 1; matrix products, arithmetic and copies ran while one was open for 8% -> 0% of each run, Pallas kernels for 0% -> 6%
where the time goes in v1:
time: 70.8 us; the launch traced here: 69.5 us
  Pallas kernels  39.4 us (56%)
  starting transfers between devices  25 us (35%)
  local copies, waits for them, and re-layouts  3.12 us (4%)
  waiting for transfers between devices  1.03 us (1%)
  between operations  0.96 us (1%)
    pallas_call x1, Pallas kernels, attend(): pl.pallas_call(functools.partial(attend_kernel, pairs, own_rows, tok_rows...  33.7 us
    ppermute x12, starting transfers between devices, move(): lax.ppermute(value, AXES, [route(place, side) for place in range(line) fo...  23.4 us
    pallas_call x1, Pallas kernels, arrange_queries(): pl.pallas_call(query_kernel, out_shape=jax.ShapeDtypeStruct((rows, heads...  3.95 us
    unnamed x27, local copies, waits for them, and re-layouts  3.12 us
    pallas_call x1, Pallas kernels, pack(): pl.pallas_call(functools.partial(pack_kernel, block_order.shape[0]), out_...  1.74 us
    ppermute x1, starting transfers between devices, exchange(): across = lax.ppermute(own, AXES, both)  1.58 us
  transfers between devices with their start and end apart: 13, of which 1 were waited for; matrix products, arithmetic and copies ran while one was open for 0% of the time, Pallas kernels for 6%

profile of v1, /device:TPU:0, one launch (start us, length us, event | category | flops | bytes accessed | tf_op | source)
XLA Modules:
  0.0 69.5 jit_solution(8099464152887309837)
XLA Ops:
  0.7 1.7 %copy.9.span_ref = bf16[128,576]{1,0:T(8,128)(2,1)} copy(bf16[128,576]{0,1:T(8,128)(2,1)} %param.9) | data formatting | bytes 294912 | tf_op args[1]
  2.4 1.7 %pack_rows.1.rest_0_ = bf16[144,640]{1,0:T(8,128)(2,1)} custom-call(s32[8]{0:T(128)} %order_ref.3, s32[1]{0:T(128)S(6)} %copy.10.prefix_ref, bf16[128,576]{1,0:T(8,128)(2,1)} %copy.9.span_ref, bf16[16,576]{1,0:T(8,128)(2,1)} %cache_ref.1, f32[1,512]{1,0:T(1,128)} %bitcast.1), custom_call_target="tpu_custom_call" | custom-call | tf_op jit(solution)/shard_map/pack_rows/pallas_call | solution.py:56
  4.1 6.9 %collective-permute-start.5 = (bf16[144,640]{1,0:T(8,128)(2,1)}, bf16[144,640]{1,0:T(8,128)(2,1)S(1)}, u32[]{:S(2)}, u32[]{:S(2)}) collective-permute-start(bf16[144,640]{1,0:T(8,128)(2,1)} %pack_rows.1.rest_0_), channel_id=1, source_target_pairs={{0,12},{2,14},{4,0},{6,2},{8,4},{10,6},{12,8},{14,10},{16,28},{18,... | collective-permute-start | bytes 552968 | tf_op jit(solution)/shard_map/ppermute | solution.py:194
  11.1 1.9 %collective-permute-start.3 = (bf16[144,640]{1,0:T(8,128)(2,1)}, bf16[144,640]{1,0:T(8,128)(2,1)S(1)}, u32[]{:S(2)}, u32[]{:S(2)}) collective-permute-start(bf16[144,640]{1,0:T(8,128)(2,1)} %pack_rows.1.rest_0_), channel_id=1, source_target_pairs={{0,8},{2,10},{4,12},{6,14},{8,0},{10,2},{12,4},{14,6},{16,24},{18,... | collective-permute-start | bytes 552968 | tf_op jit(solution)/shard_map/ppermute | solution.py:194
  13.0 2.9 %collective-permute-start.1 = (bf16[144,640]{1,0:T(8,128)(2,1)}, bf16[144,640]{1,0:T(8,128)(2,1)S(1)}, u32[]{:S(2)}, u32[]{:S(2)}) collective-permute-start(bf16[144,640]{1,0:T(8,128)(2,1)} %pack_rows.1.rest_0_), channel_id=1, source_target_pairs={{0,4},{2,6},{4,8},{6,10},{8,12},{10,14},{12,0},{14,2},{16,20},{18,... | collective-permute-start | bytes 552968 | tf_op jit(solution)/shard_map/ppermute | solution.py:194
  15.9 1.6 %collective-permute-start = (bf16[144,640]{1,0:T(8,128)(2,1)}, bf16[144,640]{1,0:T(8,128)(2,1)S(1)}, u32[]{:S(2)}, u32[]{:S(2)}) collective-permute-start(bf16[144,640]{1,0:T(8,128)(2,1)} %pack_rows.1.rest_0_), channel_id=1, source_target_pairs={{0,2},{1,3},{2,0},{3,1},{4,6},{5,7},{6,4},{7,5},{8,10},{9,11},{10,... | collective-permute-start | bytes 552968 | tf_op jit(solution)/shard_map/ppermute | solution.py:206
  17.5 0.0 collective-permute-done.5.rest_6_
  17.5 0.0 copy-start
  17.5 1.3 %collective-permute-start.11 = (bf16[144,640]{1,0:T(8,128)(2,1)S(1)}, bf16[144,640]{1,0:T(8,128)(2,1)S(1)}, u32[]{:S(2)}, u32[]{:S(2)}) collective-permute-start(bf16[144,640]{1,0:T(8,128)(2,1)S(1)} %collective-permute-done.5.rest_6_), channel_id=1, source_target_pairs={{0,3},{2,1},{4,7},{6,5},{8,11},{10,9},{12,15},{14,13},{16,19},{18,... | collective-permute-start | bytes 552968 | tf_op jit(solution)/shard_map/ppermute | solution.py:194
  18.8 1.3 %collective-permute-start.6 = (bf16[144,640]{1,0:T(8,128)(2,1)S(1)}, bf16[144,640]{1,0:T(8,128)(2,1)S(1)}, u32[]{:S(2)}, u32[]{:S(2)}) collective-permute-start(bf16[144,640]{1,0:T(8,128)(2,1)S(1)} %collective-permute-done.5.rest_6_), channel_id=1, source_target_pairs={{0,1},{2,3},{4,5},{6,7},{8,9},{10,11},{12,13},{14,15},{16,17},{18,... | collective-permute-start | bytes 552968 | tf_op jit(solution)/shard_map/ppermute | solution.py:194
  20.1 0.0 collective-permute-done.3.rest_4_
  20.1 0.0 copy-start.1
  20.1 1.3 %collective-permute-start.9 = (bf16[144,640]{1,0:T(8,128)(2,1)S(1)}, bf16[144,640]{1,0:T(8,128)(2,1)S(1)}, u32[]{:S(2)}, u32[]{:S(2)}) collective-permute-start(bf16[144,640]{1,0:T(8,128)(2,1)S(1)} %collective-permute-done.3.rest_4_), channel_id=1, source_target_pairs={{0,3},{2,1},{4,7},{6,5},{8,11},{10,9},{12,15},{14,13},{16,19},{18,... | collective-permute-start | bytes 552968 | tf_op jit(solution)/shard_map/ppermute | solution.py:194
  21.4 1.0 %collective-permute-done.1.rest_2_ = bf16[144,640]{1,0:T(8,128)(2,1)S(1)} collective-permute-done((bf16[144,640]{1,0:T(8,128)(2,1)}, bf16[144,640]{1,0:T(8,128)(2,1)S(1)}, u32[]{:S(2)}, u32[]{:S(2)}) %collective-permute-start.1) | collective-permute-done | bytes 184352 | tf_op jit(solution)/shard_map/ppermute | solution.py:194
  22.4 0.0 copy-start.2
  22.4 1.3 %collective-permute-start.7 = (bf16[144,640]{1,0:T(8,128)(2,1)S(1)}, bf16[144,640]{1,0:T(8,128)(2,1)S(1)}, u32[]{:S(2)}, u32[]{:S(2)}) collective-permute-start(bf16[144,640]{1,0:T(8,128)(2,1)S(1)} %collective-permute-done.1.rest_2_), channel_id=1, source_target_pairs={{0,3},{2,1},{4,7},{6,5},{8,11},{10,9},{12,15},{14,13},{16,19},{18,... | collective-permute-start | bytes 552968 | tf_op jit(solution)/shard_map/ppermute | solution.py:194
  23.7 0.0 collective-permute-done.rest_1_
  23.7 0.0 copy-start.3
  23.8 1.3 %collective-permute-start.4 = (bf16[144,640]{1,0:T(8,128)(2,1)S(1)}, bf16[144,640]{1,0:T(8,128)(2,1)S(1)}, u32[]{:S(2)}, u32[]{:S(2)}) collective-permute-start(bf16[144,640]{1,0:T(8,128)(2,1)S(1)} %collective-permute-done.3.rest_4_), channel_id=1, source_target_pairs={{0,1},{2,3},{4,5},{6,7},{8,9},{10,11},{12,13},{14,15},{16,17},{18,... | collective-permute-start | bytes 552968 | tf_op jit(solution)/shard_map/ppermute | solution.py:194
  25.1 0.0 collective-permute-done.11.rest_13_
  25.1 0.0 copy-start.4
  25.1 1.3 %collective-permute-start.2 = (bf16[144,640]{1,0:T(8,128)(2,1)S(1)}, bf16[144,640]{1,0:T(8,128)(2,1)S(1)}, u32[]{:S(2)}, u32[]{:S(2)}) collective-permute-start(bf16[144,640]{1,0:T(8,128)(2,1)S(1)} %collective-permute-done.1.rest_2_), channel_id=1, source_target_pairs={{0,1},{2,3},{4,5},{6,7},{8,9},{10,11},{12,13},{14,15},{16,17},{18,... | collective-permute-start | bytes 552968 | tf_op jit(solution)/shard_map/ppermute | solution.py:194
  26.4 0.0 collective-permute-done.6.rest_7_
  26.4 0.0 copy-start.5
  26.4 1.3 %collective-permute-start.12 = (bf16[144,640]{1,0:T(8,128)(2,1)S(1)}, bf16[144,640]{1,0:T(8,128)(2,1)S(1)}, u32[]{:S(2)}, u32[]{:S(2)}) collective-permute-start(bf16[144,640]{1,0:T(8,128)(2,1)S(1)} %collective-permute-done.11.rest_13_), channel_id=1, source_target_pairs={{1,0},{3,2},{5,4},{7,6},{9,8},{11,10},{13,12},{15,14},{17,16},{19,... | collective-permute-start | bytes 552968 | tf_op jit(solution)/shard_map/ppermute | solution.py:194
  27.7 0.0 collective-permute-done.9.rest_11_
  27.7 0.0 copy-start.6
  27.7 1.3 %collective-permute-start.10 = (bf16[144,640]{1,0:T(8,128)(2,1)S(1)}, bf16[144,640]{1,0:T(8,128)(2,1)S(1)}, u32[]{:S(2)}, u32[]{:S(2)}) collective-permute-start(bf16[144,640]{1,0:T(8,128)(2,1)S(1)} %collective-permute-done.9.rest_11_), channel_id=1, source_target_pairs={{1,0},{3,2},{5,4},{7,6},{9,8},{11,10},{13,12},{15,14},{17,16},{19,... | collective-permute-start | bytes 552968 | tf_op jit(solution)/shard_map/ppermute | solution.py:194
  29.0 0.0 collective-permute-done.7.rest_9_
  29.0 0.0 copy-start.7
  29.1 1.3 %collective-permute-start.8 = (bf16[144,640]{1,0:T(8,128)(2,1)S(1)}, bf16[144,640]{1,0:T(8,128)(2,1)S(1)}, u32[]{:S(2)}, u32[]{:S(2)}) collective-permute-start(bf16[144,640]{1,0:T(8,128)(2,1)S(1)} %collective-permute-done.7.rest_9_), channel_id=1, source_target_pairs={{1,0},{3,2},{5,4},{7,6},{9,8},{11,10},{13,12},{15,14},{17,16},{19,... | collective-permute-start | bytes 552968 | tf_op jit(solution)/shard_map/ppermute | solution.py:194
  30.4 3.9 %arrange_queries.1.q_ref = bf16[128,8192]{1,0:T(8,128)(2,1)} custom-call(s32[8]{0:T(128)} %order_ref.3, bf16[128,6144]{1,0:T(8,128)(2,1)} %q_ref.1), custom_call_target="tpu_custom_call" | custom-call | flops 3145728 | bytes 3145728 | tf_op jit(solution)/shard_map/arrange_queries/pallas_call | solution.py:87
  34.3 0.0 collective-permute-done.4.rest_5_
  34.3 0.0 copy-start.8
  34.3 0.0 collective-permute-done.2.rest_3_
  34.3 0.0 copy-start.9
  34.3 0.0 collective-permute-done.12.rest_12_
  34.3 0.0 copy-start.10
  34.3 0.0 collective-permute-done.10.rest_10_
  34.4 0.0 copy-start.11
  34.4 0.0 collective-permute-done.8.rest_8_
  34.4 0.0 copy-done
  34.4 0.0 copy-done.1
  34.4 0.0 copy-done.2
  34.4 0.0 copy-done.3
  34.4 0.0 copy-done.4
  34.4 0.0 copy-done.5
  34.4 0.0 copy-done.6
  34.4 0.0 copy-done.7
  34.5 0.5 copy-done.8
  35.0 0.1 copy-done.9
  35.1 0.1 copy-done.10
  35.1 0.0 copy-done.11
  35.2 0.0 copy-start.12
  35.2 0.7 copy-done.12
  35.8 33.7 %attend.1 = bf16[128,4096]{1,0:T(8,128)(2,1)} custom-call(bf16[128,8192]{1,0:T(8,128)(2,1)} %arrange_queries.1.q_ref, bf16[512,4096]{1,0:T(8,128)(2,1)} %wk_ref.1, bf16[512,4096]{1,0:T(8,128)(2,1)} %wv_ref.1, bf16[144,640]{1,0:T(8,128)(2,1)} %pack_rows.1.rest_0_, bf16[144,640]{1,0:T(8,128)(2,1)} %copy-done.3, bf16[144,640]{1,0:T(8,128)(2,1)} %copy-done.2, ...), custom_call_target="tpu_custom_call" | custom-call | flops 12079595520 | bytes 8388608 | tf_op jit(solution)/shard_map/attend/pallas_call | solution.py:161
Async XLA Ops:
  4.1 13.4 %collective-permute-start.5 = (bf16[144,640]{1,0:T(8,128)(2,1)}, bf16[144,640]{1,0:T(8,128)(2,1)S(1)}, u32[]{:S(2)}, u32[]{:S(2)}) collective-permute-start(bf16[144,640]{1,0:T(8,128)(2,1)} %pack_rows.1.rest_0_), channel_id=1, source_target_pairs={{0,12},{2,14},{4,0},{6,2},{8,4},{10,6},{12,8},{14,10},{16,28},{18,... | collective-permute-start | bytes 552968 | tf_op jit(solution)/shard_map/ppermute | solution.py:194
  11.1 9.0 %collective-permute-start.3 = (bf16[144,640]{1,0:T(8,128)(2,1)}, bf16[144,640]{1,0:T(8,128)(2,1)S(1)}, u32[]{:S(2)}, u32[]{:S(2)}) collective-permute-start(bf16[144,640]{1,0:T(8,128)(2,1)} %pack_rows.1.rest_0_), channel_id=1, source_target_pairs={{0,8},{2,10},{4,12},{6,14},{8,0},{10,2},{12,4},{14,6},{16,24},{18,... | collective-permute-start | bytes 552968 | tf_op jit(solution)/shard_map/ppermute | solution.py:194
  13.0 9.4 %collective-permute-start.1 = (bf16[144,640]{1,0:T(8,128)(2,1)}, bf16[144,640]{1,0:T(8,128)(2,1)S(1)}, u32[]{:S(2)}, u32[]{:S(2)}) collective-permute-start(bf16[144,640]{1,0:T(8,128)(2,1)} %pack_rows.1.rest_0_), channel_id=1, source_target_pairs={{0,4},{2,6},{4,8},{6,10},{8,12},{10,14},{12,0},{14,2},{16,20},{18,... | collective-permute-start | bytes 552968 | tf_op jit(solution)/shard_map/ppermute | solution.py:194
  15.9 7.8 %collective-permute-start = (bf16[144,640]{1,0:T(8,128)(2,1)}, bf16[144,640]{1,0:T(8,128)(2,1)S(1)}, u32[]{:S(2)}, u32[]{:S(2)}) collective-permute-start(bf16[144,640]{1,0:T(8,128)(2,1)} %pack_rows.1.rest_0_), channel_id=1, source_target_pairs={{0,2},{1,3},{2,0},{3,1},{4,6},{5,7},{6,4},{7,5},{8,10},{9,11},{10,... | collective-permute-start | bytes 552968 | tf_op jit(solution)/shard_map/ppermute | solution.py:206
  17.5 16.9 %copy-start = (bf16[144,640]{1,0:T(8,128)(2,1)}, bf16[144,640]{1,0:T(8,128)(2,1)S(1)}, u32[]{:S(2)}) copy-start(bf16[144,640]{1,0:T(8,128)(2,1)S(1)} %collective-permute-done.5.rest_6_) | copy-start | bytes 552964
  17.5 7.6 %collective-permute-start.11 = (bf16[144,640]{1,0:T(8,128)(2,1)S(1)}, bf16[144,640]{1,0:T(8,128)(2,1)S(1)}, u32[]{:S(2)}, u32[]{:S(2)}) collective-permute-start(bf16[144,640]{1,0:T(8,128)(2,1)S(1)} %collective-permute-done.5.rest_6_), channel_id=1, source_target_pairs={{0,3},{2,1},{4,7},{6,5},{8,11},{10,9},{12,15},{14,13},{16,19},{18,... | collective-permute-start | bytes 552968 | tf_op jit(solution)/shard_map/ppermute | solution.py:194
  18.8 7.6 %collective-permute-start.6 = (bf16[144,640]{1,0:T(8,128)(2,1)S(1)}, bf16[144,640]{1,0:T(8,128)(2,1)S(1)}, u32[]{:S(2)}, u32[]{:S(2)}) collective-permute-start(bf16[144,640]{1,0:T(8,128)(2,1)S(1)} %collective-permute-done.5.rest_6_), channel_id=1, source_target_pairs={{0,1},{2,3},{4,5},{6,7},{8,9},{10,11},{12,13},{14,15},{16,17},{18,... | collective-permute-start | bytes 552968 | tf_op jit(solution)/shard_map/ppermute | solution.py:194
  20.1 14.3 %copy-start.1 = (bf16[144,640]{1,0:T(8,128)(2,1)}, bf16[144,640]{1,0:T(8,128)(2,1)S(1)}, u32[]{:S(2)}) copy-start(bf16[144,640]{1,0:T(8,128)(2,1)S(1)} %collective-permute-done.3.rest_4_) | copy-start | bytes 552964
  20.1 7.6 %collective-permute-start.9 = (bf16[144,640]{1,0:T(8,128)(2,1)S(1)}, bf16[144,640]{1,0:T(8,128)(2,1)S(1)}, u32[]{:S(2)}, u32[]{:S(2)}) collective-permute-start(bf16[144,640]{1,0:T(8,128)(2,1)S(1)} %collective-permute-done.3.rest_4_), channel_id=1, source_target_pairs={{0,3},{2,1},{4,7},{6,5},{8,11},{10,9},{12,15},{14,13},{16,19},{18,... | collective-permute-start | bytes 552968 | tf_op jit(solution)/shard_map/ppermute | solution.py:194
  22.4 12.0 %copy-start.2 = (bf16[144,640]{1,0:T(8,128)(2,1)}, bf16[144,640]{1,0:T(8,128)(2,1)S(1)}, u32[]{:S(2)}) copy-start(bf16[144,640]{1,0:T(8,128)(2,1)S(1)} %collective-permute-done.1.rest_2_) | copy-start | bytes 552964
  22.4 6.6 %collective-permute-start.7 = (bf16[144,640]{1,0:T(8,128)(2,1)S(1)}, bf16[144,640]{1,0:T(8,128)(2,1)S(1)}, u32[]{:S(2)}, u32[]{:S(2)}) collective-permute-start(bf16[144,640]{1,0:T(8,128)(2,1)S(1)} %collective-permute-done.1.rest_2_), channel_id=1, source_target_pairs={{0,3},{2,1},{4,7},{6,5},{8,11},{10,9},{12,15},{14,13},{16,19},{18,... | collective-permute-start | bytes 552968 | tf_op jit(solution)/shard_map/ppermute | solution.py:194
  23.7 10.7 %copy-start.3 = (bf16[144,640]{1,0:T(8,128)(2,1)}, bf16[144,640]{1,0:T(8,128)(2,1)S(1)}, u32[]{:S(2)}) copy-start(bf16[144,640]{1,0:T(8,128)(2,1)S(1)} %collective-permute-done.rest_1_) | copy-start | bytes 552964
  23.8 10.5 %collective-permute-start.4 = (bf16[144,640]{1,0:T(8,128)(2,1)S(1)}, bf16[144,640]{1,0:T(8,128)(2,1)S(1)}, u32[]{:S(2)}, u32[]{:S(2)}) collective-permute-start(bf16[144,640]{1,0:T(8,128)(2,1)S(1)} %collective-permute-done.3.rest_4_), channel_id=1, source_target_pairs={{0,1},{2,3},{4,5},{6,7},{8,9},{10,11},{12,13},{14,15},{16,17},{18,... | collective-permute-start | bytes 552968 | tf_op jit(solution)/shard_map/ppermute | solution.py:194
  25.1 9.3 %copy-start.4 = (bf16[144,640]{1,0:T(8,128)(2,1)}, bf16[144,640]{1,0:T(8,128)(2,1)S(1)}, u32[]{:S(2)}) copy-start(bf16[144,640]{1,0:T(8,128)(2,1)S(1)} %collective-permute-done.11.rest_13_) | copy-start | bytes 552964
  25.1 9.2 %collective-permute-start.2 = (bf16[144,640]{1,0:T(8,128)(2,1)S(1)}, bf16[144,640]{1,0:T(8,128)(2,1)S(1)}, u32[]{:S(2)}, u32[]{:S(2)}) collective-permute-start(bf16[144,640]{1,0:T(8,128)(2,1)S(1)} %collective-permute-done.1.rest_2_), channel_id=1, source_target_pairs={{0,1},{2,3},{4,5},{6,7},{8,9},{10,11},{12,13},{14,15},{16,17},{18,... | collective-permute-start | bytes 552968 | tf_op jit(solution)/shard_map/ppermute | solution.py:194
  26.4 8.0 %copy-start.5 = (bf16[144,640]{1,0:T(8,128)(2,1)}, bf16[144,640]{1,0:T(8,128)(2,1)S(1)}, u32[]{:S(2)}) copy-start(bf16[144,640]{1,0:T(8,128)(2,1)S(1)} %collective-permute-done.6.rest_7_) | copy-start | bytes 552964
  26.4 7.9 %collective-permute-start.12 = (bf16[144,640]{1,0:T(8,128)(2,1)S(1)}, bf16[144,640]{1,0:T(8,128)(2,1)S(1)}, u32[]{:S(2)}, u32[]{:S(2)}) collective-permute-start(bf16[144,640]{1,0:T(8,128)(2,1)S(1)} %collective-permute-done.11.rest_13_), channel_id=1, source_target_pairs={{1,0},{3,2},{5,4},{7,6},{9,8},{11,10},{13,12},{15,14},{17,16},{19,... | collective-permute-start | bytes 552968 | tf_op jit(solution)/shard_map/ppermute | solution.py:194
  27.7 6.7 %copy-start.6 = (bf16[144,640]{1,0:T(8,128)(2,1)}, bf16[144,640]{1,0:T(8,128)(2,1)S(1)}, u32[]{:S(2)}) copy-start(bf16[144,640]{1,0:T(8,128)(2,1)S(1)} %collective-permute-done.9.rest_11_) | copy-start | bytes 552964
  27.7 6.6 %collective-permute-start.10 = (bf16[144,640]{1,0:T(8,128)(2,1)S(1)}, bf16[144,640]{1,0:T(8,128)(2,1)S(1)}, u32[]{:S(2)}, u32[]{:S(2)}) collective-permute-start(bf16[144,640]{1,0:T(8,128)(2,1)S(1)} %collective-permute-done.9.rest_11_), channel_id=1, source_target_pairs={{1,0},{3,2},{5,4},{7,6},{9,8},{11,10},{13,12},{15,14},{17,16},{19,... | collective-permute-start | bytes 552968 | tf_op jit(solution)/shard_map/ppermute | solution.py:194
  29.0 5.4 %copy-start.7 = (bf16[144,640]{1,0:T(8,128)(2,1)}, bf16[144,640]{1,0:T(8,128)(2,1)S(1)}, u32[]{:S(2)}) copy-start(bf16[144,640]{1,0:T(8,128)(2,1)S(1)} %collective-permute-done.7.rest_9_) | copy-start | bytes 552964
  29.1 5.3 %collective-permute-start.8 = (bf16[144,640]{1,0:T(8,128)(2,1)S(1)}, bf16[144,640]{1,0:T(8,128)(2,1)S(1)}, u32[]{:S(2)}, u32[]{:S(2)}) collective-permute-start(bf16[144,640]{1,0:T(8,128)(2,1)S(1)} %collective-permute-done.7.rest_9_), channel_id=1, source_target_pairs={{1,0},{3,2},{5,4},{7,6},{9,8},{11,10},{13,12},{15,14},{17,16},{19,... | collective-permute-start | bytes 552968 | tf_op jit(solution)/shard_map/ppermute | solution.py:194
  34.3 0.7 copy-start.8
  34.3 0.7 %copy-start.9 = (bf16[144,640]{1,0:T(8,128)(2,1)}, bf16[144,640]{1,0:T(8,128)(2,1)S(1)}, u32[]{:S(2)}) copy-start(bf16[144,640]{1,0:T(8,128)(2,1)S(1)} %collective-permute-done.2.rest_3_) | copy-start | bytes 552964
  34.3 0.8 %copy-start.10 = (bf16[144,640]{1,0:T(8,128)(2,1)}, bf16[144,640]{1,0:T(8,128)(2,1)S(1)}, u32[]{:S(2)}) copy-start(bf16[144,640]{1,0:T(8,128)(2,1)S(1)} %collective-permute-done.12.rest_12_) | copy-start | bytes 552964
  34.4 0.8 %copy-start.11 = (bf16[144,640]{1,0:T(8,128)(2,1)}, bf16[144,640]{1,0:T(8,128)(2,1)S(1)}, u32[]{:S(2)}) copy-start(bf16[144,640]{1,0:T(8,128)(2,1)S(1)} %collective-permute-done.10.rest_10_) | copy-start | bytes 552964
  35.2 0.7 copy-start.12

commit v2 on v1

v2 whole, which is shorter than its diff:
```python
import functools
import math

import jax
import jax.numpy as jnp
from jax import lax
from jax.experimental import pallas as pl
from jax.experimental.pallas import tpu as pltpu
from jax.sharding import PartitionSpec as P

LATENT = 512
ROPE = 64
NOPE = 128
VDIM = 128
PACKED = 640
QK = 256
NEG = -1e30
AXES = ("ctx", "head")
BF = jnp.bfloat16
F32 = jnp.float32


def vmem_spec():
    return pl.BlockSpec(memory_space=pltpu.VMEM)


def smem_spec():
    return pl.BlockSpec(memory_space=pltpu.SMEM)


def any_spec():
    return pl.BlockSpec(memory_space=pl.ANY)


def pack_kernel(shard_count, order_ref, prefix_ref, span_ref, cache_ref, gain_ref, out_ref):
    tok_rows = span_ref.shape[1]
    cache_rows = cache_ref.shape[0]
    me = lax.axis_index("ctx")
    latent = span_ref[:LATENT, :].astype(F32)
    mean_square = jnp.mean(latent * latent, axis=0, keepdims=True)
    normed = (latent * lax.rsqrt(mean_square + 1e-06)).T * gain_ref[...]
    out_ref[:tok_rows, :LATENT] = normed.astype(BF)
    rest = lax.broadcasted_iota(jnp.int32, (ROPE, tok_rows), 0)
    rest = jnp.where(rest == order_ref[me], 1.0, 0.0)
    tail = jnp.concatenate([span_ref[LATENT:, :].astype(F32), rest], axis=0)
    out_ref[:tok_rows, LATENT:] = tail.T.astype(BF)
    out_ref[tok_rows:, :LATENT] = cache_ref[:, :LATENT]
    lanes = lax.broadcasted_iota(jnp.int32, (cache_rows, 128), 1)
    slots = me * cache_rows + lax.broadcasted_iota(jnp.int32, (cache_rows, 128), 0)
    hidden = jnp.logical_and(lanes == ROPE + shard_count, slots >= prefix_ref[0])
    out_ref[tok_rows:, LATENT:] = jnp.where(hidden, 1.0, 0.0).astype(BF)
    out_ref[tok_rows:, LATENT : LATENT + ROPE] = cache_ref[:, LATENT:]


def pack(span_latents, cache_latents, gain, prefix_length, block_order):
    rows = span_latents.shape[0] + cache_latents.shape[0]
    return pl.pallas_call(
        functools.partial(pack_kernel, block_order.shape[0]),
        out_shape=jax.ShapeDtypeStruct((rows, PACKED), BF),
        in_specs=[smem_spec(), smem_spec(), vmem_spec(), vmem_spec(), vmem_spec()],
        out_specs=vmem_spec(),
        name="pack_rows",
    )(block_order, prefix_length, span_latents.T, cache_latents, gain.reshape(1, LATENT))


def prepare_kernel(order_ref, q_ref, wv_ref, qt_ref, wvt_ref):
    me = lax.axis_index("ctx")
    rows = q_ref.shape[0]
    places = lax.broadcasted_iota(jnp.int32, (ROPE, rows), 0)
    hide = jnp.where(places > order_ref[me], NEG, 0.0).astype(BF)
    for pair in range(q_ref.shape[1] // 384):
        base = pair * 384
        to = pair * 2 * QK
        turned = q_ref[:, base : base + 384].T
        qt_ref[to : to + 192, :] = turned[:192]
        qt_ref[to + 192 : to + 256, :] = hide
        qt_ref[to + 256 : to + 448, :] = turned[192:]
        qt_ref[to + 448 : to + 512, :] = hide
    wvt_ref[...] = wv_ref[...].T


def prepare(queries, value_weight, block_order):
    rows, width = queries.shape
    heads = width // (NOPE + ROPE)
    steps = 8
    return pl.pallas_call(
        prepare_kernel,
        out_shape=(
            jax.ShapeDtypeStruct((heads * QK, rows), BF),
            jax.ShapeDtypeStruct((heads * VDIM, LATENT), BF),
        ),
        grid=(steps,),
        in_specs=[
            smem_spec(),
            pl.BlockSpec((rows, width // steps), lambda i: (0, i)),
            pl.BlockSpec((LATENT, heads * VDIM // steps), lambda i: (0, i)),
        ],
        out_specs=(
            pl.BlockSpec((heads * QK // steps, rows), lambda i: (i, 0)),
            pl.BlockSpec((heads * VDIM // steps, LATENT), lambda i: (i, 0)),
        ),
        cost_estimate=pl.CostEstimate(
            flops=rows * width * 4, bytes_accessed=LATENT * heads * VDIM * 6, transcendentals=0
        ),
        name="prepare",
    )(block_order, queries, value_weight)


def attend_kernel(blocks, tok_rows, heads, qt_ref, wk_ref, wvt_ref, *rest):
    sources = rest[:blocks]
    out_ref, rows_ref, turned_ref = rest[blocks:]
    own_rows = sources[0].shape[0]

    @pl.when(pl.program_id(0) == 0)
    def _():
        for slot in range(blocks):
            rows_ref[slot * own_rows : (slot + 1) * own_rows, :] = sources[slot][...]
        turned_ref[...] = rows_ref[:, :LATENT].T

    scale = math.log2(math.e) / math.sqrt(NOPE + ROPE)
    latent = rows_ref[:, :LATENT]
    tail = rows_ref[:, LATENT:]
    key_ids = lax.broadcasted_iota(jnp.int32, (tok_rows, tok_rows), 0)
    query_ids = lax.broadcasted_iota(jnp.int32, (tok_rows, tok_rows), 1)
    causal = jnp.where(key_ids <= query_ids, 0.0, NEG)
    for pair in range(heads // 2):
        keys = jnp.dot(latent, wk_ref[:, pair * 256 : pair * 256 + 256], preferred_element_type=F32).astype(BF)
        weights = []
        sums = []
        for side in range(2):
            head = pair * 2 + side
            full = jnp.concatenate([keys[:, side * NOPE : side * NOPE + NOPE], tail], axis=1)
            scores = jnp.dot(full, qt_ref[head * QK : head * QK + QK, :], preferred_element_type=F32)
            scores = jnp.concatenate([scores[:tok_rows] + causal, scores[tok_rows:]], axis=0)
            col_max = jnp.max(scores, axis=0, keepdims=True)
            exponent = jnp.exp2((scores - col_max) * scale)
            sums.append(jnp.sum(exponent, axis=0, keepdims=True))
            weights.append(exponent.astype(BF))
        mixed = jnp.dot(turned_ref[...], jnp.concatenate(weights, axis=1), preferred_element_type=F32).astype(BF)
        for side in range(2):
            head = pair * 2 + side
            out = jnp.dot(
                wvt_ref[head * VDIM : head * VDIM + VDIM, :],
                mixed[:, side * tok_rows : (side + 1) * tok_rows],
                preferred_element_type=F32,
            )
            out_ref[:, head * VDIM : head * VDIM + VDIM] = (out / sums[side]).T.astype(BF)


def attend(queries_turned, key_weight, values_turned, blocks):
    tok_rows = queries_turned.shape[1]
    all_heads = key_weight.shape[1] // NOPE
    keys = len(blocks) * blocks[0].shape[0]
    heads = 4 if keys <= 2048 else 2
    return pl.pallas_call(
        functools.partial(attend_kernel, len(blocks), tok_rows, heads),
        out_shape=jax.ShapeDtypeStruct((tok_rows, all_heads * VDIM), BF),
        grid=(all_heads // heads,),
        in_specs=[
            pl.BlockSpec((heads * QK, tok_rows), lambda i: (i, 0)),
            pl.BlockSpec((LATENT, heads * NOPE), lambda i: (0, i)),
            pl.BlockSpec((heads * VDIM, LATENT), lambda i: (i, 0)),
        ]
        + [vmem_spec()] * len(blocks),
        out_specs=pl.BlockSpec((tok_rows, heads * VDIM), lambda i: (0, i)),
        scratch_shapes=[pltpu.VMEM((keys, PACKED), BF), pltpu.VMEM((LATENT, keys), BF)],
        compiler_params=pltpu.CompilerParams(vmem_limit_bytes=48 * 1024 * 1024),
        cost_estimate=pl.CostEstimate(
            flops=2 * keys * all_heads * (LATENT * NOPE + tok_rows * (QK + LATENT)),
            bytes_accessed=LATENT * all_heads * 512,
            transcendentals=keys * tok_rows * all_heads,
        ),
        name="attend",
    )(queries_turned, key_weight, values_turned, *blocks)


def exchange(own, shard_count):
    line = shard_count // 2

    def move(value, route):
        pairs = []
        for place in range(line):
            for side in range(2):
                for core in range(2):
                    to_place, to_side, to_core = route(place, side, core)
                    source = (place * 2 + side) * 2 + core
                    target = ((to_place % line) * 2 + to_side) * 2 + to_core
                    pairs.append((source, target))
        return lax.ppermute(value, AXES, pairs)

    steps = range(1, line)
    along = [move(own, lambda p, s, c, k=k: (p + k, s ^ c, c)) for k in steps]
    across = move(own, lambda p, s, c: (p, 1 - s, c))
    swapped = [move(a, lambda p, s, c: (p, s, 1 - c)) for a in along]
    return [across] + along + swapped


def per_device(
    queries,
    span_latents,
    cache_latents,
    latent_gain,
    key_weight,
    value_weight,
    prefix_length,
    block_order,
):
    shard_count = lax.axis_size("ctx")
    own = pack(span_latents, cache_latents, latent_gain, prefix_length, block_order)
    others = exchange(own, shard_count)
    queries_turned, values_turned = prepare(queries, value_weight, block_order)
    return attend(queries_turned, key_weight, values_turned, [own] + others)


def solution(mesh):
    return jax.shard_map(
        per_device,
        mesh=mesh,
        in_specs=(
            P(("groups", "ctx"), "head"),
            P(("groups", "ctx"), None),
            P(("groups", "ctx"), None),
            P(),
            P(None, "head"),
            P(None, "head"),
            P("groups"),
            P("groups"),
        ),
        out_specs=P(("groups", "ctx"), "head"),
        check_vma=False,
    )
```

time: 70.8 us -> 70.8 us (level); the launches traced: 69.5 us -> 70.4 us
  starting transfers between devices: 25 us -> 8.09 us
  waiting for transfers between devices: 1.03 us -> 14.3 us
  Pallas kernels: 39.4 us -> 45.8 us
  local copies, waits for them, and re-layouts: 3.12 us -> 1.59 us
    ppermute x13 -> x7, starting transfers between devices: 25 us -> 8.09 us  [move(): return lax.ppermute(value, AXES, pairs)]
    ppermute x13 -> x7, waiting for transfers between devices: 1.03 us -> 14.3 us  [move(): return lax.ppermute(value, AXES, pairs)]
    pallas_call x2, Pallas kernels: 37.6 us -> 43.9 us  [the longest x1 35.7 us: attend(): pl.pallas_call(functools.partial(attend_kernel, len(blocks), tok_rows, he...]
    unnamed x27 -> x4, local copies, waits for them, and re-layouts: 3.12 us -> 1.59 us
  transfers between devices with their start and end apart: 13 -> 7, of which waited for: 1 -> 2; matrix products, arithmetic and copies ran while one was open for 0% -> 0% of each run, Pallas kernels for 6% -> 12%
where the time goes in v2:
time: 70.8 us; the launch traced here: 70.4 us
  Pallas kernels  45.8 us (65%)
  waiting for transfers between devices  14.3 us (20%)
  starting transfers between devices  8.09 us (11%)
  local copies, waits for them, and re-layouts  1.59 us (2%)
    pallas_call x1, Pallas kernels, attend(): pl.pallas_call(functools.partial(attend_kernel, len(blocks), tok_rows, he...  35.7 us
    ppermute x7, waiting for transfers between devices, move(): return lax.ppermute(value, AXES, pairs)  14.3 us
    pallas_call x1, Pallas kernels, prepare(): pl.pallas_call(prepare_kernel, out_shape=(jax.ShapeDtypeStruct((heads * Q...  8.26 us
    ppermute x7, starting transfers between devices, move(): return lax.ppermute(value, AXES, pairs)  8.09 us
    pallas_call x1, Pallas kernels, pack(): pl.pallas_call(functools.partial(pack_kernel, block_order.shape[0]), out_...  1.86 us
    unnamed x4, local copies, waits for them, and re-layouts  1.59 us
  transfers between devices with their start and end apart: 7, of which 2 were waited for; matrix products, arithmetic and copies ran while one was open for 0% of the time, Pallas kernels for 12%

profile of v2, /device:TPU:0, one launch (start us, length us, event | category | flops | bytes accessed | tf_op | source)
XLA Modules:
  0.0 70.4 jit_solution(13072251455819191315)
XLA Ops:
  0.7 1.9 %pack_rows.1.rest_0_ = bf16[144,640]{1,0:T(8,128)(2,1)} custom-call(s32[8]{0:T(128)} %order_ref.3, s32[1]{0:T(128)S(6)} %copy.9.prefix_ref, bf16[576,128]{1,0:T(8,128)(2,1)} %bitcast.2, bf16[16,576]{1,0:T(8,128)(2,1)} %cache_ref.1, f32[1,512]{1,0:T(1,128)} %bitcast.3), custom_call_target="tpu_custom_call" | custom-call | tf_op jit(solution)/shard_map/pack_rows/pallas_call | solution.py:57
  2.5 0.0 copy-start
  2.5 5.0 %collective-permute-start.3 = (bf16[144,640]{1,0:T(8,128)(2,1)}, bf16[144,640]{1,0:T(8,128)(2,1)S(1)}, u32[]{:S(2)}, u32[]{:S(2)}) collective-permute-start(bf16[144,640]{1,0:T(8,128)(2,1)} %pack_rows.1.rest_0_), channel_id=1, source_target_pairs={{0,12},{1,15},{2,14},{3,13},{4,0},{5,3},{6,2},{7,1},{8,4},{9,7},{1... | collective-permute-start | bytes 552968 | tf_op jit(solution)/shard_map/ppermute | solution.py:189
  7.6 0.0 collective-permute-start.2
  7.6 1.0 %collective-permute-start.1 = (bf16[144,640]{1,0:T(8,128)(2,1)}, bf16[144,640]{1,0:T(8,128)(2,1)S(1)}, u32[]{:S(2)}, u32[]{:S(2)}) collective-permute-start(bf16[144,640]{1,0:T(8,128)(2,1)} %pack_rows.1.rest_0_), channel_id=1, source_target_pairs={{0,4},{1,7},{2,6},{3,5},{4,8},{5,11},{6,10},{7,9},{8,12},{9,15},{1... | collective-permute-start | bytes 552968 | tf_op jit(solution)/shard_map/ppermute | solution.py:189
  8.6 1.5 %collective-permute-start = (bf16[144,640]{1,0:T(8,128)(2,1)}, bf16[144,640]{1,0:T(8,128)(2,1)S(1)}, u32[]{:S(2)}, u32[]{:S(2)}) collective-permute-start(bf16[144,640]{1,0:T(8,128)(2,1)} %pack_rows.1.rest_0_), channel_id=1, source_target_pairs={{0,2},{1,3},{2,0},{3,1},{4,6},{5,7},{6,4},{7,5},{8,10},{9,11},{10,... | collective-permute-start | bytes 552968 | tf_op jit(solution)/shard_map/ppermute | solution.py:189
  10.1 2.9 %collective-permute-done.3.rest_4_ = bf16[144,640]{1,0:T(8,128)(2,1)S(1)} collective-permute-done((bf16[144,640]{1,0:T(8,128)(2,1)}, bf16[144,640]{1,0:T(8,128)(2,1)S(1)}, u32[]{:S(2)}, u32[]{:S(2)}) %collective-permute-start.3) | collective-permute-done | bytes 184352 | tf_op jit(solution)/shard_map/ppermute | solution.py:189
  13.0 0.0 collective-permute-start.6
  13.0 11.4 %collective-permute-done.2.rest_3_ = bf16[144,640]{1,0:T(8,128)(2,1)S(1)} collective-permute-done((bf16[144,640]{1,0:T(8,128)(2,1)}, bf16[144,640]{1,0:T(8,128)(2,1)S(1)}, u32[]{:S(2)}, u32[]{:S(2)}) %collective-permute-start.2) | collective-permute-done | bytes 184352 | tf_op jit(solution)/shard_map/ppermute | solution.py:189
  24.4 0.0 collective-permute-start.5
  24.4 0.0 collective-permute-done.1.rest_2_
  24.4 0.5 collective-permute-start.4
  24.9 8.3 %prepare.1 = (bf16[8192,128]{1,0:T(8,128)(2,1)}, bf16[4096,512]{1,0:T(8,128)(2,1)}) custom-call(s32[8]{0:T(128)} %order_ref.3, bf16[128,6144]{1,0:T(8,128)(2,1)} %q_ref.1, bf16[512,4096]{1,0:T(8,128)(2,1)} %wv_ref.1), custom_call_target="tpu_custom_call" | custom-call | flops 3145728 | bytes 12582912 | tf_op jit(solution)/shard_map/prepare/pallas_call | solution.py:86
  33.1 0.0 collective-permute-done.rest_1_
  33.1 0.0 collective-permute-done.6.rest_7_
  33.2 0.0 collective-permute-done.5.rest_6_
  33.2 0.0 collective-permute-done.4.rest_5_
  33.2 0.0 copy-done
  33.2 0.0 copy-start.1
  33.2 1.6 %copy-done.1 = bf16[8192,128]{1,0:T(8,128)(2,1)S(1)} copy-done((bf16[8192,128]{1,0:T(8,128)(2,1)S(1)}, bf16[8192,128]{1,0:T(8,128)(2,1)}, u32[]{:S(2)}) %copy-start.1) | copy-done | bytes 2097176
  34.8 35.7 %attend.1 = bf16[128,4096]{1,0:T(8,128)(2,1)} custom-call(bf16[8192,128]{1,0:T(8,128)(2,1)S(1)} %copy-done.1, bf16[512,4096]{1,0:T(8,128)(2,1)} %wk_ref.1, bf16[4096,512]{1,0:T(8,128)(2,1)} %get-tuple-element.8.wvt_ref, bf16[144,640]{1,0:T(8,128)(2,1)S(1)} %copy-done, bf16[144,640]{1,0:T(8,128)(2,1)S(1)} %collective-permute-done.rest_1_, ...), custom_call_target="tpu_custom_call" | custom-call | flops 12079595520 | bytes 8388608 | tf_op jit(solution)/shard_map/attend/pallas_call | solution.py:155
Async XLA Ops:
  2.5 30.7 %copy-start = (bf16[144,640]{1,0:T(8,128)(2,1)S(1)}, bf16[144,640]{1,0:T(8,128)(2,1)}, u32[]{:S(2)}) copy-start(bf16[144,640]{1,0:T(8,128)(2,1)} %pack_rows.1.rest_0_) | copy-start | bytes 552964
  2.5 10.5 %collective-permute-start.3 = (bf16[144,640]{1,0:T(8,128)(2,1)}, bf16[144,640]{1,0:T(8,128)(2,1)S(1)}, u32[]{:S(2)}, u32[]{:S(2)}) collective-permute-start(bf16[144,640]{1,0:T(8,128)(2,1)} %pack_rows.1.rest_0_), channel_id=1, source_target_pairs={{0,12},{1,15},{2,14},{3,13},{4,0},{5,3},{6,2},{7,1},{8,4},{9,7},{1... | collective-permute-start | bytes 552968 | tf_op jit(solution)/shard_map/ppermute | solution.py:189
  7.6 16.8 %collective-permute-start.2 = (bf16[144,640]{1,0:T(8,128)(2,1)}, bf16[144,640]{1,0:T(8,128)(2,1)S(1)}, u32[]{:S(2)}, u32[]{:S(2)}) collective-permute-start(bf16[144,640]{1,0:T(8,128)(2,1)} %pack_rows.1.rest_0_), channel_id=1, source_target_pairs={{0,8},{1,11},{2,10},{3,9},{4,12},{5,15},{6,14},{7,13},{8,0},{9,3},... | collective-permute-start | bytes 552968 | tf_op jit(solution)/shard_map/ppermute | solution.py:189
  7.6 16.8 %collective-permute-start.1 = (bf16[144,640]{1,0:T(8,128)(2,1)}, bf16[144,640]{1,0:T(8,128)(2,1)S(1)}, u32[]{:S(2)}, u32[]{:S(2)}) collective-permute-start(bf16[144,640]{1,0:T(8,128)(2,1)} %pack_rows.1.rest_0_), channel_id=1, source_target_pairs={{0,4},{1,7},{2,6},{3,5},{4,8},{5,11},{6,10},{7,9},{8,12},{9,15},{1... | collective-permute-start | bytes 552968 | tf_op jit(solution)/shard_map/ppermute | solution.py:189
  8.6 24.6 %collective-permute-start = (bf16[144,640]{1,0:T(8,128)(2,1)}, bf16[144,640]{1,0:T(8,128)(2,1)S(1)}, u32[]{:S(2)}, u32[]{:S(2)}) collective-permute-start(bf16[144,640]{1,0:T(8,128)(2,1)} %pack_rows.1.rest_0_), channel_id=1, source_target_pairs={{0,2},{1,3},{2,0},{3,1},{4,6},{5,7},{6,4},{7,5},{8,10},{9,11},{10,... | collective-permute-start | bytes 552968 | tf_op jit(solution)/shard_map/ppermute | solution.py:189
  13.0 20.2 %collective-permute-start.6 = (bf16[144,640]{1,0:T(8,128)(2,1)S(1)}, bf16[144,640]{1,0:T(8,128)(2,1)S(1)}, u32[]{:S(2)}, u32[]{:S(2)}) collective-permute-start(bf16[144,640]{1,0:T(8,128)(2,1)S(1)} %collective-permute-done.3.rest_4_), channel_id=1, source_target_pairs={{0,1},{1,0},{2,3},{3,2},{4,5},{5,4},{6,7},{7,6},{8,9},{9,8},{10,11... | collective-permute-start | bytes 552968 | tf_op jit(solution)/shard_map/ppermute | solution.py:189
  24.4 8.8 %collective-permute-start.5 = (bf16[144,640]{1,0:T(8,128)(2,1)S(1)}, bf16[144,640]{1,0:T(8,128)(2,1)S(1)}, u32[]{:S(2)}, u32[]{:S(2)}) collective-permute-start(bf16[144,640]{1,0:T(8,128)(2,1)S(1)} %collective-permute-done.2.rest_3_), channel_id=1, source_target_pairs={{0,1},{1,0},{2,3},{3,2},{4,5},{5,4},{6,7},{7,6},{8,9},{9,8},{10,11... | collective-permute-start | bytes 552968 | tf_op jit(solution)/shard_map/ppermute | solution.py:189
  24.4 8.8 %collective-permute-start.4 = (bf16[144,640]{1,0:T(8,128)(2,1)S(1)}, bf16[144,640]{1,0:T(8,128)(2,1)S(1)}, u32[]{:S(2)}, u32[]{:S(2)}) collective-permute-start(bf16[144,640]{1,0:T(8,128)(2,1)S(1)} %collective-permute-done.1.rest_2_), channel_id=1, source_target_pairs={{0,1},{1,0},{2,3},{3,2},{4,5},{5,4},{6,7},{7,6},{8,9},{9,8},{10,11... | collective-permute-start | bytes 552968 | tf_op jit(solution)/shard_map/ppermute | solution.py:189
  33.2 1.6 %copy-start.1 = (bf16[8192,128]{1,0:T(8,128)(2,1)S(1)}, bf16[8192,128]{1,0:T(8,128)(2,1)}, u32[]{:S(2)}) copy-start(bf16[8192,128]{1,0:T(8,128)(2,1)} %get-tuple-element.7.qt_ref) | copy-start | bytes 6291460

commit v3 on v2

v3 whole, which is shorter than its diff:
```python
import functools
import math

import jax
import jax.numpy as jnp
from jax import lax
from jax.experimental import pallas as pl
from jax.experimental.pallas import tpu as pltpu
from jax.sharding import PartitionSpec as P

LATENT = 512
ROPE = 64
NOPE = 128
VDIM = 128
PACKED = 640
QK = 256
NEG = -1e30
AXES = ("ctx", "head")
BF = jnp.bfloat16
F32 = jnp.float32


def vmem_spec():
    return pl.BlockSpec(memory_space=pltpu.VMEM)


def smem_spec():
    return pl.BlockSpec(memory_space=pltpu.SMEM)


def any_spec():
    return pl.BlockSpec(memory_space=pl.ANY)


def pack_kernel(shard_count, order_ref, prefix_ref, span_ref, cache_ref, gain_ref, out_ref):
    tok_rows = span_ref.shape[1]
    cache_rows = cache_ref.shape[0]
    me = lax.axis_index("ctx")
    latent = span_ref[:LATENT, :].astype(F32)
    mean_square = jnp.mean(latent * latent, axis=0, keepdims=True)
    normed = (latent * lax.rsqrt(mean_square + 1e-06)).T * gain_ref[...]
    out_ref[:tok_rows, :LATENT] = normed.astype(BF)
    rest = lax.broadcasted_iota(jnp.int32, (ROPE, tok_rows), 0)
    rest = jnp.where(rest == order_ref[me], 1.0, 0.0)
    tail = jnp.concatenate([span_ref[LATENT:, :].astype(F32), rest], axis=0)
    out_ref[:tok_rows, LATENT:] = tail.T.astype(BF)
    out_ref[tok_rows:, :LATENT] = cache_ref[:, :LATENT]
    lanes = lax.broadcasted_iota(jnp.int32, (cache_rows, 128), 1)
    slots = me * cache_rows + lax.broadcasted_iota(jnp.int32, (cache_rows, 128), 0)
    hidden = jnp.logical_and(lanes == ROPE + shard_count, slots >= prefix_ref[0])
    out_ref[tok_rows:, LATENT:] = jnp.where(hidden, 1.0, 0.0).astype(BF)
    out_ref[tok_rows:, LATENT : LATENT + ROPE] = cache_ref[:, LATENT:]


def pack(span_latents, cache_latents, gain, prefix_length, block_order):
    rows = span_latents.shape[0] + cache_latents.shape[0]
    return pl.pallas_call(
        functools.partial(pack_kernel, block_order.shape[0]),
        out_shape=jax.ShapeDtypeStruct((rows, PACKED), BF),
        in_specs=[smem_spec(), smem_spec(), vmem_spec(), vmem_spec(), vmem_spec()],
        out_specs=vmem_spec(),
        name="pack_rows",
    )(block_order, prefix_length, span_latents.T, cache_latents, gain.reshape(1, LATENT))


def prepare_kernel(order_ref, q_ref, wk_ref, q_out_ref, wkt_ref):
    me = lax.axis_index("ctx")
    rows = q_ref.shape[0]
    lanes = lax.broadcasted_iota(jnp.int32, (rows, 128), 1)
    low = lanes < ROPE
    hide = jnp.where(lanes - ROPE > order_ref[me], NEG, 0.0)
    for pair in range(q_ref.shape[1] // 384):
        base = pair * 384
        second = q_ref[:, base + 128 : base + 256].astype(F32)
        third = q_ref[:, base + 256 : base + 384].astype(F32)
        second_turned = pltpu.roll(second, 64, 1)
        third_turned = pltpu.roll(third, 64, 1)
        to = pair * 2 * QK
        q_out_ref[:, to : to + 128] = q_ref[:, base : base + 128]
        q_out_ref[:, to + 128 : to + 256] = jnp.where(low, second, hide).astype(BF)
        q_out_ref[:, to + 256 : to + 384] = jnp.where(low, second_turned, third_turned).astype(BF)
        q_out_ref[:, to + 384 : to + 512] = jnp.where(low, third_turned, hide).astype(BF)
    wkt_ref[...] = wk_ref[...].T


def prepare(queries, key_weight, block_order):
    rows, width = queries.shape
    heads = width // (NOPE + ROPE)
    steps = 8
    return pl.pallas_call(
        prepare_kernel,
        out_shape=(
            jax.ShapeDtypeStruct((rows, heads * QK), BF),
            jax.ShapeDtypeStruct((heads * NOPE, LATENT), BF),
        ),
        grid=(steps,),
        in_specs=[
            smem_spec(),
            pl.BlockSpec((rows, width // steps), lambda i: (0, i)),
            pl.BlockSpec((LATENT, heads * NOPE // steps), lambda i: (0, i)),
        ],
        out_specs=(
            pl.BlockSpec((rows, heads * QK // steps), lambda i: (0, i)),
            pl.BlockSpec((heads * NOPE // steps, LATENT), lambda i: (i, 0)),
        ),
        cost_estimate=pl.CostEstimate(
            flops=rows * width * 4, bytes_accessed=LATENT * heads * NOPE * 6, transcendentals=0
        ),
        name="prepare",
    )(block_order, queries, key_weight)


def attend_kernel(blocks, tok_rows, heads, q_ref, wkt_ref, wv_ref, *rest):
    sources = rest[:blocks]
    out_ref, rows_ref, turned_ref = rest[blocks:]
    own_rows = sources[0].shape[0]

    @pl.when(pl.program_id(0) == 0)
    def _():
        for slot in range(blocks):
            rows_ref[slot * own_rows : (slot + 1) * own_rows, :] = sources[slot][...]
        turned_ref[...] = rows_ref[...].T

    scale = math.log2(math.e) / math.sqrt(NOPE + ROPE)
    row_ids = lax.broadcasted_iota(jnp.int32, (tok_rows, tok_rows), 0)
    col_ids = lax.broadcasted_iota(jnp.int32, (tok_rows, tok_rows), 1)
    causal = jnp.where(col_ids <= row_ids, 0.0, NEG)
    keys = jnp.dot(wkt_ref[...], turned_ref[:LATENT, :], preferred_element_type=F32).astype(BF)
    tail = turned_ref[LATENT:, :]
    weights = []
    sums = []
    for head in range(heads):
        full = jnp.concatenate([keys[head * NOPE : head * NOPE + NOPE], tail], axis=0)
        scores = jnp.dot(q_ref[:, head * QK : head * QK + QK], full, preferred_element_type=F32)
        scores = jnp.concatenate([scores[:, :tok_rows] + causal, scores[:, tok_rows:]], axis=1)
        row_max = jnp.max(scores, axis=1, keepdims=True)
        exponent = jnp.exp2((scores - row_max) * scale)
        sums.append(jnp.sum(exponent, axis=1, keepdims=True))
        weights.append(exponent.astype(BF))
    mixed = jnp.dot(jnp.concatenate(weights, axis=0), rows_ref[:, :LATENT], preferred_element_type=F32).astype(BF)
    for head in range(heads):
        wv = wv_ref[:, head * VDIM : head * VDIM + VDIM]
        out = jnp.dot(mixed[head * tok_rows : (head + 1) * tok_rows], wv, preferred_element_type=F32)
        out_ref[:, head * VDIM : head * VDIM + VDIM] = (out / sums[head]).astype(BF)


def attend(arranged, keys_turned, value_weight, blocks):
    tok_rows = arranged.shape[0]
    all_heads = value_weight.shape[1] // VDIM
    keys = len(blocks) * blocks[0].shape[0]
    heads = 4 if keys <= 2048 else 2
    return pl.pallas_call(
        functools.partial(attend_kernel, len(blocks), tok_rows, heads),
        out_shape=jax.ShapeDtypeStruct((tok_rows, all_heads * VDIM), BF),
        grid=(all_heads // heads,),
        in_specs=[
            pl.BlockSpec((tok_rows, heads * QK), lambda i: (0, i)),
            pl.BlockSpec((heads * NOPE, LATENT), lambda i: (i, 0)),
            pl.BlockSpec((LATENT, heads * VDIM), lambda i: (0, i)),
        ]
        + [vmem_spec()] * len(blocks),
        out_specs=pl.BlockSpec((tok_rows, heads * VDIM), lambda i: (0, i)),
        scratch_shapes=[pltpu.VMEM((keys, PACKED), BF), pltpu.VMEM((PACKED, keys), BF)],
        compiler_params=pltpu.CompilerParams(vmem_limit_bytes=(24 if keys <= 2048 else 56) * 1024 * 1024),
        cost_estimate=pl.CostEstimate(
            flops=2 * keys * all_heads * (LATENT * NOPE + tok_rows * (QK + LATENT)),
            bytes_accessed=LATENT * all_heads * 512,
            transcendentals=keys * tok_rows * all_heads,
        ),
        name="attend",
    )(arranged, keys_turned, value_weight, *blocks)


def exchange(own, shard_count, beside):
    line = shard_count // 2

    def move(value, route):
        pairs = []
        for place in range(line):
            for side in range(2):
                for core in range(2):
                    to_place, to_side, to_core = route(place, side, core)
                    source = (place * 2 + side) * 2 + core
                    target = ((to_place % line) * 2 + to_side) * 2 + to_core
                    pairs.append((source, target))
        return lax.ppermute(value, AXES, pairs)

    steps = range(1, line)
    along = [move(own, lambda p, s, c, k=k: (p + k, s ^ c, c)) for k in steps]
    across = move(own, lambda p, s, c: (p, 1 - s, c))
    along, beside = lax.optimization_barrier((along, beside))
    swapped = [move(a, lambda p, s, c: (p, s, 1 - c)) for a in along]
    return [across] + along + swapped, *beside


def per_device(
    queries,
    span_latents,
    cache_latents,
    latent_gain,
    key_weight,
    value_weight,
    prefix_length,
    block_order,
):
    shard_count = lax.axis_size("ctx")
    own = pack(span_latents, cache_latents, latent_gain, prefix_length, block_order)
    arranged, keys_turned = prepare(queries, key_weight, block_order)
    others, arranged, keys_turned = exchange(own, shard_count, (arranged, keys_turned))
    return attend(arranged, keys_turned, value_weight, [own] + others)


def solution(mesh):
    return jax.shard_map(
        per_device,
        mesh=mesh,
        in_specs=(
            P(("groups", "ctx"), "head"),
            P(("groups", "ctx"), None),
            P(("groups", "ctx"), None),
            P(),
            P(None, "head"),
            P(None, "head"),
            P("groups"),
            P("groups"),
        ),
        out_specs=P(("groups", "ctx"), "head"),
        check_vma=False,
    )
```

time: 70.8 us -> 53.2 us (0.75)
  Pallas kernels: 45.8 us -> 30.7 us
  waiting for transfers between devices: 14.3 us -> 7.39 us
  local copies, waits for them, and re-layouts: 1.59 us -> 5.97 us
    pallas_call x1, Pallas kernels: 35.7 us -> 20.5 us  [attend(): pl.pallas_call(functools.partial(attend_kernel, len(blocks), tok_rows, he...]
    ppermute x7, waiting for transfers between devices: 14.3 us -> 7.39 us  [move(): return lax.ppermute(value, AXES, pairs)]
    unnamed x4 -> x8, local copies, waits for them, and re-layouts: 1.59 us -> 5.97 us
  transfers between devices with their start and end apart: 7 -> 7, of which waited for: 2 -> 4; matrix products, arithmetic and copies ran while one was open for 0% -> 0% of each run, Pallas kernels for 12% -> 16%
where the time goes in v3:
time: 53.2 us; the launch traced here: 52.8 us
  Pallas kernels  30.7 us (58%)
  starting transfers between devices  8.1 us (15%)
  waiting for transfers between devices  7.39 us (14%)
  local copies, waits for them, and re-layouts  5.97 us (11%)
  between operations  0.66 us (1%)
    pallas_call x1, Pallas kernels, attend(): pl.pallas_call(functools.partial(attend_kernel, len(blocks), tok_rows, he...  20.5 us
    pallas_call x1, Pallas kernels, prepare(): pl.pallas_call(prepare_kernel, out_shape=(jax.ShapeDtypeStruct((rows, hea...  8.31 us
    ppermute x7, starting transfers between devices, move(): return lax.ppermute(value, AXES, pairs)  8.1 us
    ppermute x7, waiting for transfers between devices, move(): return lax.ppermute(value, AXES, pairs)  7.39 us
    unnamed x8, local copies, waits for them, and re-layouts  5.97 us
    pallas_call x1, Pallas kernels, pack(): pl.pallas_call(functools.partial(pack_kernel, block_order.shape[0]), out_...  1.86 us
  transfers between devices with their start and end apart: 7, of which 4 were waited for; matrix products, arithmetic and copies ran while one was open for 0% of the time, Pallas kernels for 16%

profile of v3, /device:TPU:0, one launch (start us, length us, event | category | flops | bytes accessed | tf_op | source)
XLA Modules:
  0.0 52.8 jit_solution(2508744117205162338)
XLA Ops:
  0.7 1.9 %pack_rows.1.rest_0_ = bf16[144,640]{1,0:T(8,128)(2,1)} custom-call(s32[8]{0:T(128)} %order_ref.3, s32[1]{0:T(128)S(6)} %copy.9.prefix_ref, bf16[576,128]{1,0:T(8,128)(2,1)} %bitcast.2, bf16[16,576]{1,0:T(8,128)(2,1)} %cache_ref.1, f32[1,512]{1,0:T(1,128)} %bitcast.3), custom_call_target="tpu_custom_call" | custom-call | tf_op jit(solution)/shard_map/pack_rows/pallas_call | solution.py:57
  2.5 0.0 copy-start
  2.5 5.0 %collective-permute-start.2 = (bf16[144,640]{1,0:T(8,128)(2,1)}, bf16[144,640]{1,0:T(8,128)(2,1)S(1)}, u32[]{:S(2)}, u32[]{:S(2)}) collective-permute-start(bf16[144,640]{1,0:T(8,128)(2,1)} %pack_rows.1.rest_0_), channel_id=1, source_target_pairs={{0,12},{1,15},{2,14},{3,13},{4,0},{5,3},{6,2},{7,1},{8,4},{9,7},{1... | collective-permute-start | bytes 552968 | tf_op jit(solution)/shard_map/ppermute | solution.py:186
  7.6 0.0 collective-permute-start.1
  7.6 1.0 %collective-permute-start = (bf16[144,640]{1,0:T(8,128)(2,1)}, bf16[144,640]{1,0:T(8,128)(2,1)S(1)}, u32[]{:S(2)}, u32[]{:S(2)}) collective-permute-start(bf16[144,640]{1,0:T(8,128)(2,1)} %pack_rows.1.rest_0_), channel_id=1, source_target_pairs={{0,4},{1,7},{2,6},{3,5},{4,8},{5,11},{6,10},{7,9},{8,12},{9,15},{1... | collective-permute-start | bytes 552968 | tf_op jit(solution)/shard_map/ppermute | solution.py:186
  8.6 1.5 %collective-permute-start.3 = (bf16[144,640]{1,0:T(8,128)(2,1)}, bf16[144,640]{1,0:T(8,128)(2,1)S(1)}, u32[]{:S(2)}, u32[]{:S(2)}) collective-permute-start(bf16[144,640]{1,0:T(8,128)(2,1)} %pack_rows.1.rest_0_), channel_id=1, source_target_pairs={{0,2},{1,3},{2,0},{3,1},{4,6},{5,7},{6,4},{7,5},{8,10},{9,11},{10,... | collective-permute-start | bytes 552968 | tf_op jit(solution)/shard_map/ppermute | solution.py:186
  10.1 8.3 %prepare.1 = (bf16[128,8192]{1,0:T(8,128)(2,1)}, bf16[4096,512]{1,0:T(8,128)(2,1)}) custom-call(s32[8]{0:T(128)} %order_ref.3, bf16[128,6144]{1,0:T(8,128)(2,1)} %q_ref.1, bf16[512,4096]{1,0:T(8,128)(2,1)} %wk_ref.1), custom_call_target="tpu_custom_call" | custom-call | flops 3145728 | bytes 12582912 | tf_op jit(solution)/shard_map/prepare/pallas_call | solution.py:90
  18.4 0.0 collective-permute-done.2.rest_4_
  18.4 6.0 %collective-permute-done.1.rest_3_ = bf16[144,640]{1,0:T(8,128)(2,1)S(1)} collective-permute-done((bf16[144,640]{1,0:T(8,128)(2,1)}, bf16[144,640]{1,0:T(8,128)(2,1)S(1)}, u32[]{:S(2)}, u32[]{:S(2)}) %collective-permute-start.1) | collective-permute-done | bytes 184352 | tf_op jit(solution)/shard_map/ppermute | solution.py:186
  24.4 0.0 collective-permute-done.rest_2_
  24.4 0.0 collective-permute-start.4
  24.4 0.5 collective-permute-start.5
  24.9 0.0 collective-permute-start.6
  24.9 0.0 collective-permute-done.3.rest_1_
  24.9 0.9 %collective-permute-done.4.rest_5_ = bf16[144,640]{1,0:T(8,128)(2,1)S(1)} collective-permute-done((bf16[144,640]{1,0:T(8,128)(2,1)S(1)}, bf16[144,640]{1,0:T(8,128)(2,1)S(1)}, u32[]{:S(2)}, u32[]{:S(2)}) %collective-permute-start.4) | collective-permute-done | bytes 184352 | tf_op jit(solution)/shard_map/ppermute | solution.py:186
  25.8 0.3 collective-permute-done.5.rest_6_
  26.1 0.3 collective-permute-done.6.rest_7_
  26.3 0.0 copy-done
  26.3 0.0 copy-start.1
  26.3 2.2 %copy-done.1 = bf16[512,4096]{1,0:T(8,128)(2,1)S(1)} copy-done((bf16[512,4096]{1,0:T(8,128)(2,1)S(1)}, bf16[512,4096]{1,0:T(8,128)(2,1)}, u32[]{:S(2)}) %copy-start.1) | copy-done | bytes 4194328
  28.5 0.0 copy-start.2
  28.5 2.2 %copy-done.2 = bf16[4096,512]{1,0:T(8,128)(2,1)S(1)} copy-done((bf16[4096,512]{1,0:T(8,128)(2,1)S(1)}, bf16[4096,512]{1,0:T(8,128)(2,1)}, u32[]{:S(2)}) %copy-start.2) | copy-done | bytes 4194328
  30.7 0.0 copy-start.3
  30.7 1.6 %copy-done.3 = bf16[128,8192]{1,0:T(8,128)(2,1)S(1)} copy-done((bf16[128,8192]{1,0:T(8,128)(2,1)S(1)}, bf16[128,8192]{1,0:T(8,128)(2,1)}, u32[]{:S(2)}) %copy-start.3) | copy-done | bytes 2097176
  32.3 20.5 %attend.1 = bf16[128,4096]{1,0:T(8,128)(2,1)} custom-call(bf16[128,8192]{1,0:T(8,128)(2,1)S(1)} %copy-done.3, bf16[4096,512]{1,0:T(8,128)(2,1)S(1)} %copy-done.2, bf16[512,4096]{1,0:T(8,128)(2,1)S(1)} %copy-done.1, bf16[144,640]{1,0:T(8,128)(2,1)S(1)} %copy-done, bf16[144,640]{1,0:T(8,128)(2,1)S(1)} %collective-permute-done.3.rest_1_, ...), custom_call_target="tpu_custom_call" | custom-call | flops 12079595520 | bytes 8388608 | tf_op jit(solution)/shard_map/attend/pallas_call | solution.py:152
Async XLA Ops:
  2.5 23.8 %copy-start = (bf16[144,640]{1,0:T(8,128)(2,1)S(1)}, bf16[144,640]{1,0:T(8,128)(2,1)}, u32[]{:S(2)}) copy-start(bf16[144,640]{1,0:T(8,128)(2,1)} %pack_rows.1.rest_0_) | copy-start | bytes 552964
  2.5 15.9 %collective-permute-start.2 = (bf16[144,640]{1,0:T(8,128)(2,1)}, bf16[144,640]{1,0:T(8,128)(2,1)S(1)}, u32[]{:S(2)}, u32[]{:S(2)}) collective-permute-start(bf16[144,640]{1,0:T(8,128)(2,1)} %pack_rows.1.rest_0_), channel_id=1, source_target_pairs={{0,12},{1,15},{2,14},{3,13},{4,0},{5,3},{6,2},{7,1},{8,4},{9,7},{1... | collective-permute-start | bytes 552968 | tf_op jit(solution)/shard_map/ppermute | solution.py:186
  7.6 16.8 %collective-permute-start.1 = (bf16[144,640]{1,0:T(8,128)(2,1)}, bf16[144,640]{1,0:T(8,128)(2,1)S(1)}, u32[]{:S(2)}, u32[]{:S(2)}) collective-permute-start(bf16[144,640]{1,0:T(8,128)(2,1)} %pack_rows.1.rest_0_), channel_id=1, source_target_pairs={{0,8},{1,11},{2,10},{3,9},{4,12},{5,15},{6,14},{7,13},{8,0},{9,3},... | collective-permute-start | bytes 552968 | tf_op jit(solution)/shard_map/ppermute | solution.py:186
  7.6 16.8 %collective-permute-start = (bf16[144,640]{1,0:T(8,128)(2,1)}, bf16[144,640]{1,0:T(8,128)(2,1)S(1)}, u32[]{:S(2)}, u32[]{:S(2)}) collective-permute-start(bf16[144,640]{1,0:T(8,128)(2,1)} %pack_rows.1.rest_0_), channel_id=1, source_target_pairs={{0,4},{1,7},{2,6},{3,5},{4,8},{5,11},{6,10},{7,9},{8,12},{9,15},{1... | collective-permute-start | bytes 552968 | tf_op jit(solution)/shard_map/ppermute | solution.py:186
  8.6 16.3 %collective-permute-start.3 = (bf16[144,640]{1,0:T(8,128)(2,1)}, bf16[144,640]{1,0:T(8,128)(2,1)S(1)}, u32[]{:S(2)}, u32[]{:S(2)}) collective-permute-start(bf16[144,640]{1,0:T(8,128)(2,1)} %pack_rows.1.rest_0_), channel_id=1, source_target_pairs={{0,2},{1,3},{2,0},{3,1},{4,6},{5,7},{6,4},{7,5},{8,10},{9,11},{10,... | collective-permute-start | bytes 552968 | tf_op jit(solution)/shard_map/ppermute | solution.py:186
  24.4 1.4 %collective-permute-start.4 = (bf16[144,640]{1,0:T(8,128)(2,1)S(1)}, bf16[144,640]{1,0:T(8,128)(2,1)S(1)}, u32[]{:S(2)}, u32[]{:S(2)}) collective-permute-start(bf16[144,640]{1,0:T(8,128)(2,1)S(1)} %collective-permute-done.rest_2_), channel_id=1, source_target_pairs={{0,1},{1,0},{2,3},{3,2},{4,5},{5,4},{6,7},{7,6},{8,9},{9,8},{10,11... | collective-permute-start | bytes 552968 | tf_op jit(solution)/shard_map/ppermute | solution.py:186
  24.4 1.7 %collective-permute-start.5 = (bf16[144,640]{1,0:T(8,128)(2,1)S(1)}, bf16[144,640]{1,0:T(8,128)(2,1)S(1)}, u32[]{:S(2)}, u32[]{:S(2)}) collective-permute-start(bf16[144,640]{1,0:T(8,128)(2,1)S(1)} %collective-permute-done.1.rest_3_), channel_id=1, source_target_pairs={{0,1},{1,0},{2,3},{3,2},{4,5},{5,4},{6,7},{7,6},{8,9},{9,8},{10,11... | collective-permute-start | bytes 552968 | tf_op jit(solution)/shard_map/ppermute | solution.py:186
  24.9 1.4 %collective-permute-start.6 = (bf16[144,640]{1,0:T(8,128)(2,1)S(1)}, bf16[144,640]{1,0:T(8,128)(2,1)S(1)}, u32[]{:S(2)}, u32[]{:S(2)}) collective-permute-start(bf16[144,640]{1,0:T(8,128)(2,1)S(1)} %collective-permute-done.2.rest_4_), channel_id=1, source_target_pairs={{0,1},{1,0},{2,3},{3,2},{4,5},{5,4},{6,7},{7,6},{8,9},{9,8},{10,11... | collective-permute-start | bytes 552968 | tf_op jit(solution)/shard_map/ppermute | solution.py:186
  26.3 2.2 %copy-start.1 = (bf16[512,4096]{1,0:T(8,128)(2,1)S(1)}, bf16[512,4096]{1,0:T(8,128)(2,1)}, u32[]{:S(2)}) copy-start(bf16[512,4096]{1,0:T(8,128)(2,1)} %wv_ref.1) | copy-start | bytes 12582916
  28.5 2.2 %copy-start.2 = (bf16[4096,512]{1,0:T(8,128)(2,1)S(1)}, bf16[4096,512]{1,0:T(8,128)(2,1)}, u32[]{:S(2)}) copy-start(bf16[4096,512]{1,0:T(8,128)(2,1)} %get-tuple-element.15.wkt_ref) | copy-start | bytes 12582916
  30.7 1.6 %copy-start.3 = (bf16[128,8192]{1,0:T(8,128)(2,1)S(1)}, bf16[128,8192]{1,0:T(8,128)(2,1)}, u32[]{:S(2)}) copy-start(bf16[128,8192]{1,0:T(8,128)(2,1)} %get-tuple-element.14.q_ref) | copy-start | bytes 6291460

commit v4 on v3

v4 whole, which is shorter than its diff:
```python
import functools
import math

import jax
import jax.numpy as jnp
from jax import lax
from jax.experimental import pallas as pl
from jax.experimental.pallas import tpu as pltpu
from jax.sharding import PartitionSpec as P

LATENT = 512
ROPE = 64
NOPE = 128
VDIM = 128
PACKED = 640
QK = 256
NEG = -1e30
AXES = ("ctx", "head")
BF = jnp.bfloat16
F32 = jnp.float32


def vmem_spec():
    return pl.BlockSpec(memory_space=pltpu.VMEM)


def smem_spec():
    return pl.BlockSpec(memory_space=pltpu.SMEM)


def any_spec():
    return pl.BlockSpec(memory_space=pl.ANY)


def pack_kernel(shard_count, order_ref, prefix_ref, span_ref, cache_ref, gain_ref, out_ref, half_ref):
    tok_rows = span_ref.shape[1]
    cache_rows = cache_ref.shape[0]
    half_rows = tok_rows // 2
    me = lax.axis_index("ctx")
    core = lax.axis_index("head")
    latent = span_ref[:LATENT, :].astype(F32)
    mean_square = jnp.mean(latent * latent, axis=0, keepdims=True)
    normed = (latent * lax.rsqrt(mean_square + 1e-06)).T * gain_ref[...]
    rest = lax.broadcasted_iota(jnp.int32, (ROPE, tok_rows), 0)
    rest = jnp.where(rest == order_ref[me], 1.0, 0.0)
    tail = jnp.concatenate([span_ref[LATENT:, :].astype(F32), rest], axis=0)
    span = jnp.concatenate([normed, tail.T], axis=1)
    out_ref[:tok_rows, :] = span.astype(BF)
    half_ref[:half_rows, :] = jnp.where(core == 0, span[:half_rows], span[half_rows:]).astype(BF)
    lanes = lax.broadcasted_iota(jnp.int32, (cache_rows, 128), 1)
    slots = me * cache_rows + lax.broadcasted_iota(jnp.int32, (cache_rows, 128), 0)
    hidden = jnp.logical_and(lanes == ROPE + shard_count, slots >= prefix_ref[0])
    for ref, at in ((out_ref, tok_rows), (half_ref, half_rows)):
        ref[at:, :LATENT] = cache_ref[:, :LATENT]
        ref[at:, LATENT:] = jnp.where(hidden, 1.0, 0.0).astype(BF)
        ref[at:, LATENT : LATENT + ROPE] = cache_ref[:, LATENT:]


def pack(span_latents, cache_latents, gain, prefix_length, block_order):
    tok_rows = span_latents.shape[0]
    cache_rows = cache_latents.shape[0]
    return pl.pallas_call(
        functools.partial(pack_kernel, block_order.shape[0]),
        out_shape=(
            jax.ShapeDtypeStruct((tok_rows + cache_rows, PACKED), BF),
            jax.ShapeDtypeStruct((tok_rows // 2 + cache_rows, PACKED), BF),
        ),
        in_specs=[smem_spec(), smem_spec(), vmem_spec(), vmem_spec(), vmem_spec()],
        out_specs=(vmem_spec(), vmem_spec()),
        name="pack_rows",
    )(block_order, prefix_length, span_latents.T, cache_latents, gain.reshape(1, LATENT))


def turn_kernel(wk_ref, wkt_ref):
    wkt_ref[...] = wk_ref[...].T


def turn(key_weight):
    depth, width = key_weight.shape
    steps = 8
    return pl.pallas_call(
        turn_kernel,
        out_shape=jax.ShapeDtypeStruct((width, depth), BF),
        grid=(steps,),
        in_specs=[pl.BlockSpec((depth, width // steps), lambda i: (0, i))],
        out_specs=pl.BlockSpec((width // steps, depth), lambda i: (i, 0)),
        cost_estimate=pl.CostEstimate(flops=0, bytes_accessed=depth * width * 4, transcendentals=0),
        name="turn_key_weight",
    )(key_weight)


def attend_kernel(blocks, heads, order_ref, q_ref, wkt_ref, wv_ref, own_ref, *rest):
    halves = rest[: 2 * (blocks - 1)]
    out_ref, rows_ref, turned_ref, bias_ref = rest[2 * (blocks - 1) :]
    tok_rows = q_ref.shape[0]
    own_rows = own_ref.shape[0]
    half = tok_rows // 2
    keys_count = blocks * own_rows

    @pl.when(pl.program_id(0) == 0)
    def _():
        rows_ref[:own_rows, :] = own_ref[...]
        for slot in range(1, blocks):
            at = slot * own_rows
            mine, theirs = halves[2 * slot - 2 : 2 * slot]
            rows_ref[at : at + half, :] = mine[:half, :]
            rows_ref[at + half : at + tok_rows, :] = theirs[:half, :]
            rows_ref[at + tok_rows : at + own_rows, :] = mine[half:, :]
        turned_ref[...] = rows_ref[...].T
        marks = turned_ref[LATENT + ROPE :, :].astype(F32)
        places = lax.broadcasted_iota(jnp.int32, marks.shape, 0)
        hide = jnp.where(places > order_ref[lax.axis_index("ctx")], marks, 0.0)
        bias_ref[...] = jnp.sum(hide, axis=0, keepdims=True) * NEG

    scale = math.log2(math.e) / math.sqrt(NOPE + ROPE)
    row_ids = lax.broadcasted_iota(jnp.int32, (tok_rows, tok_rows), 0)
    col_ids = lax.broadcasted_iota(jnp.int32, (tok_rows, tok_rows), 1)
    causal = jnp.where(col_ids <= row_ids, 0.0, NEG)
    bias = bias_ref[...]
    keys = jnp.dot(wkt_ref[...], turned_ref[:LATENT, :], preferred_element_type=F32).astype(BF)
    rotary = turned_ref[LATENT : LATENT + ROPE, :]
    nothing = jnp.zeros((QK - NOPE - ROPE, keys_count), BF)
    weights = []
    sums = []
    for head in range(heads):
        nope = keys[head * NOPE : head * NOPE + NOPE]
        if head % 2 == 0:
            at = (head // 2) * 384
            full = jnp.concatenate([nope, rotary, nothing], axis=0)
        else:
            at = (head // 2) * 384 + 128
            full = jnp.concatenate([nothing, nope, rotary], axis=0)
        scores = jnp.dot(q_ref[:, at : at + QK], full, preferred_element_type=F32)
        scores = jnp.concatenate([scores[:, :tok_rows] + causal, scores[:, tok_rows:] + bias[:, tok_rows:]], axis=1)
        row_max = jnp.max(scores, axis=1, keepdims=True)
        exponent = jnp.exp2((scores - row_max) * scale)
        sums.append(jnp.sum(exponent, axis=1, keepdims=True))
        weights.append(exponent.astype(BF))
    mixed = jnp.dot(jnp.concatenate(weights, axis=0), rows_ref[:, :LATENT], preferred_element_type=F32).astype(BF)
    for head in range(heads):
        wv = wv_ref[:, head * VDIM : head * VDIM + VDIM]
        out = jnp.dot(mixed[head * tok_rows : (head + 1) * tok_rows], wv, preferred_element_type=F32)
        out_ref[:, head * VDIM : head * VDIM + VDIM] = (out / sums[head]).astype(BF)


def attend(queries, keys_turned, value_weight, block_order, own, halves):
    tok_rows = queries.shape[0]
    all_heads = value_weight.shape[1] // VDIM
    blocks = 1 + len(halves) // 2
    keys = blocks * own.shape[0]
    heads = 4 if keys <= 2048 else 2
    return pl.pallas_call(
        functools.partial(attend_kernel, blocks, heads),
        out_shape=jax.ShapeDtypeStruct((tok_rows, all_heads * VDIM), BF),
        grid=(all_heads // heads,),
        in_specs=[
            smem_spec(),
            pl.BlockSpec((tok_rows, heads * (NOPE + ROPE)), lambda i: (0, i)),
            pl.BlockSpec((heads * NOPE, LATENT), lambda i: (i, 0)),
            pl.BlockSpec((LATENT, heads * VDIM), lambda i: (0, i)),
        ]
        + [vmem_spec()] * (1 + len(halves)),
        out_specs=pl.BlockSpec((tok_rows, heads * VDIM), lambda i: (0, i)),
        scratch_shapes=[
            pltpu.VMEM((keys, PACKED), BF),
            pltpu.VMEM((PACKED, keys), BF),
            pltpu.VMEM((1, keys), F32),
        ],
        compiler_params=pltpu.CompilerParams(vmem_limit_bytes=54 * 1024 * 1024),
        cost_estimate=pl.CostEstimate(
            flops=2 * keys * all_heads * (LATENT * NOPE + tok_rows * (QK + LATENT)),
            bytes_accessed=LATENT * all_heads * 512,
            transcendentals=keys * tok_rows * all_heads,
        ),
        name="attend",
    )(block_order, queries, keys_turned, value_weight, own, *halves)


def exchange(half, shard_count, beside):
    line = shard_count // 2

    def move(value, route):
        pairs = []
        for place in range(line):
            for side in range(2):
                for core in range(2):
                    to_place, to_side, to_core = route(place, side, core)
                    source = (place * 2 + side) * 2 + core
                    target = ((to_place % line) * 2 + to_side) * 2 + to_core
                    pairs.append((source, target))
        return lax.ppermute(value, AXES, pairs)

    def cross(value):
        return move(value, lambda p, s, c: (p, 1 - s, c))

    def swap(value):
        return move(value, lambda p, s, c: (p, s, 1 - c))

    along = [move(half, lambda p, s, c, k=k: (p + k, s, c)) for k in range(1, line)]
    across = cross(half)
    along, across, beside = lax.optimization_barrier((along, across, beside))
    crossed = [cross(a) for a in along]
    mine = [across] + along + crossed
    halves = []
    for value in mine:
        halves += [value, swap(value)]
    return halves, beside


def per_device(
    queries,
    span_latents,
    cache_latents,
    latent_gain,
    key_weight,
    value_weight,
    prefix_length,
    block_order,
):
    shard_count = lax.axis_size("ctx")
    own, half = pack(span_latents, cache_latents, latent_gain, prefix_length, block_order)
    halves, keys_turned = exchange(half, shard_count, turn(key_weight))
    return attend(queries, keys_turned, value_weight, block_order, own, halves)


def solution(mesh):
    return jax.shard_map(
        per_device,
        mesh=mesh,
        in_specs=(
            P(("groups", "ctx"), "head"),
            P(("groups", "ctx"), None),
            P(("groups", "ctx"), None),
            P(),
            P(None, "head"),
            P(None, "head"),
            P("groups"),
            P("groups"),
        ),
        out_specs=P(("groups", "ctx"), "head"),
        check_vma=False,
    )
```

time: 53.2 us -> 53.5 us (level)
  local copies, waits for them, and re-layouts: 5.97 us -> 0.58 us
  starting transfers between devices: 8.1 us -> 10.9 us
  Pallas kernels: 30.7 us -> 32.6 us
  waiting for transfers between devices: 7.39 us -> 8.3 us
    unnamed x8 -> x28, local copies, waits for them, and re-layouts: 5.97 us -> 0.58 us
    ppermute x7 -> x14, starting transfers between devices: 8.1 us -> 10.9 us  [move(): return lax.ppermute(value, AXES, pairs)]
    pallas_call x2, Pallas kernels: 28.8 us -> 30.7 us  [the longest x1 23.5 us: attend(): pl.pallas_call(functools.partial(attend_kernel, blocks, heads), out_shape...]
    ppermute x7 -> x14, waiting for transfers between devices: 7.39 us -> 8.3 us  [move(): return lax.ppermute(value, AXES, pairs)]
  transfers between devices with their start and end apart: 7 -> 14, of which waited for: 4 -> 5; matrix products, arithmetic and copies ran while one was open for 0% -> 0% of each run, Pallas kernels for 16% -> 13%
where the time goes in v4:
time: 53.5 us; the launch traced here: 53.2 us
  Pallas kernels  32.6 us (61%)
  starting transfers between devices  10.9 us (20%)
  waiting for transfers between devices  8.3 us (16%)
  between operations  0.84 us (2%)
  local copies, waits for them, and re-layouts  0.58 us (1%)
    pallas_call x1, Pallas kernels, attend(): pl.pallas_call(functools.partial(attend_kernel, blocks, heads), out_shape...  23.5 us
    ppermute x14, starting transfers between devices, move(): return lax.ppermute(value, AXES, pairs)  10.9 us
    ppermute x14, waiting for transfers between devices, move(): return lax.ppermute(value, AXES, pairs)  8.3 us
    pallas_call x1, Pallas kernels, turn(): pl.pallas_call(turn_kernel, out_shape=jax.ShapeDtypeStruct((width, depth)...  7.17 us
    pallas_call x1, Pallas kernels, pack(): pl.pallas_call(functools.partial(pack_kernel, block_order.shape[0]), out_...  1.9 us
  transfers between devices with their start and end apart: 14, of which 5 were waited for; matrix products, arithmetic and copies ran while one was open for 0% of the time, Pallas kernels for 13%

profile of v4, /device:TPU:0, one launch (start us, length us, event | category | flops | bytes accessed | tf_op | source)
XLA Modules:
  0.0 53.2 jit_solution(5365772621068035223)
XLA Ops:
  0.7 1.9 %pack_rows.1 = (bf16[144,640]{1,0:T(8,128)(2,1)}, bf16[80,640]{1,0:T(8,128)(2,1)}) custom-call(s32[8]{0:T(128)} %order_ref.3, s32[1]{0:T(128)S(6)} %copy.9.prefix_ref, bf16[576,128]{1,0:T(8,128)(2,1)} %bitcast.2, bf16[16,576]{1,0:T(8,128)(2,1)} %cache_ref.1, f32[1,512]{1,0:T(1,128)} %bitcast.3), custom_call_target="tpu_custom_call" | custom-call | tf_op jit(solution)/shard_map/pack_rows/pallas_call | solution.py:62
  2.6 3.0 %collective-permute-start.3 = (bf16[80,640]{1,0:T(8,128)(2,1)}, bf16[80,640]{1,0:T(8,128)(2,1)S(1)}, u32[]{:S(2)}, u32[]{:S(2)}) collective-permute-start(bf16[80,640]{1,0:T(8,128)(2,1)} %get-tuple-element.12), channel_id=1, source_target_pairs={{0,2},{1,3},{2,0},{3,1},{4,6},{5,7},{6,4},{7,5},{8,10},{9,11},{10,... | collective-permute-start | bytes 307208 | tf_op jit(solution)/shard_map/ppermute | solution.py:191
  5.5 3.6 %collective-permute-start.2 = (bf16[80,640]{1,0:T(8,128)(2,1)}, bf16[80,640]{1,0:T(8,128)(2,1)S(1)}, u32[]{:S(2)}, u32[]{:S(2)}) collective-permute-start(bf16[80,640]{1,0:T(8,128)(2,1)} %get-tuple-element.12), channel_id=1, source_target_pairs={{0,12},{1,13},{2,14},{3,15},{4,0},{5,1},{6,2},{7,3},{8,4},{9,5},{1... | collective-permute-start | bytes 307208 | tf_op jit(solution)/shard_map/ppermute | solution.py:191
  9.1 0.0 collective-permute-start.1
  9.1 1.0 %collective-permute-start = (bf16[80,640]{1,0:T(8,128)(2,1)}, bf16[80,640]{1,0:T(8,128)(2,1)S(1)}, u32[]{:S(2)}, u32[]{:S(2)}) collective-permute-start(bf16[80,640]{1,0:T(8,128)(2,1)} %get-tuple-element.12), channel_id=1, source_target_pairs={{0,4},{1,5},{2,6},{3,7},{4,8},{5,9},{6,10},{7,11},{8,12},{9,13},{1... | collective-permute-start | bytes 307208 | tf_op jit(solution)/shard_map/ppermute | solution.py:191
  10.1 7.2 %turn_key_weight.1.wkt_ref = bf16[4096,512]{1,0:T(8,128)(2,1)} custom-call(bf16[512,4096]{1,0:T(8,128)(2,1)} %wk_ref.1), custom_call_target="tpu_custom_call" | custom-call | bytes 8388608 | tf_op jit(solution)/shard_map/turn_key_weight/pallas_call | solution.py:81
  17.3 0.0 collective-permute-done.3.rest_0_
  17.3 0.0 copy-start
  17.3 0.0 collective-permute-done.2.rest_6_
  17.3 0.0 copy-start.1
  17.3 0.7 %collective-permute-done.1.rest_4_ = bf16[80,640]{1,0:T(8,128)(2,1)S(1)} collective-permute-done((bf16[80,640]{1,0:T(8,128)(2,1)}, bf16[80,640]{1,0:T(8,128)(2,1)S(1)}, u32[]{:S(2)}, u32[]{:S(2)}) %collective-permute-start.1) | collective-permute-done | bytes 102432 | tf_op jit(solution)/shard_map/ppermute | solution.py:191
  18.0 0.0 copy-start.2
  18.0 0.0 collective-permute-done.rest_2_
  18.0 0.0 copy-start.3
  18.0 0.1 collective-permute-start.4
  18.1 0.6 %collective-permute-start.8 = (bf16[80,640]{1,0:T(8,128)(2,1)S(1)}, bf16[80,640]{1,0:T(8,128)(2,1)S(1)}, u32[]{:S(2)}, u32[]{:S(2)}) collective-permute-start(bf16[80,640]{1,0:T(8,128)(2,1)S(1)} %collective-permute-done.rest_2_), channel_id=1, source_target_pairs={{0,2},{1,3},{2,0},{3,1},{4,6},{5,7},{6,4},{7,5},{8,10},{9,11},{10,... | collective-permute-start | bytes 307208 | tf_op jit(solution)/shard_map/ppermute | solution.py:191
  18.6 0.2 collective-permute-start.5
  18.8 1.5 %collective-permute-start.10 = (bf16[80,640]{1,0:T(8,128)(2,1)S(1)}, bf16[80,640]{1,0:T(8,128)(2,1)S(1)}, u32[]{:S(2)}, u32[]{:S(2)}) collective-permute-start(bf16[80,640]{1,0:T(8,128)(2,1)S(1)} %collective-permute-done.1.rest_4_), channel_id=1, source_target_pairs={{0,2},{1,3},{2,0},{3,1},{4,6},{5,7},{6,4},{7,5},{8,10},{9,11},{10,... | collective-permute-start | bytes 307208 | tf_op jit(solution)/shard_map/ppermute | solution.py:191
  20.3 0.5 collective-permute-start.12
  20.8 0.0 collective-permute-done.4.rest_1_
  20.8 0.0 copy-start.4
  20.8 0.0 collective-permute-start.6
  20.8 3.0 %collective-permute-done.8.rest_8_ = bf16[80,640]{1,0:T(8,128)(2,1)S(1)} collective-permute-done((bf16[80,640]{1,0:T(8,128)(2,1)S(1)}, bf16[80,640]{1,0:T(8,128)(2,1)S(1)}, u32[]{:S(2)}, u32[]{:S(2)}) %collective-permute-start.8) | collective-permute-done | bytes 102432 | tf_op jit(solution)/shard_map/ppermute | solution.py:191
  23.8 0.0 copy-start.5
  23.8 0.0 collective-permute-start.7
  23.8 0.0 collective-permute-done.5.rest_3_
  23.8 0.0 copy-start.6
  23.8 0.5 collective-permute-start.9
  24.3 1.7 %collective-permute-done.10.rest_10_ = bf16[80,640]{1,0:T(8,128)(2,1)S(1)} collective-permute-done((bf16[80,640]{1,0:T(8,128)(2,1)S(1)}, bf16[80,640]{1,0:T(8,128)(2,1)S(1)}, u32[]{:S(2)}, u32[]{:S(2)}) %collective-permute-start.10) | collective-permute-done | bytes 102432 | tf_op jit(solution)/shard_map/ppermute | solution.py:191
  26.0 0.0 copy-start.7
  26.0 0.0 collective-permute-start.11
  26.0 1.7 %collective-permute-done.12.rest_12_ = bf16[80,640]{1,0:T(8,128)(2,1)S(1)} collective-permute-done((bf16[80,640]{1,0:T(8,128)(2,1)S(1)}, bf16[80,640]{1,0:T(8,128)(2,1)S(1)}, u32[]{:S(2)}, u32[]{:S(2)}) %collective-permute-start.12) | collective-permute-done | bytes 102432 | tf_op jit(solution)/shard_map/ppermute | solution.py:191
  27.8 0.0 copy-start.8
  27.8 0.0 collective-permute-start.13
  27.8 0.0 collective-permute-done.6.rest_5_
  27.8 0.0 copy-start.9
  27.8 0.0 collective-permute-done.7.rest_7_
  27.8 0.0 copy-start.10
  27.8 0.0 collective-permute-done.9.rest_9_
  27.8 0.0 copy-start.11
  27.8 0.0 collective-permute-done.11.rest_11_
  27.8 0.0 copy-start.12
  27.8 1.2 %collective-permute-done.13.rest_13_ = bf16[80,640]{1,0:T(8,128)(2,1)S(1)} collective-permute-done((bf16[80,640]{1,0:T(8,128)(2,1)S(1)}, bf16[80,640]{1,0:T(8,128)(2,1)S(1)}, u32[]{:S(2)}, u32[]{:S(2)}) %collective-permute-start.13) | collective-permute-done | bytes 102432 | tf_op jit(solution)/shard_map/ppermute | solution.py:191
  29.1 0.0 copy-start.13
  29.1 0.0 copy-done
  29.1 0.0 copy-done.1
  29.1 0.0 copy-done.2
  29.1 0.0 copy-done.3
  29.1 0.0 copy-done.4
  29.1 0.0 copy-done.5
  29.1 0.0 copy-done.6
  29.1 0.0 copy-done.7
  29.1 0.0 copy-done.8
  29.1 0.0 copy-done.9
  29.1 0.0 copy-done.10
  29.2 0.0 copy-done.11
  29.2 0.0 copy-done.12
  29.2 0.5 copy-done.13
  29.7 23.5 %attend.1 = bf16[128,4096]{1,0:T(8,128)(2,1)} custom-call(s32[8]{0:T(128)} %order_ref.3, bf16[128,6144]{1,0:T(8,128)(2,1)} %q_ref.1, bf16[4096,512]{1,0:T(8,128)(2,1)} %turn_key_weight.1.wkt_ref, bf16[512,4096]{1,0:T(8,128)(2,1)} %wv_ref.1, bf16[144,640]{1,0:T(8,128)(2,1)} %get-tuple-element.14.own_ref, bf16[80,640]{1,0:T(8,128)(2,1)} %copy-done, ...), custom_call_target="tpu_custom_call" | custom-call | flops 12079595520 | bytes 8388608 | tf_op jit(solution)/shard_map/attend/pallas_call | solution.py:152
Async XLA Ops:
  2.6 14.8 %collective-permute-start.3 = (bf16[80,640]{1,0:T(8,128)(2,1)}, bf16[80,640]{1,0:T(8,128)(2,1)S(1)}, u32[]{:S(2)}, u32[]{:S(2)}) collective-permute-start(bf16[80,640]{1,0:T(8,128)(2,1)} %get-tuple-element.12), channel_id=1, source_target_pairs={{0,2},{1,3},{2,0},{3,1},{4,6},{5,7},{6,4},{7,5},{8,10},{9,11},{10,... | collective-permute-start | bytes 307208 | tf_op jit(solution)/shard_map/ppermute | solution.py:191
  5.5 11.8 %collective-permute-start.2 = (bf16[80,640]{1,0:T(8,128)(2,1)}, bf16[80,640]{1,0:T(8,128)(2,1)S(1)}, u32[]{:S(2)}, u32[]{:S(2)}) collective-permute-start(bf16[80,640]{1,0:T(8,128)(2,1)} %get-tuple-element.12), channel_id=1, source_target_pairs={{0,12},{1,13},{2,14},{3,15},{4,0},{5,1},{6,2},{7,3},{8,4},{9,5},{1... | collective-permute-start | bytes 307208 | tf_op jit(solution)/shard_map/ppermute | solution.py:191
  9.1 8.9 %collective-permute-start.1 = (bf16[80,640]{1,0:T(8,128)(2,1)}, bf16[80,640]{1,0:T(8,128)(2,1)S(1)}, u32[]{:S(2)}, u32[]{:S(2)}) collective-permute-start(bf16[80,640]{1,0:T(8,128)(2,1)} %get-tuple-element.12), channel_id=1, source_target_pairs={{0,8},{1,9},{2,10},{3,11},{4,12},{5,13},{6,14},{7,15},{8,0},{9,1},... | collective-permute-start | bytes 307208 | tf_op jit(solution)/shard_map/ppermute | solution.py:191
  9.1 8.9 %collective-permute-start = (bf16[80,640]{1,0:T(8,128)(2,1)}, bf16[80,640]{1,0:T(8,128)(2,1)S(1)}, u32[]{:S(2)}, u32[]{:S(2)}) collective-permute-start(bf16[80,640]{1,0:T(8,128)(2,1)} %get-tuple-element.12), channel_id=1, source_target_pairs={{0,4},{1,5},{2,6},{3,7},{4,8},{5,9},{6,10},{7,11},{8,12},{9,13},{1... | collective-permute-start | bytes 307208 | tf_op jit(solution)/shard_map/ppermute | solution.py:191
  17.3 11.8 %copy-start = (bf16[80,640]{1,0:T(8,128)(2,1)}, bf16[80,640]{1,0:T(8,128)(2,1)S(1)}, u32[]{:S(2)}) copy-start(bf16[80,640]{1,0:T(8,128)(2,1)S(1)} %collective-permute-done.3.rest_0_) | copy-start | bytes 307204
  17.3 11.8 %copy-start.1 = (bf16[80,640]{1,0:T(8,128)(2,1)}, bf16[80,640]{1,0:T(8,128)(2,1)S(1)}, u32[]{:S(2)}) copy-start(bf16[80,640]{1,0:T(8,128)(2,1)S(1)} %collective-permute-done.2.rest_6_) | copy-start | bytes 307204
  18.0 11.1 %copy-start.2 = (bf16[80,640]{1,0:T(8,128)(2,1)}, bf16[80,640]{1,0:T(8,128)(2,1)S(1)}, u32[]{:S(2)}) copy-start(bf16[80,640]{1,0:T(8,128)(2,1)S(1)} %collective-permute-done.1.rest_4_) | copy-start | bytes 307204
  18.0 11.1 %copy-start.3 = (bf16[80,640]{1,0:T(8,128)(2,1)}, bf16[80,640]{1,0:T(8,128)(2,1)S(1)}, u32[]{:S(2)}) copy-start(bf16[80,640]{1,0:T(8,128)(2,1)S(1)} %collective-permute-done.rest_2_) | copy-start | bytes 307204
  18.0 2.8 %collective-permute-start.4 = (bf16[80,640]{1,0:T(8,128)(2,1)S(1)}, bf16[80,640]{1,0:T(8,128)(2,1)S(1)}, u32[]{:S(2)}, u32[]{:S(2)}) collective-permute-start(bf16[80,640]{1,0:T(8,128)(2,1)S(1)} %collective-permute-done.3.rest_0_), channel_id=1, source_target_pairs={{0,1},{1,0},{2,3},{3,2},{4,5},{5,4},{6,7},{7,6},{8,9},{9,8},{10,11... | collective-permute-start | bytes 307208 | tf_op jit(solution)/shard_map/ppermute | solution.py:191
  18.1 5.7 %collective-permute-start.8 = (bf16[80,640]{1,0:T(8,128)(2,1)S(1)}, bf16[80,640]{1,0:T(8,128)(2,1)S(1)}, u32[]{:S(2)}, u32[]{:S(2)}) collective-permute-start(bf16[80,640]{1,0:T(8,128)(2,1)S(1)} %collective-permute-done.rest_2_), channel_id=1, source_target_pairs={{0,2},{1,3},{2,0},{3,1},{4,6},{5,7},{6,4},{7,5},{8,10},{9,11},{10,... | collective-permute-start | bytes 307208 | tf_op jit(solution)/shard_map/ppermute | solution.py:191
  18.6 5.2 %collective-permute-start.5 = (bf16[80,640]{1,0:T(8,128)(2,1)S(1)}, bf16[80,640]{1,0:T(8,128)(2,1)S(1)}, u32[]{:S(2)}, u32[]{:S(2)}) collective-permute-start(bf16[80,640]{1,0:T(8,128)(2,1)S(1)} %collective-permute-done.rest_2_), channel_id=1, source_target_pairs={{0,1},{1,0},{2,3},{3,2},{4,5},{5,4},{6,7},{7,6},{8,9},{9,8},{10,11... | collective-permute-start | bytes 307208 | tf_op jit(solution)/shard_map/ppermute | solution.py:191
  18.8 7.2 %collective-permute-start.10 = (bf16[80,640]{1,0:T(8,128)(2,1)S(1)}, bf16[80,640]{1,0:T(8,128)(2,1)S(1)}, u32[]{:S(2)}, u32[]{:S(2)}) collective-permute-start(bf16[80,640]{1,0:T(8,128)(2,1)S(1)} %collective-permute-done.1.rest_4_), channel_id=1, source_target_pairs={{0,2},{1,3},{2,0},{3,1},{4,6},{5,7},{6,4},{7,5},{8,10},{9,11},{10,... | collective-permute-start | bytes 307208 | tf_op jit(solution)/shard_map/ppermute | solution.py:191
  20.3 7.4 %collective-permute-start.12 = (bf16[80,640]{1,0:T(8,128)(2,1)S(1)}, bf16[80,640]{1,0:T(8,128)(2,1)S(1)}, u32[]{:S(2)}, u32[]{:S(2)}) collective-permute-start(bf16[80,640]{1,0:T(8,128)(2,1)S(1)} %collective-permute-done.2.rest_6_), channel_id=1, source_target_pairs={{0,2},{1,3},{2,0},{3,1},{4,6},{5,7},{6,4},{7,5},{8,10},{9,11},{10,... | collective-permute-start | bytes 307208 | tf_op jit(solution)/shard_map/ppermute | solution.py:191
  20.8 8.3 %copy-start.4 = (bf16[80,640]{1,0:T(8,128)(2,1)}, bf16[80,640]{1,0:T(8,128)(2,1)S(1)}, u32[]{:S(2)}) copy-start(bf16[80,640]{1,0:T(8,128)(2,1)S(1)} %collective-permute-done.4.rest_1_) | copy-start | bytes 307204
  20.8 6.9 %collective-permute-start.6 = (bf16[80,640]{1,0:T(8,128)(2,1)S(1)}, bf16[80,640]{1,0:T(8,128)(2,1)S(1)}, u32[]{:S(2)}, u32[]{:S(2)}) collective-permute-start(bf16[80,640]{1,0:T(8,128)(2,1)S(1)} %collective-permute-done.1.rest_4_), channel_id=1, source_target_pairs={{0,1},{1,0},{2,3},{3,2},{4,5},{5,4},{6,7},{7,6},{8,9},{9,8},{10,11... | collective-permute-start | bytes 307208 | tf_op jit(solution)/shard_map/ppermute | solution.py:191
  23.8 5.3 %copy-start.5 = (bf16[80,640]{1,0:T(8,128)(2,1)}, bf16[80,640]{1,0:T(8,128)(2,1)S(1)}, u32[]{:S(2)}) copy-start(bf16[80,640]{1,0:T(8,128)(2,1)S(1)} %collective-permute-done.8.rest_8_) | copy-start | bytes 307204
  23.8 4.0 %collective-permute-start.7 = (bf16[80,640]{1,0:T(8,128)(2,1)S(1)}, bf16[80,640]{1,0:T(8,128)(2,1)S(1)}, u32[]{:S(2)}, u32[]{:S(2)}) collective-permute-start(bf16[80,640]{1,0:T(8,128)(2,1)S(1)} %collective-permute-done.2.rest_6_), channel_id=1, source_target_pairs={{0,1},{1,0},{2,3},{3,2},{4,5},{5,4},{6,7},{7,6},{8,9},{9,8},{10,11... | collective-permute-start | bytes 307208 | tf_op jit(solution)/shard_map/ppermute | solution.py:191
  23.8 5.3 %copy-start.6 = (bf16[80,640]{1,0:T(8,128)(2,1)}, bf16[80,640]{1,0:T(8,128)(2,1)S(1)}, u32[]{:S(2)}) copy-start(bf16[80,640]{1,0:T(8,128)(2,1)S(1)} %collective-permute-done.5.rest_3_) | copy-start | bytes 307204
  23.8 4.0 %collective-permute-start.9 = (bf16[80,640]{1,0:T(8,128)(2,1)S(1)}, bf16[80,640]{1,0:T(8,128)(2,1)S(1)}, u32[]{:S(2)}, u32[]{:S(2)}) collective-permute-start(bf16[80,640]{1,0:T(8,128)(2,1)S(1)} %collective-permute-done.8.rest_8_), channel_id=1, source_target_pairs={{0,1},{1,0},{2,3},{3,2},{4,5},{5,4},{6,7},{7,6},{8,9},{9,8},{10,11... | collective-permute-start | bytes 307208 | tf_op jit(solution)/shard_map/ppermute | solution.py:191
  26.0 3.1 %copy-start.7 = (bf16[80,640]{1,0:T(8,128)(2,1)}, bf16[80,640]{1,0:T(8,128)(2,1)S(1)}, u32[]{:S(2)}) copy-start(bf16[80,640]{1,0:T(8,128)(2,1)S(1)} %collective-permute-done.10.rest_10_) | copy-start | bytes 307204
  26.0 1.8 %collective-permute-start.11 = (bf16[80,640]{1,0:T(8,128)(2,1)S(1)}, bf16[80,640]{1,0:T(8,128)(2,1)S(1)}, u32[]{:S(2)}, u32[]{:S(2)}) collective-permute-start(bf16[80,640]{1,0:T(8,128)(2,1)S(1)} %collective-permute-done.10.rest_10_), channel_id=1, source_target_pairs={{0,1},{1,0},{2,3},{3,2},{4,5},{5,4},{6,7},{7,6},{8,9},{9,8},{10,11... | collective-permute-start | bytes 307208 | tf_op jit(solution)/shard_map/ppermute | solution.py:191
  27.8 1.4 %copy-start.8 = (bf16[80,640]{1,0:T(8,128)(2,1)}, bf16[80,640]{1,0:T(8,128)(2,1)S(1)}, u32[]{:S(2)}) copy-start(bf16[80,640]{1,0:T(8,128)(2,1)S(1)} %collective-permute-done.12.rest_12_) | copy-start | bytes 307204
  27.8 1.3 %collective-permute-start.13 = (bf16[80,640]{1,0:T(8,128)(2,1)S(1)}, bf16[80,640]{1,0:T(8,128)(2,1)S(1)}, u32[]{:S(2)}, u32[]{:S(2)}) collective-permute-start(bf16[80,640]{1,0:T(8,128)(2,1)S(1)} %collective-permute-done.12.rest_12_), channel_id=1, source_target_pairs={{0,1},{1,0},{2,3},{3,2},{4,5},{5,4},{6,7},{7,6},{8,9},{9,8},{10,11... | collective-permute-start | bytes 307208 | tf_op jit(solution)/shard_map/ppermute | solution.py:191
  27.8 1.4 %copy-start.9 = (bf16[80,640]{1,0:T(8,128)(2,1)}, bf16[80,640]{1,0:T(8,128)(2,1)S(1)}, u32[]{:S(2)}) copy-start(bf16[80,640]{1,0:T(8,128)(2,1)S(1)} %collective-permute-done.6.rest_5_) | copy-start | bytes 307204
  27.8 1.4 %copy-start.10 = (bf16[80,640]{1,0:T(8,128)(2,1)}, bf16[80,640]{1,0:T(8,128)(2,1)S(1)}, u32[]{:S(2)}) copy-start(bf16[80,640]{1,0:T(8,128)(2,1)S(1)} %collective-permute-done.7.rest_7_) | copy-start | bytes 307204
  27.8 1.4 %copy-start.11 = (bf16[80,640]{1,0:T(8,128)(2,1)}, bf16[80,640]{1,0:T(8,128)(2,1)S(1)}, u32[]{:S(2)}) copy-start(bf16[80,640]{1,0:T(8,128)(2,1)S(1)} %collective-permute-done.9.rest_9_) | copy-start | bytes 307204
  27.8 1.3 %copy-start.12 = (bf16[80,640]{1,0:T(8,128)(2,1)}, bf16[80,640]{1,0:T(8,128)(2,1)S(1)}, u32[]{:S(2)}) copy-start(bf16[80,640]{1,0:T(8,128)(2,1)S(1)} %collective-permute-done.11.rest_11_) | copy-start | bytes 307204
  29.1 0.6 %copy-start.13 = (bf16[80,640]{1,0:T(8,128)(2,1)}, bf16[80,640]{1,0:T(8,128)(2,1)S(1)}, u32[]{:S(2)}) copy-start(bf16[80,640]{1,0:T(8,128)(2,1)S(1)} %collective-permute-done.13.rest_13_) | copy-start | bytes 307204

commit v5 on v4

v5 whole, which is shorter than its diff:
```python
import functools
import math

import jax
import jax.numpy as jnp
from jax import lax
from jax.experimental import pallas as pl
from jax.experimental.pallas import tpu as pltpu
from jax.sharding import PartitionSpec as P

LATENT = 512
ROPE = 64
NOPE = 128
VDIM = 128
PACKED = 640
QK = 256
NEG = -1e30
AXES = ("ctx", "head")
BF = jnp.bfloat16
F32 = jnp.float32


def vmem_spec():
    return pl.BlockSpec(memory_space=pltpu.VMEM)


def smem_spec():
    return pl.BlockSpec(memory_space=pltpu.SMEM)


def pack_kernel(span_ref, cache_ref, gain_ref, out_ref):
    tok_rows = span_ref.shape[1]
    cache_rows = cache_ref.shape[0]
    latent = span_ref[:LATENT, :].astype(F32)
    mean_square = jnp.mean(latent * latent, axis=0, keepdims=True)
    normed = ((latent * lax.rsqrt(mean_square + 1e-06)).T * gain_ref[...]).astype(BF)
    tiles = LATENT // 128
    for tile in range(tiles):
        out_ref[tile * tok_rows : (tile + 1) * tok_rows, :] = normed[:, tile * 128 : (tile + 1) * 128]
    at = tiles * tok_rows
    out_ref[at : at + ROPE, :] = span_ref[LATENT:, :]
    at += ROPE
    for tile in range(tiles):
        out_ref[at : at + cache_rows, :] = cache_ref[:, tile * 128 : (tile + 1) * 128]
        at += cache_rows
    out_ref[at:, :] = jnp.zeros((cache_rows, 128), BF)
    out_ref[at:, :ROPE] = cache_ref[:, LATENT:]


def pack(span_latents, cache_latents, gain):
    tok_rows = span_latents.shape[0]
    cache_rows = cache_latents.shape[0]
    rows = (LATENT // 128) * (tok_rows + cache_rows) + ROPE + cache_rows
    return pl.pallas_call(
        pack_kernel,
        out_shape=jax.ShapeDtypeStruct((rows, 128), BF),
        in_specs=[vmem_spec(), vmem_spec(), vmem_spec()],
        out_specs=vmem_spec(),
        name="pack_rows",
    )(span_latents.T, cache_latents, gain.reshape(1, LATENT))


def origin(route, place, side, core, line):
    kind, step = route
    if kind == "own":
        return place * 2 + side
    if kind == "across":
        return place * 2 + 1 - side
    came = lax.rem(place + line - step, line)
    lane_side = lax.rem(side + core, 2) if kind == "along" else lax.rem(side + 1 - core, 2)
    return came * 2 + lane_side


def chunk_kernel(cfg, order_ref, prefix_ref, q_ref, wk_ref, wv_ref, *rest):
    first, last, routes, cached, heads, line, cache_rows = cfg
    held = 0 if first else 2
    prev = rest[:held]
    blocks = rest[held : held + len(routes)]
    tails = rest[held + len(routes) : held + len(routes) + len(cached)]
    rest = rest[held + len(routes) + len(cached) :]
    outs = 1 if last else (3 if first else 2)
    out_refs = rest[:outs]
    rows_ref, turned_ref, bias_ref = rest[outs:]
    tok_rows = q_ref.shape[0]
    tiles = LATENT // 128
    scale = math.log2(math.e) / math.sqrt(NOPE + ROPE)

    @pl.when(pl.program_id(0) == 0)
    def _():
        me = lax.axis_index("ctx")
        core = lax.axis_index("head")
        place = lax.div(me, 2)
        side = lax.rem(me, 2)
        for slot, route in enumerate(routes):
            to = slice(slot * tok_rows, (slot + 1) * tok_rows)
            for tile in range(tiles):
                part = blocks[slot][tile * tok_rows : (tile + 1) * tok_rows, :]
                rows_ref[to, tile * 128 : (tile + 1) * 128] = part
                turned_ref[tile * 128 : (tile + 1) * 128, to] = part.T
            turned_ref[LATENT:, to] = blocks[slot][tiles * tok_rows : tiles * tok_rows + ROPE, :]
            hidden = order_ref[origin(route, place, side, core, line)] > order_ref[me]
            bias_ref[:, to] = jnp.full((1, tok_rows), jnp.where(hidden, NEG, 0.0), F32)
        at = len(routes) * tok_rows
        lanes = lax.broadcasted_iota(jnp.int32, (1, max(1, len(cached)) * cache_rows), 1)
        slots = jnp.zeros_like(lanes)
        base = tiles * tok_rows + ROPE
        if cached:
            rotary = []
            for index, route in enumerate(cached):
                to = slice(at + index * cache_rows, at + (index + 1) * cache_rows)
                for tile in range(tiles):
                    begin = base + tile * cache_rows
                    rows_ref[to, tile * 128 : (tile + 1) * 128] = tails[index][begin : begin + cache_rows, :]
                rotary.append(tails[index][base + tiles * cache_rows :, :])
                inside = lanes - index * cache_rows
                source = origin(route, place, side, core, line) * cache_rows
                slots = jnp.where(jnp.logical_and(inside >= 0, inside < cache_rows), source + inside, slots)
            turned_ref[:LATENT, at:] = rows_ref[at:, :].T
            turned_ref[LATENT:, at:] = jnp.concatenate(rotary, axis=0).T[:ROPE, :]
            bias_ref[:, at:] = jnp.where(slots >= prefix_ref[0], NEG, 0.0)

    wk = wk_ref[...]
    if first:
        wk = wk.T
        out_refs[2][...] = wk
    keys = jnp.dot(wk, turned_ref[:LATENT, :], preferred_element_type=F32).astype(BF)
    rotary = turned_ref[LATENT:, :]
    nothing = jnp.zeros((QK - NOPE - ROPE, rotary.shape[1]), BF)
    bias = bias_ref[...]
    if first:
        row_ids = lax.broadcasted_iota(jnp.int32, (tok_rows, tok_rows), 0)
        col_ids = lax.broadcasted_iota(jnp.int32, (tok_rows, tok_rows), 1)
        causal = jnp.where(col_ids <= row_ids, 0.0, NEG)
    weights = []
    peaks = []
    sums = []
    for head in range(heads):
        nope = keys[head * NOPE : head * NOPE + NOPE]
        if head % 2 == 0:
            at = (head // 2) * 384
            full = jnp.concatenate([nope, rotary, nothing], axis=0)
        else:
            at = (head // 2) * 384 + 128
            full = jnp.concatenate([nothing, nope, rotary], axis=0)
        scores = jnp.dot(q_ref[:, at : at + QK], full, preferred_element_type=F32)
        if first:
            own = scores[:, :tok_rows] + causal
            scores = jnp.concatenate([own, scores[:, tok_rows:] + bias[:, tok_rows:]], axis=1)
        else:
            scores = scores + bias
        peak = jnp.max(scores, axis=1, keepdims=True)
        exponent = jnp.exp2((scores - peak) * scale)
        peaks.append(peak)
        sums.append(jnp.sum(exponent, axis=1, keepdims=True))
        weights.append(exponent.astype(BF))
    mixed = jnp.dot(jnp.concatenate(weights, axis=0), rows_ref[...], preferred_element_type=F32).astype(BF)
    lanes = lax.broadcasted_iota(jnp.int32, (tok_rows, 128), 1)
    state = jnp.zeros((tok_rows, 128), F32)
    for head in range(heads):
        here = slice(head * VDIM, (head + 1) * VDIM)
        out = jnp.dot(mixed[head * tok_rows : (head + 1) * tok_rows], wv_ref[:, here], preferred_element_type=F32)
        peak, total = peaks[head], sums[head]
        if not first:
            old_peak = prev[1][:, head : head + 1]
            old_total = prev[1][:, heads + head : heads + head + 1]
            top = jnp.maximum(old_peak, peak)
            keep = jnp.exp2((old_peak - top) * scale)
            add = jnp.exp2((peak - top) * scale)
            out = prev[0][:, here] * keep + out * add
            total = old_total * keep + total * add
            peak = top
        if last:
            out_refs[0][:, here] = (out / total).astype(BF)
        else:
            out_refs[0][:, here] = out
            state = jnp.where(lanes == head, peak, jnp.where(lanes == heads + head, total, state))
    if not last:
        out_refs[1][...] = state


def attend_chunk(first, last, scalars, queries, wk, wv, held, blocks, tails, line, cache_rows):
    tok_rows = queries.shape[0]
    all_heads = wv.shape[1] // VDIM
    routes = tuple(route for route, _ in blocks)
    cached = tuple(route for route, _ in tails)
    keys = len(routes) * tok_rows + len(cached) * cache_rows
    heads = 4
    if keys > 2048:
        heads = 2
    steps = all_heads // heads
    acc_spec = pl.BlockSpec((tok_rows, heads * VDIM), lambda i: (0, i))
    ml_spec = pl.BlockSpec((tok_rows, 128), lambda i: (0, i))
    across_spec = pl.BlockSpec((LATENT, heads * NOPE), lambda i: (0, i))
    down_spec = pl.BlockSpec((heads * NOPE, LATENT), lambda i: (i, 0))
    if last:
        out_shape = [jax.ShapeDtypeStruct((tok_rows, all_heads * VDIM), BF)]
        out_specs = [acc_spec]
    else:
        out_shape = [
            jax.ShapeDtypeStruct((tok_rows, all_heads * VDIM), F32),
            jax.ShapeDtypeStruct((tok_rows, steps * 128), F32),
        ]
        out_specs = [acc_spec, ml_spec]
        if first:
            out_shape.append(jax.ShapeDtypeStruct((all_heads * NOPE, LATENT), BF))
            out_specs.append(down_spec)
    return pl.pallas_call(
        functools.partial(chunk_kernel, (first, last, routes, cached, heads, line, cache_rows)),
        out_shape=out_shape,
        grid=(steps,),
        in_specs=[
            smem_spec(),
            smem_spec(),
            pl.BlockSpec((tok_rows, heads * (NOPE + ROPE)), lambda i: (0, i)),
            across_spec if first else down_spec,
            across_spec,
        ]
        + [acc_spec, ml_spec][: len(held)]
        + [vmem_spec()] * (len(blocks) + len(tails)),
        out_specs=out_specs,
        scratch_shapes=[
            pltpu.VMEM((keys, LATENT), BF),
            pltpu.VMEM((LATENT + ROPE, keys), BF),
            pltpu.VMEM((1, keys), F32),
        ],
        compiler_params=pltpu.CompilerParams(vmem_limit_bytes=54 * 1024 * 1024),
        cost_estimate=pl.CostEstimate(
            flops=2 * keys * all_heads * (LATENT * NOPE + tok_rows * (QK + LATENT)),
            bytes_accessed=LATENT * all_heads * 512,
            transcendentals=keys * tok_rows * all_heads,
        ),
        name="attend_first" if first else "attend_last" if last else "attend_next",
    )(*scalars, queries, wk, wv, *held, *[x for _, x in blocks], *[x for _, x in tails])


def mover(line):
    def move(value, route):
        pairs = []
        for place in range(line):
            for side in range(2):
                for core in range(2):
                    to_place, to_side, to_core = route(place, side, core)
                    source = (place * 2 + side) * 2 + core
                    target = ((to_place % line) * 2 + to_side) * 2 + to_core
                    pairs.append((source, target))
        return lax.ppermute(value, AXES, pairs)

    return move


def per_device(
    queries,
    span_latents,
    cache_latents,
    latent_gain,
    key_weight,
    value_weight,
    prefix_length,
    block_order,
):
    line = lax.axis_size("ctx") // 2
    cache_rows = cache_latents.shape[0]
    move = mover(line)
    own = pack(span_latents, cache_latents, latent_gain)
    across = move(own, lambda p, s, c: (p, 1 - s, c))
    along = [move(own, lambda p, s, c, k=k: (p + k, s ^ c, c)) for k in range(1, line)]
    near = [(("own", 0), own), (("across", 0), across)]
    chunk = functools.partial(attend_chunk, line=line, cache_rows=cache_rows)
    scalars = (block_order, prefix_length)
    acc, state, turned = chunk(True, False, scalars, queries, key_weight, value_weight, (), near, [])
    along, acc, state, turned = lax.optimization_barrier((along, acc, state, turned))
    swapped = [move(a, lambda p, s, c: (p, s, 1 - c)) for a in along]
    far = [(("along", k + 1), a) for k, a in enumerate(along)]
    far += [(("swapped", k + 1), w) for k, w in enumerate(swapped)]
    return chunk(False, True, scalars, queries, turned, value_weight, (acc, state), far, near + far)[0]


def solution(mesh):
    return jax.shard_map(
        per_device,
        mesh=mesh,
        in_specs=(
            P(("groups", "ctx"), "head"),
            P(("groups", "ctx"), None),
            P(("groups", "ctx"), None),
            P(),
            P(None, "head"),
            P(None, "head"),
            P("groups"),
            P("groups"),
        ),
        out_specs=P(("groups", "ctx"), "head"),
        check_vma=False,
    )
```

time: 53.5 us -> 49.8 us (0.931)
  the two profiles are of different devices: /device:TPU:0 before, /device:TPU:13 now
where the time goes in v5:
time: 49.8 us; the launch traced here: 49.4 us
  Pallas kernels  36.1 us (72%)
  starting transfers between devices  9.72 us (20%)
  local copies, waits for them, and re-layouts  1.81 us (4%)
  waiting for transfers between devices  1.14 us (2%)
  between operations  0.73 us (1%)
    pallas_call x2, Pallas kernels, attend_chunk(): pl.pallas_call(functools.partial(chunk_kernel, (first, last, routes, cach...  34.2 us
    ppermute x7, starting transfers between devices, move(): return lax.ppermute(value, AXES, pairs)  9.72 us
    pallas_call x1, Pallas kernels, pack(): pl.pallas_call(pack_kernel, out_shape=jax.ShapeDtypeStruct((rows, 128), B...  1.81 us
    unnamed x14, local copies, waits for them, and re-layouts  1.81 us
    ppermute x7, waiting for transfers between devices, move(): return lax.ppermute(value, AXES, pairs)  1.14 us
  transfers between devices with their start and end apart: 7, of which 3 were waited for; matrix products, arithmetic and copies ran while one was open for 0% of the time, Pallas kernels for 25%

profile of v5, /device:TPU:13, one launch (start us, length us, event | category | flops | bytes accessed | tf_op | source)
XLA Modules:
  0.0 49.4 jit_solution(5721438123891581006)
XLA Ops:
  0.0 1.8 %pack_rows.1.rest_0_.rest_8_ = bf16[656,128]{1,0:T(8,128)(2,1)} custom-call(bf16[576,128]{1,0:T(8,128)(2,1)} %bitcast.2, bf16[16,576]{1,0:T(8,128)(2,1)} %cache_ref.1, f32[1,512]{1,0:T(1,128)} %bitcast.3), custom_call_target="tpu_custom_call" | custom-call | tf_op jit(solution)/shard_map/pack_rows/pallas_call | solution.py:54
  1.8 0.2 collective-permute-start.3
  2.0 1.1 %collective-permute-start.2 = (bf16[656,128]{1,0:T(8,128)(2,1)}, bf16[656,128]{1,0:T(8,128)(2,1)S(1)}, u32[]{:S(2)}, u32[]{:S(2)}) collective-permute-start(bf16[656,128]{1,0:T(8,128)(2,1)} %pack_rows.1.rest_0_.rest_8_), channel_id=1, source_target_pairs={{0,12},{1,15},{2,14},{3,13},{4,0},{5,3},{6,2},{7,1},{8,4},{9,7},{1... | collective-permute-start | bytes 503816 | tf_op jit(solution)/shard_map/ppermute | solution.py:246
  3.2 2.3 %collective-permute-start.1 = (bf16[656,128]{1,0:T(8,128)(2,1)}, bf16[656,128]{1,0:T(8,128)(2,1)S(1)}, u32[]{:S(2)}, u32[]{:S(2)}) collective-permute-start(bf16[656,128]{1,0:T(8,128)(2,1)} %pack_rows.1.rest_0_.rest_8_), channel_id=1, source_target_pairs={{0,8},{1,11},{2,10},{3,9},{4,12},{5,15},{6,14},{7,13},{8,0},{9,3},... | collective-permute-start | bytes 503816 | tf_op jit(solution)/shard_map/ppermute | solution.py:246
  5.4 3.2 %collective-permute-start = (bf16[656,128]{1,0:T(8,128)(2,1)}, bf16[656,128]{1,0:T(8,128)(2,1)S(1)}, u32[]{:S(2)}, u32[]{:S(2)}) collective-permute-start(bf16[656,128]{1,0:T(8,128)(2,1)} %pack_rows.1.rest_0_.rest_8_), channel_id=1, source_target_pairs={{0,4},{1,7},{2,6},{3,5},{4,8},{5,11},{6,10},{7,9},{8,12},{9,15},{1... | collective-permute-start | bytes 503816 | tf_op jit(solution)/shard_map/ppermute | solution.py:246
  9.2 0.0 collective-permute-done.3.rest_1_.rest_9_
  9.2 0.0 copy-start
  9.2 0.7 %copy-done = bf16[656,128]{1,0:T(8,128)(2,1)} copy-done((bf16[656,128]{1,0:T(8,128)(2,1)}, bf16[656,128]{1,0:T(8,128)(2,1)S(1)}, u32[]{:S(2)}) %copy-start) | copy-done | bytes 167960
  9.9 12.2 %attend_first.1 = (f32[128,4096]{1,0:T(8,128)}, f32[128,1024]{1,0:T(8,128)}, bf16[4096,512]{1,0:T(8,128)(2,1)}) custom-call(s32[8]{0:T(128)} %order_ref.3, s32[1]{0:T(128)S(6)} %copy.9.prefix_ref, bf16[128,6144]{1,0:T(8,128)(2,1)} %q_ref.3, bf16[512,4096]{1,0:T(8,128)(2,1)} %wk_ref.1, bf16[512,4096]{1,0:T(8,128)(2,1)} %wv_ref.3, ...), custom_call_target="tpu_custom_call" | custom-call | flops 2684354560 | bytes 8388608 | tf_op jit(solution)/shard_map/attend_first/pallas_call | solution.py:207
  22.2 0.0 collective-permute-done.2.rest_4_.rest_12_
  22.2 0.0 copy-start.1
  22.2 0.0 collective-permute-done.1.rest_3_.rest_11_
  22.2 0.0 copy-start.2
  22.2 0.0 collective-permute-done.rest_2_.rest_10_
  22.2 0.0 copy-start.3
  22.2 2.5 %collective-permute-start.4 = (bf16[656,128]{1,0:T(8,128)(2,1)S(1)}, bf16[656,128]{1,0:T(8,128)(2,1)S(1)}, u32[]{:S(2)}, u32[]{:S(2)}) collective-permute-start(bf16[656,128]{1,0:T(8,128)(2,1)S(1)} %collective-permute-done.rest_2_.rest_10_), channel_id=1, source_target_pairs={{0,1},{1,0},{2,3},{3,2},{4,5},{5,4},{6,7},{7,6},{8,9},{9,8},{10,11... | collective-permute-start | bytes 503816 | tf_op jit(solution)/shard_map/ppermute | solution.py:246
  24.7 0.1 collective-permute-start.5
  24.8 0.4 collective-permute-start.6
  25.2 0.5 %collective-permute-done.4.rest_5_.rest_13_ = bf16[656,128]{1,0:T(8,128)(2,1)S(1)} collective-permute-done((bf16[656,128]{1,0:T(8,128)(2,1)S(1)}, bf16[656,128]{1,0:T(8,128)(2,1)S(1)}, u32[]{:S(2)}, u32[]{:S(2)}) %collective-permute-start.4) | collective-permute-done | bytes 167968 | tf_op jit(solution)/shard_map/ppermute | solution.py:246
  25.7 0.0 copy-start.4
  25.7 0.4 collective-permute-done.5.rest_6_.rest_14_
  26.1 0.0 copy-start.5
  26.1 0.2 collective-permute-done.6.rest_7_.rest_15_
  26.3 0.0 copy-done.1
  26.3 0.0 copy-done.2
  26.3 0.0 copy-done.3
  26.3 0.0 copy-done.4
  26.4 0.4 copy-done.5
  26.7 0.0 copy-start.6
  26.7 0.7 %copy-done.6 = bf16[656,128]{1,0:T(8,128)(2,1)} copy-done((bf16[656,128]{1,0:T(8,128)(2,1)}, bf16[656,128]{1,0:T(8,128)(2,1)S(1)}, u32[]{:S(2)}) %copy-start.6) | copy-done | bytes 167960
  27.4 22.0 %attend_last.1 = bf16[128,4096]{1,0:T(8,128)(2,1)} custom-call(s32[8]{0:T(128)} %order_ref.3, s32[1]{0:T(128)S(6)} %copy.9.prefix_ref, bf16[128,6144]{1,0:T(8,128)(2,1)} %q_ref.3, bf16[4096,512]{1,0:T(8,128)(2,1)} %get-tuple-element.17.wk_ref, bf16[512,4096]{1,0:T(8,128)(2,1)} %wv_ref.3, f32[128,4096]{1,0:T(8,128)} %get-tuple-element.18.rest_0_, ...), custom_call_target="tpu_custom_call" | custom-call | flops 9395240960 | bytes 8388608 | tf_op jit(solution)/shard_map/attend_last/pallas_call | solution.py:207
Async XLA Ops:
  1.8 7.4 %collective-permute-start.3 = (bf16[656,128]{1,0:T(8,128)(2,1)}, bf16[656,128]{1,0:T(8,128)(2,1)S(1)}, u32[]{:S(2)}, u32[]{:S(2)}) collective-permute-start(bf16[656,128]{1,0:T(8,128)(2,1)} %pack_rows.1.rest_0_.rest_8_), channel_id=1, source_target_pairs={{0,2},{1,3},{2,0},{3,1},{4,6},{5,7},{6,4},{7,5},{8,10},{9,11},{10,... | collective-permute-start | bytes 503816 | tf_op jit(solution)/shard_map/ppermute | solution.py:246
  2.0 20.1 %collective-permute-start.2 = (bf16[656,128]{1,0:T(8,128)(2,1)}, bf16[656,128]{1,0:T(8,128)(2,1)S(1)}, u32[]{:S(2)}, u32[]{:S(2)}) collective-permute-start(bf16[656,128]{1,0:T(8,128)(2,1)} %pack_rows.1.rest_0_.rest_8_), channel_id=1, source_target_pairs={{0,12},{1,15},{2,14},{3,13},{4,0},{5,3},{6,2},{7,1},{8,4},{9,7},{1... | collective-permute-start | bytes 503816 | tf_op jit(solution)/shard_map/ppermute | solution.py:246
  3.2 19.0 %collective-permute-start.1 = (bf16[656,128]{1,0:T(8,128)(2,1)}, bf16[656,128]{1,0:T(8,128)(2,1)S(1)}, u32[]{:S(2)}, u32[]{:S(2)}) collective-permute-start(bf16[656,128]{1,0:T(8,128)(2,1)} %pack_rows.1.rest_0_.rest_8_), channel_id=1, source_target_pairs={{0,8},{1,11},{2,10},{3,9},{4,12},{5,15},{6,14},{7,13},{8,0},{9,3},... | collective-permute-start | bytes 503816 | tf_op jit(solution)/shard_map/ppermute | solution.py:246
  5.4 16.8 %collective-permute-start = (bf16[656,128]{1,0:T(8,128)(2,1)}, bf16[656,128]{1,0:T(8,128)(2,1)S(1)}, u32[]{:S(2)}, u32[]{:S(2)}) collective-permute-start(bf16[656,128]{1,0:T(8,128)(2,1)} %pack_rows.1.rest_0_.rest_8_), channel_id=1, source_target_pairs={{0,4},{1,7},{2,6},{3,5},{4,8},{5,11},{6,10},{7,9},{8,12},{9,15},{1... | collective-permute-start | bytes 503816 | tf_op jit(solution)/shard_map/ppermute | solution.py:246
  9.2 0.7 %copy-start = (bf16[656,128]{1,0:T(8,128)(2,1)}, bf16[656,128]{1,0:T(8,128)(2,1)S(1)}, u32[]{:S(2)}) copy-start(bf16[656,128]{1,0:T(8,128)(2,1)S(1)} %collective-permute-done.3.rest_1_.rest_9_) | copy-start | bytes 503812
  22.2 4.2 %copy-start.1 = (bf16[656,128]{1,0:T(8,128)(2,1)}, bf16[656,128]{1,0:T(8,128)(2,1)S(1)}, u32[]{:S(2)}) copy-start(bf16[656,128]{1,0:T(8,128)(2,1)S(1)} %collective-permute-done.2.rest_4_.rest_12_) | copy-start | bytes 503812
  22.2 4.1 %copy-start.2 = (bf16[656,128]{1,0:T(8,128)(2,1)}, bf16[656,128]{1,0:T(8,128)(2,1)S(1)}, u32[]{:S(2)}) copy-start(bf16[656,128]{1,0:T(8,128)(2,1)S(1)} %collective-permute-done.1.rest_3_.rest_11_) | copy-start | bytes 503812
  22.2 4.1 %copy-start.3 = (bf16[656,128]{1,0:T(8,128)(2,1)}, bf16[656,128]{1,0:T(8,128)(2,1)S(1)}, u32[]{:S(2)}) copy-start(bf16[656,128]{1,0:T(8,128)(2,1)S(1)} %collective-permute-done.rest_2_.rest_10_) | copy-start | bytes 503812
  22.2 3.5 %collective-permute-start.4 = (bf16[656,128]{1,0:T(8,128)(2,1)S(1)}, bf16[656,128]{1,0:T(8,128)(2,1)S(1)}, u32[]{:S(2)}, u32[]{:S(2)}) collective-permute-start(bf16[656,128]{1,0:T(8,128)(2,1)S(1)} %collective-permute-done.rest_2_.rest_10_), channel_id=1, source_target_pairs={{0,1},{1,0},{2,3},{3,2},{4,5},{5,4},{6,7},{7,6},{8,9},{9,8},{10,11... | collective-permute-start | bytes 503816 | tf_op jit(solution)/shard_map/ppermute | solution.py:246
  24.7 1.4 %collective-permute-start.5 = (bf16[656,128]{1,0:T(8,128)(2,1)S(1)}, bf16[656,128]{1,0:T(8,128)(2,1)S(1)}, u32[]{:S(2)}, u32[]{:S(2)}) collective-permute-start(bf16[656,128]{1,0:T(8,128)(2,1)S(1)} %collective-permute-done.1.rest_3_.rest_11_), channel_id=1, source_target_pairs={{0,1},{1,0},{2,3},{3,2},{4,5},{5,4},{6,7},{7,6},{8,9},{9,8},{10,11... | collective-permute-start | bytes 503816 | tf_op jit(solution)/shard_map/ppermute | solution.py:246
  24.8 1.6 %collective-permute-start.6 = (bf16[656,128]{1,0:T(8,128)(2,1)S(1)}, bf16[656,128]{1,0:T(8,128)(2,1)S(1)}, u32[]{:S(2)}, u32[]{:S(2)}) collective-permute-start(bf16[656,128]{1,0:T(8,128)(2,1)S(1)} %collective-permute-done.2.rest_4_.rest_12_), channel_id=1, source_target_pairs={{0,1},{1,0},{2,3},{3,2},{4,5},{5,4},{6,7},{7,6},{8,9},{9,8},{10,11... | collective-permute-start | bytes 503816 | tf_op jit(solution)/shard_map/ppermute | solution.py:246
  25.7 0.7 %copy-start.4 = (bf16[656,128]{1,0:T(8,128)(2,1)}, bf16[656,128]{1,0:T(8,128)(2,1)S(1)}, u32[]{:S(2)}) copy-start(bf16[656,128]{1,0:T(8,128)(2,1)S(1)} %collective-permute-done.4.rest_5_.rest_13_) | copy-start | bytes 503812
  26.1 0.7 %copy-start.5 = (bf16[656,128]{1,0:T(8,128)(2,1)}, bf16[656,128]{1,0:T(8,128)(2,1)S(1)}, u32[]{:S(2)}) copy-start(bf16[656,128]{1,0:T(8,128)(2,1)S(1)} %collective-permute-done.5.rest_6_.rest_14_) | copy-start | bytes 503812
  26.7 0.7 %copy-start.6 = (bf16[656,128]{1,0:T(8,128)(2,1)}, bf16[656,128]{1,0:T(8,128)(2,1)S(1)}, u32[]{:S(2)}) copy-start(bf16[656,128]{1,0:T(8,128)(2,1)S(1)} %collective-permute-done.6.rest_7_.rest_15_) | copy-start | bytes 503812

commit v6 on v5

v6 whole, which is shorter than its diff:
```python
import functools
import math

import jax
import jax.numpy as jnp
from jax import lax
from jax.experimental import pallas as pl
from jax.experimental.pallas import tpu as pltpu
from jax.sharding import PartitionSpec as P

LATENT = 512
ROPE = 64
NOPE = 128
VDIM = 128
PACKED = 640
QK = 256
NEG = -1e30
AXES = ("ctx", "head")
BF = jnp.bfloat16
F32 = jnp.float32


def vmem_spec():
    return pl.BlockSpec(memory_space=pltpu.VMEM)


def smem_spec():
    return pl.BlockSpec(memory_space=pltpu.SMEM)


def any_spec():
    return pl.BlockSpec(memory_space=pl.ANY)


def pack_kernel(span_ref, cache_ref, gain_ref, out_ref):
    tok_rows = span_ref.shape[1]
    cache_rows = cache_ref.shape[0]
    latent = span_ref[:LATENT, :].astype(F32)
    mean_square = jnp.mean(latent * latent, axis=0, keepdims=True)
    normed = ((latent * lax.rsqrt(mean_square + 1e-06)).T * gain_ref[...]).astype(BF)
    tiles = LATENT // 128
    for tile in range(tiles):
        out_ref[tile * tok_rows : (tile + 1) * tok_rows, :] = normed[:, tile * 128 : (tile + 1) * 128]
    at = tiles * tok_rows
    out_ref[at : at + ROPE, :] = span_ref[LATENT:, :]
    at += ROPE
    for tile in range(tiles):
        out_ref[at : at + cache_rows, :] = cache_ref[:, tile * 128 : (tile + 1) * 128]
        at += cache_rows
    out_ref[at:, :] = jnp.zeros((cache_rows, 128), BF)
    out_ref[at:, :ROPE] = cache_ref[:, LATENT:]


def pack(span_latents, cache_latents, gain):
    tok_rows = span_latents.shape[0]
    cache_rows = cache_latents.shape[0]
    rows = (LATENT // 128) * (tok_rows + cache_rows) + ROPE + cache_rows
    return pl.pallas_call(
        pack_kernel,
        out_shape=jax.ShapeDtypeStruct((rows, 128), BF),
        in_specs=[vmem_spec(), vmem_spec(), vmem_spec()],
        out_specs=vmem_spec(),
        name="pack_rows",
    )(span_latents.T, cache_latents, gain.reshape(1, LATENT))


def origin(route, place, side, core, line):
    kind, step = route
    if kind == "own":
        return place * 2 + side
    if kind == "across":
        return place * 2 + 1 - side
    came = lax.rem(place + line - step, line)
    lane_side = lax.rem(side + core, 2) if kind == "along" else lax.rem(side + 1 - core, 2)
    return came * 2 + lane_side


def turn_kernel(wk_ref, *rest):
    rest[-1][...] = wk_ref[...].T


def turn(key_weight, part, before):
    depth, width = key_weight.shape
    steps = 4
    block = width // (2 * steps)
    return pl.pallas_call(
        turn_kernel,
        out_shape=jax.ShapeDtypeStruct((width, depth), BF),
        grid=(steps,),
        in_specs=[pl.BlockSpec((depth, block), lambda i: (0, i + part * steps))] + [any_spec()] * len(before),
        out_specs=pl.BlockSpec((block, depth), lambda i: (i + part * steps, 0)),
        input_output_aliases={1: 0} if before else {},
        cost_estimate=pl.CostEstimate(flops=0, bytes_accessed=1024, transcendentals=0),
        name="turn_key_weight",
    )(key_weight, *before)


def gather_rows(cfg, order_ref, prefix_ref, blocks, tails, rows_ref, turned_ref, bias_ref):
    routes, cached, line, cache_rows, tok_rows = cfg
    tiles = LATENT // 128
    me = lax.axis_index("ctx")
    core = lax.axis_index("head")
    place = lax.div(me, 2)
    side = lax.rem(me, 2)
    for slot, route in enumerate(routes):
        to = slice(slot * tok_rows, (slot + 1) * tok_rows)
        for tile in range(tiles):
            part = blocks[slot][tile * tok_rows : (tile + 1) * tok_rows, :]
            rows_ref[to, tile * 128 : (tile + 1) * 128] = part
            turned_ref[tile * 128 : (tile + 1) * 128, to] = part.T
        turned_ref[LATENT:, to] = blocks[slot][tiles * tok_rows : tiles * tok_rows + ROPE, :]
        hidden = order_ref[origin(route, place, side, core, line)] > order_ref[me]
        bias_ref[:, to] = jnp.full((1, tok_rows), jnp.where(hidden, NEG, 0.0), F32)
    if not cached:
        return
    at = len(routes) * tok_rows
    lanes = lax.broadcasted_iota(jnp.int32, (1, len(cached) * cache_rows), 1)
    slots = jnp.zeros_like(lanes)
    base = tiles * tok_rows + ROPE
    rotary = []
    for index, route in enumerate(cached):
        to = slice(at + index * cache_rows, at + (index + 1) * cache_rows)
        for tile in range(tiles):
            begin = base + tile * cache_rows
            rows_ref[to, tile * 128 : (tile + 1) * 128] = tails[index][begin : begin + cache_rows, :]
        rotary.append(tails[index][base + tiles * cache_rows :, :])
        inside = lanes - index * cache_rows
        source = origin(route, place, side, core, line) * cache_rows
        slots = jnp.where(jnp.logical_and(inside >= 0, inside < cache_rows), source + inside, slots)
    turned_ref[:LATENT, at:] = rows_ref[at:, :].T
    turned_ref[LATENT:, at:] = jnp.concatenate(rotary, axis=0).T[:ROPE, :]
    bias_ref[:, at:] = jnp.where(slots >= prefix_ref[0], NEG, 0.0)


def chunk_kernel(cfg, last, steps, order_ref, prefix_ref, q_old_ref, q_new_ref, wk_ref, wv_ref, *rest):
    routes, cached = cfg[:2]
    tok_rows = cfg[4]
    if last:
        acc_ref, state_old_ref, state_new_ref = rest[:3]
        rest = rest[3:]
    blocks = rest[: len(routes)]
    tails = rest[len(routes) : len(routes) + len(cached)]
    rest = rest[len(routes) + len(cached) :]
    outs = 1 if last else 2
    out_refs = rest[:outs]
    rows_ref, turned_ref, bias_ref = rest[outs : outs + 3]
    key_refs = rest[outs + 3 : outs + 5]
    weight_refs = rest[outs + 5 : outs + 7]
    stat_refs = rest[outs + 7 : outs + 9]
    scale = math.log2(math.e) / math.sqrt(NOPE + ROPE)
    step = pl.program_id(0)

    def make_keys(buffer):
        wk = wk_ref[buffer * 256 : buffer * 256 + 256, :]
        key_refs[buffer][...] = jnp.dot(wk, turned_ref[:LATENT, :], preferred_element_type=F32).astype(BF)

    def make_scores(buffer, q_ref):
        rotary = turned_ref[LATENT:, :]
        nothing = jnp.zeros((QK - NOPE - ROPE, rotary.shape[1]), BF)
        result = []
        for head in range(2):
            nope = key_refs[buffer][head * NOPE : head * NOPE + NOPE, :]
            parts = [nope, rotary, nothing] if head == 0 else [nothing, nope, rotary]
            full = jnp.concatenate(parts, axis=0)
            query = q_ref[:, head * 128 : head * 128 + QK]
            result.append(jnp.dot(query, full, preferred_element_type=F32))
        return result

    def make_weights(buffer, both, state_ref):
        bias = bias_ref[...]
        for head in range(2):
            scores = both[head]
            if last:
                scores = scores + bias
            else:
                row_ids = lax.broadcasted_iota(jnp.int32, (tok_rows, tok_rows), 0)
                col_ids = lax.broadcasted_iota(jnp.int32, (tok_rows, tok_rows), 1)
                causal = jnp.where(col_ids <= row_ids, 0.0, NEG)
                own = scores[:, :tok_rows] + causal
                scores = jnp.concatenate([own, scores[:, tok_rows:] + bias[:, tok_rows:]], axis=1)
            peak = jnp.max(scores, axis=1, keepdims=True)
            if last:
                old_peak = state_ref[:, 2 * head : 2 * head + 1]
                peak = jnp.maximum(peak, old_peak)
                keep = jnp.exp2((old_peak - peak) * scale)
            exponent = jnp.exp2((scores - peak) * scale)
            total = jnp.sum(exponent, axis=1, keepdims=True)
            if last:
                total = total + state_ref[:, 2 * head + 1 : 2 * head + 2] * keep
                stat_refs[buffer][:, 2 * head : 2 * head + 1] = keep
            else:
                stat_refs[buffer][:, 2 * head : 2 * head + 1] = peak
            stat_refs[buffer][:, 2 * head + 1 : 2 * head + 2] = total
            weight_refs[buffer][head * tok_rows : (head + 1) * tok_rows, :] = exponent.astype(BF)

    def make_outputs(buffer):
        mixed = jnp.dot(weight_refs[buffer][...], rows_ref[...], preferred_element_type=F32).astype(BF)
        for head in range(2):
            here = slice((buffer * 2 + head) * VDIM, (buffer * 2 + head + 1) * VDIM)
            out = jnp.dot(mixed[head * tok_rows : (head + 1) * tok_rows], wv_ref[:, here], preferred_element_type=F32)
            if last:
                out = out + acc_ref[:, here] * stat_refs[buffer][:, 2 * head : 2 * head + 1]
                total = stat_refs[buffer][:, 2 * head + 1 : 2 * head + 2]
                out_refs[0][:, here] = (out / total).astype(BF)
            else:
                out_refs[0][:, here] = out
        if not last:
            out_refs[1][:, buffer * 128 : buffer * 128 + 128] = stat_refs[buffer][...]

    states = (state_old_ref, state_new_ref) if last else (None, None)

    @pl.when(step == 0)
    def _():
        gather_rows(cfg, order_ref, prefix_ref, blocks, tails, rows_ref, turned_ref, bias_ref)
        for ref in stat_refs:
            ref[...] = jnp.zeros_like(ref)
        make_keys(0)
        scores = make_scores(0, q_new_ref)
        make_keys(1)
        make_weights(0, scores, states[1])

    @pl.when(jnp.logical_and(step > 0, step < steps))
    def _():
        scores = make_scores(1, q_old_ref)
        make_keys(0)
        make_outputs(0)
        make_weights(1, scores, states[0])
        scores = make_scores(0, q_new_ref)
        make_keys(1)
        make_outputs(1)
        make_weights(0, scores, states[1])

    @pl.when(step == steps)
    def _():
        scores = make_scores(1, q_old_ref)
        make_outputs(0)
        make_weights(1, scores, states[0])
        make_outputs(1)


def attend_chunk(last, scalars, queries, wkt, wv, held, blocks, tails, line, cache_rows):
    tok_rows = queries.shape[0]
    all_heads = wv.shape[1] // VDIM
    routes = tuple(route for route, _ in blocks)
    cached = tuple(route for route, _ in tails)
    keys = len(routes) * tok_rows + len(cached) * cache_rows
    steps = all_heads // 4
    pairs = all_heads // 2
    pair_width = 2 * (NOPE + ROPE)

    def behind(i):
        return jnp.maximum(i - 1, 0)

    def ahead(i):
        return jnp.minimum(i, steps - 1)

    def old_pair(i):
        return jnp.maximum(2 * i - 1, 0)

    def new_pair(i):
        return jnp.minimum(2 * i, pairs - 1)

    out_spec = pl.BlockSpec((tok_rows, 4 * VDIM), lambda i: (0, behind(i)))
    in_specs = [
        smem_spec(),
        smem_spec(),
        pl.BlockSpec((tok_rows, pair_width), lambda i: (0, old_pair(i))),
        pl.BlockSpec((tok_rows, pair_width), lambda i: (0, new_pair(i))),
        pl.BlockSpec((4 * NOPE, LATENT), lambda i: (ahead(i), 0)),
        pl.BlockSpec((LATENT, 4 * VDIM), lambda i: (0, behind(i))),
    ]
    if last:
        out_shape = [jax.ShapeDtypeStruct((tok_rows, all_heads * VDIM), BF)]
        out_specs = [out_spec]
        in_specs += [
            out_spec,
            pl.BlockSpec((tok_rows, 128), lambda i: (0, old_pair(i))),
            pl.BlockSpec((tok_rows, 128), lambda i: (0, new_pair(i))),
        ]
        held = (held[0], held[1], held[1])
    else:
        out_shape = [
            jax.ShapeDtypeStruct((tok_rows, all_heads * VDIM), F32),
            jax.ShapeDtypeStruct((tok_rows, pairs * 128), F32),
        ]
        out_specs = [out_spec, pl.BlockSpec((tok_rows, 256), lambda i: (0, behind(i)))]
    cfg = (routes, cached, line, cache_rows, tok_rows)
    return pl.pallas_call(
        functools.partial(chunk_kernel, cfg, last, steps),
        out_shape=out_shape,
        grid=(steps + 1,),
        in_specs=in_specs + [vmem_spec()] * (len(blocks) + len(tails)),
        out_specs=out_specs,
        scratch_shapes=[
            pltpu.VMEM((keys, LATENT), BF),
            pltpu.VMEM((LATENT + ROPE, keys), BF),
            pltpu.VMEM((1, keys), F32),
            pltpu.VMEM((2 * NOPE, keys), BF),
            pltpu.VMEM((2 * NOPE, keys), BF),
            pltpu.VMEM((2 * tok_rows, keys), BF),
            pltpu.VMEM((2 * tok_rows, keys), BF),
            pltpu.VMEM((tok_rows, 128), F32),
            pltpu.VMEM((tok_rows, 128), F32),
        ],
        compiler_params=pltpu.CompilerParams(vmem_limit_bytes=54 * 1024 * 1024),
        cost_estimate=pl.CostEstimate(flops=0, bytes_accessed=1024, transcendentals=0),
        name="attend_last" if last else "attend_first",
    )(*scalars, queries, queries, wkt, wv, *held, *[x for _, x in blocks], *[x for _, x in tails])


def mover(line):
    def move(value, route):
        pairs = []
        for place in range(line):
            for side in range(2):
                for core in range(2):
                    to_place, to_side, to_core = route(place, side, core)
                    source = (place * 2 + side) * 2 + core
                    target = ((to_place % line) * 2 + to_side) * 2 + to_core
                    pairs.append((source, target))
        return lax.ppermute(value, AXES, pairs)

    return move


def per_device(
    queries,
    span_latents,
    cache_latents,
    latent_gain,
    key_weight,
    value_weight,
    prefix_length,
    block_order,
):
    line = lax.axis_size("ctx") // 2
    cache_rows = cache_latents.shape[0]
    move = mover(line)
    own = pack(span_latents, cache_latents, latent_gain)

    def swap(value):
        return move(value, lambda p, s, c: (p, s, 1 - c))

    across = move(own, lambda p, s, c: (p, 1 - s, c))
    along = {k: move(own, lambda p, s, c, k=k: (p + k, s ^ c, c)) for k in range(1, line)}
    soon = line - 1
    early = along.pop(soon)
    chunk = functools.partial(attend_chunk, line=line, cache_rows=cache_rows)
    scalars = (block_order, prefix_length)
    turned, early = lax.optimization_barrier((turn(key_weight, 0, ()), early))
    turned = turn(key_weight, 1, (turned,))
    near = [(("own", 0), own), (("across", 0), across)]
    near += [(("along", soon), early), (("swapped", soon), swap(early))]
    held = chunk(False, scalars, queries, turned, value_weight, (), near, [])
    along, held = lax.optimization_barrier((along, held))
    far = [(("along", k), a) for k, a in along.items()]
    far += [(("swapped", k), swap(a)) for k, a in along.items()]
    return chunk(True, scalars, queries, turned, value_weight, held, far, near + far)[0]


def solution(mesh):
    return jax.shard_map(
        per_device,
        mesh=mesh,
        in_specs=(
            P(("groups", "ctx"), "head"),
            P(("groups", "ctx"), None),
            P(("groups", "ctx"), None),
            P(),
            P(None, "head"),
            P(None, "head"),
            P("groups"),
            P("groups"),
        ),
        out_specs=P(("groups", "ctx"), "head"),
        check_vma=False,
    )
```

time: 49.8 us -> 59.2 us (1.19)
  the two profiles are of different devices: /device:TPU:13 before, /device:TPU:0 now
where the time goes in v6:
time: 59.2 us; the launch traced here: 58.7 us
  Pallas kernels  42.8 us (72%)
  starting transfers between devices  11.5 us (19%)
  local copies, waits for them, and re-layouts  2.32 us (4%)
  waiting for transfers between devices  1.33 us (2%)
  between operations  0.72 us (1%)
    pallas_call x2, Pallas kernels, attend_chunk(): pl.pallas_call(functools.partial(chunk_kernel, cfg, last, steps), out_sha...  32.8 us
    ppermute x7, starting transfers between devices, move(): return lax.ppermute(value, AXES, pairs)  11.5 us
    pallas_call x2, Pallas kernels, turn(): pl.pallas_call(turn_kernel, out_shape=jax.ShapeDtypeStruct((width, depth)...  8.21 us
    unnamed x16, local copies, waits for them, and re-layouts  2.32 us
    pallas_call x1, Pallas kernels, pack(): pl.pallas_call(pack_kernel, out_shape=jax.ShapeDtypeStruct((rows, 128), B...  1.81 us
    ppermute x7, waiting for transfers between devices, move(): return lax.ppermute(value, AXES, pairs)  1.33 us
  transfers between devices with their start and end apart: 7, of which 2 were waited for; matrix products, arithmetic and copies ran while one was open for 0% of the time, Pallas kernels for 36%

profile of v6, /device:TPU:0, one launch (start us, length us, event | category | flops | bytes accessed | tf_op | source)
XLA Modules:
  0.0 58.7 jit_solution(13475675352937779034)
XLA Ops:
  0.0 1.8 %pack_rows.1.rest_0_.rest_7_ = bf16[656,128]{1,0:T(8,128)(2,1)} custom-call(bf16[576,128]{1,0:T(8,128)(2,1)} %bitcast.2, bf16[16,576]{1,0:T(8,128)(2,1)} %cache_ref.1, f32[1,512]{1,0:T(1,128)} %bitcast.3), custom_call_target="tpu_custom_call" | custom-call | tf_op jit(solution)/shard_map/pack_rows/pallas_call | solution.py:58
  1.8 0.0 copy-start
  1.8 5.0 %collective-permute-start = (bf16[656,128]{1,0:T(8,128)(2,1)}, bf16[656,128]{1,0:T(8,128)(2,1)S(1)}, u32[]{:S(2)}, u32[]{:S(2)}) collective-permute-start(bf16[656,128]{1,0:T(8,128)(2,1)} %pack_rows.1.rest_0_.rest_7_), channel_id=1, source_target_pairs={{0,12},{1,15},{2,14},{3,13},{4,0},{5,3},{6,2},{7,1},{8,4},{9,7},{1... | collective-permute-start | bytes 503816 | tf_op jit(solution)/shard_map/ppermute | solution.py:321
  6.9 1.5 %collective-permute-start.3 = (bf16[656,128]{1,0:T(8,128)(2,1)}, bf16[656,128]{1,0:T(8,128)(2,1)S(1)}, u32[]{:S(2)}, u32[]{:S(2)}) collective-permute-start(bf16[656,128]{1,0:T(8,128)(2,1)} %pack_rows.1.rest_0_.rest_7_), channel_id=1, source_target_pairs={{0,2},{1,3},{2,0},{3,1},{4,6},{5,7},{6,4},{7,5},{8,10},{9,11},{10,... | collective-permute-start | bytes 503816 | tf_op jit(solution)/shard_map/ppermute | solution.py:321
  8.4 4.1 %turn_key_weight.2.rest_0_ = bf16[4096,512]{1,0:T(8,128)(2,1)} custom-call(bf16[512,4096]{1,0:T(8,128)(2,1)} %wk_ref.3), custom_call_target="tpu_custom_call" | custom-call | bytes 1024 | tf_op jit(solution)/shard_map/turn_key_weight/pallas_call | solution.py:86
  12.5 0.0 collective-permute-done.rest_2_.rest_9_
  12.5 0.0 copy-start.1
  12.5 0.0 collective-permute-start.4
  12.5 0.0 copy-done
  12.5 0.6 %collective-permute-start.2 = (bf16[656,128]{1,0:T(8,128)(2,1)S(1)}, bf16[656,128]{1,0:T(8,128)(2,1)S(1)}, u32[]{:S(2)}, u32[]{:S(2)}) collective-permute-start(bf16[656,128]{1,0:T(8,128)(2,1)S(1)} %copy-done), channel_id=1, source_target_pairs={{0,8},{1,11},{2,10},{3,9},{4,12},{5,15},{6,14},{7,13},{8,0},{9,3},... | collective-permute-start | bytes 503816 | tf_op jit(solution)/shard_map/ppermute | solution.py:321
  13.1 3.4 %collective-permute-start.1 = (bf16[656,128]{1,0:T(8,128)(2,1)S(1)}, bf16[656,128]{1,0:T(8,128)(2,1)S(1)}, u32[]{:S(2)}, u32[]{:S(2)}) collective-permute-start(bf16[656,128]{1,0:T(8,128)(2,1)S(1)} %copy-done), channel_id=1, source_target_pairs={{0,4},{1,7},{2,6},{3,5},{4,8},{5,11},{6,10},{7,9},{8,12},{9,15},{1... | collective-permute-start | bytes 503816 | tf_op jit(solution)/shard_map/ppermute | solution.py:321
  17.1 4.1 %turn_key_weight.3.wk_ref = bf16[4096,512]{1,0:T(8,128)(2,1)} custom-call(bf16[512,4096]{1,0:T(8,128)(2,1)} %wk_ref.3, bf16[4096,512]{1,0:T(8,128)(2,1)} %turn_key_weight.2.rest_0_), custom_call_target="tpu_custom_call", output_to_operand_aliasing={{}: (1, {})} | custom-call | bytes 1024 | tf_op jit(solution)/shard_map/turn_key_weight/pallas_call | solution.py:86
  21.3 0.0 copy-done.1
  21.3 0.0 collective-permute-done.3.rest_1_.rest_8_
  21.3 0.0 copy-start.2
  21.3 0.0 collective-permute-done.4.rest_3_.rest_10_
  21.3 0.7 %copy-done.2 = bf16[656,128]{1,0:T(8,128)(2,1)} copy-done((bf16[656,128]{1,0:T(8,128)(2,1)}, bf16[656,128]{1,0:T(8,128)(2,1)S(1)}, u32[]{:S(2)}) %copy-start.2) | copy-done | bytes 167960
  21.9 0.0 copy-start.3
  21.9 0.7 %copy-done.3 = bf16[656,128]{1,0:T(8,128)(2,1)} copy-done((bf16[656,128]{1,0:T(8,128)(2,1)}, bf16[656,128]{1,0:T(8,128)(2,1)S(1)}, u32[]{:S(2)}) %copy-start.3) | copy-done | bytes 167960
  22.6 13.1 %attend_first.1 = (f32[128,4096]{1,0:T(8,128)}, f32[128,2048]{1,0:T(8,128)}) custom-call(s32[8]{0:T(128)} %order_ref.3, s32[1]{0:T(128)S(6)} %copy.11.prefix_ref, bf16[128,6144]{1,0:T(8,128)(2,1)} %q_new_ref.3, bf16[128,6144]{1,0:T(8,128)(2,1)} %q_new_ref.3, bf16[4096,512]{1,0:T(8,128)(2,1)} %turn_key_weight.3.wk_ref, bf16[512,4096]{1,0:T(8,128)(2,1)} %wv_ref.3, ...), custom_call_target="tpu_custom_call" | custom-call | bytes 1024 | tf_op jit(solution)/shard_map/attend_first/pallas_call | solution.py:288
  35.7 0.0 collective-permute-done.2.rest_4_.rest_12_
  35.7 0.0 copy-start.4
  35.7 0.0 collective-permute-done.1.rest_3_.rest_11_
  35.7 0.0 copy-start.5
  35.7 0.9 %collective-permute-start.5 = (bf16[656,128]{1,0:T(8,128)(2,1)S(1)}, bf16[656,128]{1,0:T(8,128)(2,1)S(1)}, u32[]{:S(2)}, u32[]{:S(2)}) collective-permute-start(bf16[656,128]{1,0:T(8,128)(2,1)S(1)} %collective-permute-done.1.rest_3_.rest_11_), channel_id=1, source_target_pairs={{0,1},{1,0},{2,3},{3,2},{4,5},{5,4},{6,7},{7,6},{8,9},{9,8},{10,11... | collective-permute-start | bytes 503816 | tf_op jit(solution)/shard_map/ppermute | solution.py:321
  36.6 0.1 collective-permute-start.6
  36.7 1.0 %collective-permute-done.5.rest_5_.rest_13_ = bf16[656,128]{1,0:T(8,128)(2,1)S(1)} collective-permute-done((bf16[656,128]{1,0:T(8,128)(2,1)S(1)}, bf16[656,128]{1,0:T(8,128)(2,1)S(1)}, u32[]{:S(2)}, u32[]{:S(2)}) %collective-permute-start.5) | collective-permute-done | bytes 167968 | tf_op jit(solution)/shard_map/ppermute | solution.py:321
  37.6 0.0 copy-start.6
  37.6 0.4 collective-permute-done.6.rest_6_.rest_14_
  38.0 0.0 copy-done.4
  38.0 0.0 copy-done.5
  38.0 0.3 copy-done.6
  38.3 0.0 copy-start.7
  38.3 0.7 %copy-done.7 = bf16[656,128]{1,0:T(8,128)(2,1)} copy-done((bf16[656,128]{1,0:T(8,128)(2,1)}, bf16[656,128]{1,0:T(8,128)(2,1)S(1)}, u32[]{:S(2)}) %copy-start.7) | copy-done | bytes 167960
  39.0 19.7 %attend_last.1 = bf16[128,4096]{1,0:T(8,128)(2,1)} custom-call(s32[8]{0:T(128)} %order_ref.3, s32[1]{0:T(128)S(6)} %copy.11.prefix_ref, bf16[128,6144]{1,0:T(8,128)(2,1)} %q_new_ref.3, bf16[128,6144]{1,0:T(8,128)(2,1)} %q_new_ref.3, bf16[4096,512]{1,0:T(8,128)(2,1)} %turn_key_weight.3.wk_ref, bf16[512,4096]{1,0:T(8,128)(2,1)} %wv_ref.3, ...), custom_call_target="tpu_custom_call" | custom-call | bytes 1024 | tf_op jit(solution)/shard_map/attend_last/pallas_call | solution.py:288
Async XLA Ops:
  1.8 10.7 %copy-start = (bf16[656,128]{1,0:T(8,128)(2,1)S(1)}, bf16[656,128]{1,0:T(8,128)(2,1)}, u32[]{:S(2)}) copy-start(bf16[656,128]{1,0:T(8,128)(2,1)} %pack_rows.1.rest_0_.rest_7_) | copy-start | bytes 503812
  1.8 10.7 %collective-permute-start = (bf16[656,128]{1,0:T(8,128)(2,1)}, bf16[656,128]{1,0:T(8,128)(2,1)S(1)}, u32[]{:S(2)}, u32[]{:S(2)}) collective-permute-start(bf16[656,128]{1,0:T(8,128)(2,1)} %pack_rows.1.rest_0_.rest_7_), channel_id=1, source_target_pairs={{0,12},{1,15},{2,14},{3,13},{4,0},{5,3},{6,2},{7,1},{8,4},{9,7},{1... | collective-permute-start | bytes 503816 | tf_op jit(solution)/shard_map/ppermute | solution.py:321
  6.9 14.4 %collective-permute-start.3 = (bf16[656,128]{1,0:T(8,128)(2,1)}, bf16[656,128]{1,0:T(8,128)(2,1)S(1)}, u32[]{:S(2)}, u32[]{:S(2)}) collective-permute-start(bf16[656,128]{1,0:T(8,128)(2,1)} %pack_rows.1.rest_0_.rest_7_), channel_id=1, source_target_pairs={{0,2},{1,3},{2,0},{3,1},{4,6},{5,7},{6,4},{7,5},{8,10},{9,11},{10,... | collective-permute-start | bytes 503816 | tf_op jit(solution)/shard_map/ppermute | solution.py:321
  12.5 8.8 %copy-start.1 = (bf16[656,128]{1,0:T(8,128)(2,1)}, bf16[656,128]{1,0:T(8,128)(2,1)S(1)}, u32[]{:S(2)}) copy-start(bf16[656,128]{1,0:T(8,128)(2,1)S(1)} %collective-permute-done.rest_2_.rest_9_) | copy-start | bytes 503812
  12.5 8.8 %collective-permute-start.4 = (bf16[656,128]{1,0:T(8,128)(2,1)S(1)}, bf16[656,128]{1,0:T(8,128)(2,1)S(1)}, u32[]{:S(2)}, u32[]{:S(2)}) collective-permute-start(bf16[656,128]{1,0:T(8,128)(2,1)S(1)} %collective-permute-done.rest_2_.rest_9_), channel_id=1, source_target_pairs={{0,1},{1,0},{2,3},{3,2},{4,5},{5,4},{6,7},{7,6},{8,9},{9,8},{10,11... | collective-permute-start | bytes 503816 | tf_op jit(solution)/shard_map/ppermute | solution.py:321
  12.5 23.2 %collective-permute-start.2 = (bf16[656,128]{1,0:T(8,128)(2,1)S(1)}, bf16[656,128]{1,0:T(8,128)(2,1)S(1)}, u32[]{:S(2)}, u32[]{:S(2)}) collective-permute-start(bf16[656,128]{1,0:T(8,128)(2,1)S(1)} %copy-done), channel_id=1, source_target_pairs={{0,8},{1,11},{2,10},{3,9},{4,12},{5,15},{6,14},{7,13},{8,0},{9,3},... | collective-permute-start | bytes 503816 | tf_op jit(solution)/shard_map/ppermute | solution.py:321
  13.1 22.6 %collective-permute-start.1 = (bf16[656,128]{1,0:T(8,128)(2,1)S(1)}, bf16[656,128]{1,0:T(8,128)(2,1)S(1)}, u32[]{:S(2)}, u32[]{:S(2)}) collective-permute-start(bf16[656,128]{1,0:T(8,128)(2,1)S(1)} %copy-done), channel_id=1, source_target_pairs={{0,4},{1,7},{2,6},{3,5},{4,8},{5,11},{6,10},{7,9},{8,12},{9,15},{1... | collective-permute-start | bytes 503816 | tf_op jit(solution)/shard_map/ppermute | solution.py:321
  21.3 0.7 %copy-start.2 = (bf16[656,128]{1,0:T(8,128)(2,1)}, bf16[656,128]{1,0:T(8,128)(2,1)S(1)}, u32[]{:S(2)}) copy-start(bf16[656,128]{1,0:T(8,128)(2,1)S(1)} %collective-permute-done.3.rest_1_.rest_8_) | copy-start | bytes 503812
  21.9 0.7 %copy-start.3 = (bf16[656,128]{1,0:T(8,128)(2,1)}, bf16[656,128]{1,0:T(8,128)(2,1)S(1)}, u32[]{:S(2)}) copy-start(bf16[656,128]{1,0:T(8,128)(2,1)S(1)} %collective-permute-done.4.rest_3_.rest_10_) | copy-start | bytes 503812
  35.7 2.3 %copy-start.4 = (bf16[656,128]{1,0:T(8,128)(2,1)}, bf16[656,128]{1,0:T(8,128)(2,1)S(1)}, u32[]{:S(2)}) copy-start(bf16[656,128]{1,0:T(8,128)(2,1)S(1)} %collective-permute-done.2.rest_4_.rest_12_) | copy-start | bytes 503812
  35.7 2.3 %copy-start.5 = (bf16[656,128]{1,0:T(8,128)(2,1)}, bf16[656,128]{1,0:T(8,128)(2,1)S(1)}, u32[]{:S(2)}) copy-start(bf16[656,128]{1,0:T(8,128)(2,1)S(1)} %collective-permute-done.1.rest_3_.rest_11_) | copy-start | bytes 503812
  35.7 1.9 %collective-permute-start.5 = (bf16[656,128]{1,0:T(8,128)(2,1)S(1)}, bf16[656,128]{1,0:T(8,128)(2,1)S(1)}, u32[]{:S(2)}, u32[]{:S(2)}) collective-permute-start(bf16[656,128]{1,0:T(8,128)(2,1)S(1)} %collective-permute-done.1.rest_3_.rest_11_), channel_id=1, source_target_pairs={{0,1},{1,0},{2,3},{3,2},{4,5},{5,4},{6,7},{7,6},{8,9},{9,8},{10,11... | collective-permute-start | bytes 503816 | tf_op jit(solution)/shard_map/ppermute | solution.py:321
  36.6 1.4 %collective-permute-start.6 = (bf16[656,128]{1,0:T(8,128)(2,1)S(1)}, bf16[656,128]{1,0:T(8,128)(2,1)S(1)}, u32[]{:S(2)}, u32[]{:S(2)}) collective-permute-start(bf16[656,128]{1,0:T(8,128)(2,1)S(1)} %collective-permute-done.2.rest_4_.rest_12_), channel_id=1, source_target_pairs={{0,1},{1,0},{2,3},{3,2},{4,5},{5,4},{6,7},{7,6},{8,9},{9,8},{10,11... | collective-permute-start | bytes 503816 | tf_op jit(solution)/shard_map/ppermute | solution.py:321
  37.6 0.7 %copy-start.6 = (bf16[656,128]{1,0:T(8,128)(2,1)}, bf16[656,128]{1,0:T(8,128)(2,1)S(1)}, u32[]{:S(2)}) copy-start(bf16[656,128]{1,0:T(8,128)(2,1)S(1)} %collective-permute-done.5.rest_5_.rest_13_) | copy-start | bytes 503812
  38.3 0.7 %copy-start.7 = (bf16[656,128]{1,0:T(8,128)(2,1)}, bf16[656,128]{1,0:T(8,128)(2,1)S(1)}, u32[]{:S(2)}) copy-start(bf16[656,128]{1,0:T(8,128)(2,1)S(1)} %collective-permute-done.6.rest_6_.rest_14_) | copy-start | bytes 503812

commit v7 on v5

v7 whole, which is shorter than its diff:
```python
import functools
import math

import jax
import jax.numpy as jnp
from jax import lax
from jax.experimental import pallas as pl
from jax.experimental.pallas import tpu as pltpu
from jax.sharding import PartitionSpec as P

LATENT = 512
ROPE = 64
NOPE = 128
VDIM = 128
PACKED = 640
QK = 256
NEG = -1e30
VMEM_BYTES = 50 * 1024 * 1024
AXES = ("ctx", "head")
BF = jnp.bfloat16
F32 = jnp.float32


def vmem_spec():
    return pl.BlockSpec(memory_space=pltpu.VMEM)


def smem_spec():
    return pl.BlockSpec(memory_space=pltpu.SMEM)


def pack_kernel(span_ref, cache_ref, gain_ref, out_ref):
    tok_rows = span_ref.shape[1]
    cache_rows = cache_ref.shape[0]
    latent = span_ref[:LATENT, :].astype(F32)
    mean_square = jnp.mean(latent * latent, axis=0, keepdims=True)
    normed = ((latent * lax.rsqrt(mean_square + 1e-06)).T * gain_ref[...]).astype(BF)
    tiles = LATENT // 128
    for tile in range(tiles):
        out_ref[tile * tok_rows : (tile + 1) * tok_rows, :] = normed[:, tile * 128 : (tile + 1) * 128]
    at = tiles * tok_rows
    out_ref[at : at + ROPE, :] = span_ref[LATENT:, :]
    at += ROPE
    for tile in range(tiles):
        out_ref[at : at + cache_rows, :] = cache_ref[:, tile * 128 : (tile + 1) * 128]
        at += cache_rows
    out_ref[at:, :] = jnp.zeros((cache_rows, 128), BF)
    out_ref[at:, :ROPE] = cache_ref[:, LATENT:]


def pack(span_latents, cache_latents, gain):
    tok_rows = span_latents.shape[0]
    cache_rows = cache_latents.shape[0]
    rows = (LATENT // 128) * (tok_rows + cache_rows) + ROPE + cache_rows
    return pl.pallas_call(
        pack_kernel,
        out_shape=jax.ShapeDtypeStruct((rows, 128), BF),
        in_specs=[vmem_spec(), vmem_spec(), vmem_spec()],
        out_specs=vmem_spec(),
        name="pack_rows",
    )(span_latents.T, cache_latents, gain.reshape(1, LATENT))


def origin(route, place, side, core, line):
    kind, step = route
    if kind == "own":
        return place * 2 + side
    if kind == "across":
        return place * 2 + 1 - side
    came = lax.rem(place + line - step, line)
    lane_side = lax.rem(side + core, 2) if kind == "along" else lax.rem(side + 1 - core, 2)
    return came * 2 + lane_side


def start_kernel(wk_ref, *rest):
    blocks = rest[:-3]
    wkt_ref, keys_ref, turned_ref = rest[-3:]
    tok_rows = turned_ref.shape[1] // len(blocks)

    @pl.when(pl.program_id(0) == 0)
    def _():
        for slot, block in enumerate(blocks):
            for tile in range(LATENT // 128):
                part = block[tile * tok_rows : (tile + 1) * tok_rows, :]
                turned_ref[tile * 128 : (tile + 1) * 128, slot * tok_rows : (slot + 1) * tok_rows] = part.T

    wkt = wk_ref[...].T
    wkt_ref[...] = wkt
    keys_ref[...] = jnp.dot(wkt, turned_ref[...], preferred_element_type=F32).astype(BF)


def start(key_weight, blocks, tok_rows):
    depth, width = key_weight.shape
    steps = 8
    block = width // steps
    keys = len(blocks) * tok_rows
    return pl.pallas_call(
        start_kernel,
        out_shape=(jax.ShapeDtypeStruct((width, depth), BF), jax.ShapeDtypeStruct((width, keys), BF)),
        grid=(steps,),
        in_specs=[pl.BlockSpec((depth, block), lambda i: (0, i))] + [vmem_spec()] * len(blocks),
        out_specs=(
            pl.BlockSpec((block, depth), lambda i: (i, 0)),
            pl.BlockSpec((block, keys), lambda i: (i, 0)),
        ),
        scratch_shapes=[pltpu.VMEM((depth, keys), BF)],
        compiler_params=pltpu.CompilerParams(vmem_limit_bytes=VMEM_BYTES),
        cost_estimate=pl.CostEstimate(
            flops=2 * keys * depth * width, bytes_accessed=depth * width * 4, transcendentals=0
        ),
        name="start_keys",
    )(key_weight, *blocks)


def gather_rows(cfg, early, order_ref, prefix_ref, blocks, tails, rows_ref, turned_ref, bias_ref):
    routes, cached, line, cache_rows, tok_rows = cfg
    tiles = LATENT // 128
    me = lax.axis_index("ctx")
    core = lax.axis_index("head")
    place = lax.div(me, 2)
    side = lax.rem(me, 2)
    for slot, route in enumerate(routes):
        to = slice(slot * tok_rows, (slot + 1) * tok_rows)
        for tile in range(tiles):
            part = blocks[slot][tile * tok_rows : (tile + 1) * tok_rows, :]
            rows_ref[to, tile * 128 : (tile + 1) * 128] = part
            if slot >= early:
                turned_ref[tile * 128 : (tile + 1) * 128, to] = part.T
        turned_ref[LATENT:, to] = blocks[slot][tiles * tok_rows : tiles * tok_rows + ROPE, :]
        hidden = order_ref[origin(route, place, side, core, line)] > order_ref[me]
        bias_ref[:, to] = jnp.full((1, tok_rows), jnp.where(hidden, NEG, 0.0), F32)
    if not cached:
        return
    at = len(routes) * tok_rows
    lanes = lax.broadcasted_iota(jnp.int32, (1, len(cached) * cache_rows), 1)
    slots = jnp.zeros_like(lanes)
    base = tiles * tok_rows + ROPE
    rotary = []
    for index, route in enumerate(cached):
        to = slice(at + index * cache_rows, at + (index + 1) * cache_rows)
        for tile in range(tiles):
            begin = base + tile * cache_rows
            rows_ref[to, tile * 128 : (tile + 1) * 128] = tails[index][begin : begin + cache_rows, :]
        rotary.append(tails[index][base + tiles * cache_rows :, :])
        inside = lanes - index * cache_rows
        source = origin(route, place, side, core, line) * cache_rows
        slots = jnp.where(jnp.logical_and(inside >= 0, inside < cache_rows), source + inside, slots)
    turned_ref[:LATENT, at:] = rows_ref[at:, :].T
    turned_ref[LATENT:, at:] = jnp.concatenate(rotary, axis=0).T[:ROPE, :]
    bias_ref[:, at:] = jnp.where(slots >= prefix_ref[0], NEG, 0.0)


def attend_kernel(cfg, early, heads, order_ref, prefix_ref, q_ref, wkt_ref, keys_ref, wv_ref, *rest):
    routes, cached = cfg[:2]
    tok_rows = cfg[4]
    blocks = rest[: len(routes)]
    out_ref, rows_ref, turned_ref, bias_ref = rest[len(routes) :]
    scale = math.log2(math.e) / math.sqrt(NOPE + ROPE)

    @pl.when(pl.program_id(0) == 0)
    def _():
        gather_rows(cfg, early, order_ref, prefix_ref, blocks, blocks, rows_ref, turned_ref, bias_ref)

    here = early * tok_rows
    late = jnp.dot(wkt_ref[...], turned_ref[:LATENT, here:], preferred_element_type=F32).astype(BF)
    keys = jnp.concatenate([keys_ref[...], late], axis=1)
    rotary = turned_ref[LATENT:, :]
    nothing = jnp.zeros((QK - NOPE - ROPE, rotary.shape[1]), BF)
    bias = bias_ref[:, tok_rows:]
    row_ids = lax.broadcasted_iota(jnp.int32, (tok_rows, tok_rows), 0)
    col_ids = lax.broadcasted_iota(jnp.int32, (tok_rows, tok_rows), 1)
    causal = jnp.where(col_ids <= row_ids, 0.0, NEG)
    weights = []
    sums = []
    for head in range(heads):
        nope = keys[head * NOPE : head * NOPE + NOPE]
        if head % 2 == 0:
            at = (head // 2) * 384
            full = jnp.concatenate([nope, rotary, nothing], axis=0)
        else:
            at = (head // 2) * 384 + 128
            full = jnp.concatenate([nothing, nope, rotary], axis=0)
        scores = jnp.dot(q_ref[:, at : at + QK], full, preferred_element_type=F32)
        scores = jnp.concatenate([scores[:, :tok_rows] + causal, scores[:, tok_rows:] + bias], axis=1)
        peak = jnp.max(scores, axis=1, keepdims=True)
        exponent = jnp.exp2((scores - peak) * scale)
        sums.append(jnp.sum(exponent, axis=1, keepdims=True))
        weights.append(exponent.astype(BF))
    mixed = jnp.dot(jnp.concatenate(weights, axis=0), rows_ref[...], preferred_element_type=F32).astype(BF)
    for pair in range(heads // 2):
        lanes = slice(pair * 2 * VDIM, (pair + 1) * 2 * VDIM)
        rows = mixed[pair * 2 * tok_rows : (pair + 1) * 2 * tok_rows]
        both = jnp.dot(rows, wv_ref[:, lanes], preferred_element_type=F32)
        for side in range(2):
            head = pair * 2 + side
            out = both[side * tok_rows : (side + 1) * tok_rows, side * VDIM : (side + 1) * VDIM]
            out_ref[:, head * VDIM : (head + 1) * VDIM] = (out / sums[head]).astype(BF)


def attend(scalars, queries, wkt, early_keys, wv, blocks, early, line, cache_rows):
    tok_rows = queries.shape[0]
    all_heads = wv.shape[1] // VDIM
    routes = tuple(route for route, _ in blocks)
    keys = len(routes) * (tok_rows + cache_rows)
    heads = 4 if keys <= 2048 else 2
    cfg = (routes, routes, line, cache_rows, tok_rows)
    return pl.pallas_call(
        functools.partial(attend_kernel, cfg, early, heads),
        out_shape=jax.ShapeDtypeStruct((tok_rows, all_heads * VDIM), BF),
        grid=(all_heads // heads,),
        in_specs=[
            smem_spec(),
            smem_spec(),
            pl.BlockSpec((tok_rows, heads * (NOPE + ROPE)), lambda i: (0, i)),
            pl.BlockSpec((heads * NOPE, LATENT), lambda i: (i, 0)),
            pl.BlockSpec((heads * NOPE, early * tok_rows), lambda i: (i, 0)),
            pl.BlockSpec((LATENT, heads * VDIM), lambda i: (0, i)),
        ]
        + [vmem_spec()] * len(blocks),
        out_specs=pl.BlockSpec((tok_rows, heads * VDIM), lambda i: (0, i)),
        scratch_shapes=[
            pltpu.VMEM((keys, LATENT), BF),
            pltpu.VMEM((LATENT + ROPE, keys), BF),
            pltpu.VMEM((1, keys), F32),
        ],
        compiler_params=pltpu.CompilerParams(vmem_limit_bytes=VMEM_BYTES),
        cost_estimate=pl.CostEstimate(
            flops=2 * keys * all_heads * (LATENT * NOPE + tok_rows * (QK + LATENT)),
            bytes_accessed=LATENT * all_heads * 512,
            transcendentals=keys * tok_rows * all_heads,
        ),
        name="attend",
    )(*scalars, queries, wkt, early_keys, wv, *[x for _, x in blocks])


def mover(line):
    def move(value, route):
        pairs = []
        for place in range(line):
            for side in range(2):
                for core in range(2):
                    to_place, to_side, to_core = route(place, side, core)
                    source = (place * 2 + side) * 2 + core
                    target = ((to_place % line) * 2 + to_side) * 2 + to_core
                    pairs.append((source, target))
        return lax.ppermute(value, AXES, pairs)

    return move


def per_device(
    queries,
    span_latents,
    cache_latents,
    latent_gain,
    key_weight,
    value_weight,
    prefix_length,
    block_order,
):
    line = lax.axis_size("ctx") // 2
    cache_rows = cache_latents.shape[0]
    move = mover(line)
    own = pack(span_latents, cache_latents, latent_gain)
    across = move(own, lambda p, s, c: (p, 1 - s, c))
    along = [move(own, lambda p, s, c, k=k: (p + k, s ^ c, c)) for k in range(1, line)]
    turned, early_keys = start(key_weight, [own, across], queries.shape[0])
    along, turned, early_keys = lax.optimization_barrier((along, turned, early_keys))
    swapped = [move(a, lambda p, s, c: (p, s, 1 - c)) for a in along]
    blocks = [(("own", 0), own), (("across", 0), across)]
    blocks += [(("along", k + 1), a) for k, a in enumerate(along)]
    blocks += [(("swapped", k + 1), w) for k, w in enumerate(swapped)]
    scalars = (block_order, prefix_length)
    return attend(scalars, queries, turned, early_keys, value_weight, blocks, 2, line, cache_rows)


def solution(mesh):
    return jax.shard_map(
        per_device,
        mesh=mesh,
        in_specs=(
            P(("groups", "ctx"), "head"),
            P(("groups", "ctx"), None),
            P(("groups", "ctx"), None),
            P(),
            P(None, "head"),
            P(None, "head"),
            P("groups"),
            P("groups"),
        ),
        out_specs=P(("groups", "ctx"), "head"),
        check_vma=False,
    )
```

time: 49.8 us -> 46.1 us (0.926)
  the two profiles are of different devices: /device:TPU:13 before, /device:TPU:0 now
where the time goes in v7:
time: 46.1 us; the launch traced here: 45.7 us
  Pallas kernels  30.4 us (66%)
  starting transfers between devices  8.42 us (18%)
  waiting for transfers between devices  3.99 us (9%)
  local copies, waits for them, and re-layouts  2.25 us (5%)
  between operations  0.68 us (1%)
    pallas_call x1, Pallas kernels, attend(): pl.pallas_call(functools.partial(attend_kernel, cfg, early, heads), out_s...  21.2 us
    ppermute x7, starting transfers between devices, move(): return lax.ppermute(value, AXES, pairs)  8.42 us
    pallas_call x1, Pallas kernels, start(): pl.pallas_call(start_kernel, out_shape=(jax.ShapeDtypeStruct((width, dept...  7.4 us
    ppermute x7, waiting for transfers between devices, move(): return lax.ppermute(value, AXES, pairs)  3.99 us
    unnamed x10, local copies, waits for them, and re-layouts  2.25 us
    pallas_call x1, Pallas kernels, pack(): pl.pallas_call(pack_kernel, out_shape=jax.ShapeDtypeStruct((rows, 128), B...  1.83 us
  transfers between devices with their start and end apart: 7, of which 4 were waited for; matrix products, arithmetic and copies ran while one was open for 0% of the time, Pallas kernels for 16%

profile of v7, /device:TPU:0, one launch (start us, length us, event | category | flops | bytes accessed | tf_op | source)
XLA Modules:
  0.0 45.7 jit_solution(9208736957613961726)
XLA Ops:
  0.0 0.0 copy-start.4
  0.0 1.8 %pack_rows.1.rest_0_ = bf16[656,128]{1,0:T(8,128)(2,1)} custom-call(bf16[576,128]{1,0:T(8,128)(2,1)} %bitcast.2, bf16[16,576]{1,0:T(8,128)(2,1)} %cache_ref.1, f32[1,512]{1,0:T(1,128)} %bitcast.3), custom_call_target="tpu_custom_call" | custom-call | tf_op jit(solution)/shard_map/pack_rows/pallas_call | solution.py:55
  1.8 3.0 %collective-permute-start.3 = (bf16[656,128]{1,0:T(8,128)(2,1)}, bf16[656,128]{1,0:T(8,128)(2,1)S(1)}, u32[]{:S(2)}, u32[]{:S(2)}) collective-permute-start(bf16[656,128]{1,0:T(8,128)(2,1)} %pack_rows.1.rest_0_), channel_id=1, source_target_pairs={{0,2},{1,3},{2,0},{3,1},{4,6},{5,7},{6,4},{7,5},{8,10},{9,11},{10,... | collective-permute-start | bytes 503816 | tf_op jit(solution)/shard_map/ppermute | solution.py:246
  4.8 3.6 %collective-permute-start.2 = (bf16[656,128]{1,0:T(8,128)(2,1)}, bf16[656,128]{1,0:T(8,128)(2,1)S(1)}, u32[]{:S(2)}, u32[]{:S(2)}) collective-permute-start(bf16[656,128]{1,0:T(8,128)(2,1)} %pack_rows.1.rest_0_), channel_id=1, source_target_pairs={{0,12},{1,15},{2,14},{3,13},{4,0},{5,3},{6,2},{7,1},{8,4},{9,7},{1... | collective-permute-start | bytes 503816 | tf_op jit(solution)/shard_map/ppermute | solution.py:246
  8.4 0.0 collective-permute-start.1
  8.4 1.0 %collective-permute-start = (bf16[656,128]{1,0:T(8,128)(2,1)}, bf16[656,128]{1,0:T(8,128)(2,1)S(1)}, u32[]{:S(2)}, u32[]{:S(2)}) collective-permute-start(bf16[656,128]{1,0:T(8,128)(2,1)} %pack_rows.1.rest_0_), channel_id=1, source_target_pairs={{0,4},{1,7},{2,6},{3,5},{4,8},{5,11},{6,10},{7,9},{8,12},{9,15},{1... | collective-permute-start | bytes 503816 | tf_op jit(solution)/shard_map/ppermute | solution.py:246
  9.4 1.2 %collective-permute-done.3.rest_1_ = bf16[656,128]{1,0:T(8,128)(2,1)S(1)} collective-permute-done((bf16[656,128]{1,0:T(8,128)(2,1)}, bf16[656,128]{1,0:T(8,128)(2,1)S(1)}, u32[]{:S(2)}, u32[]{:S(2)}) %collective-permute-start.3) | collective-permute-done | bytes 167968 | tf_op jit(solution)/shard_map/ppermute | solution.py:246
  10.6 0.0 copy-start
  10.6 0.9 %copy-done = bf16[656,128]{1,0:T(8,128)(2,1)S(1)} copy-done((bf16[656,128]{1,0:T(8,128)(2,1)S(1)}, bf16[656,128]{1,0:T(8,128)(2,1)}, u32[]{:S(2)}) %copy-start) | copy-done | bytes 167960
  11.5 0.0 copy-start.1
  11.5 0.0 copy-start.3
  11.5 7.4 %start_keys.1 = (bf16[4096,512]{1,0:T(8,128)(2,1)}, bf16[4096,256]{1,0:T(8,128)(2,1)S(1)}) custom-call(bf16[512,4096]{1,0:T(8,128)(2,1)} %wk_ref.1, bf16[656,128]{1,0:T(8,128)(2,1)S(1)} %copy-done, bf16[656,128]{1,0:T(8,128)(2,1)S(1)} %collective-permute-done.3.rest_1_), custom_call_target="tpu_custom_call" | custom-call | flops 1073741824 | bytes 8388608 | tf_op jit(solution)/shard_map/start_keys/pallas_call | solution.py:97
  18.9 0.0 copy-start.2
  18.9 1.3 %copy-done.2 = bf16[4096,256]{1,0:T(8,128)(2,1)} copy-done((bf16[4096,256]{1,0:T(8,128)(2,1)}, bf16[4096,256]{1,0:T(8,128)(2,1)S(1)}, u32[]{:S(2)}) %copy-start.2) | copy-done | bytes 2097176
  20.2 0.0 collective-permute-done.2.rest_4_
  20.2 2.4 %collective-permute-done.1.rest_3_ = bf16[656,128]{1,0:T(8,128)(2,1)S(1)} collective-permute-done((bf16[656,128]{1,0:T(8,128)(2,1)}, bf16[656,128]{1,0:T(8,128)(2,1)S(1)}, u32[]{:S(2)}, u32[]{:S(2)}) %collective-permute-start.1) | collective-permute-done | bytes 167968 | tf_op jit(solution)/shard_map/ppermute | solution.py:246
  22.6 0.0 collective-permute-done.rest_2_
  22.6 0.3 collective-permute-start.4
  22.9 0.2 collective-permute-start.5
  23.1 0.3 collective-permute-start.6
  24.1 0.0 collective-permute-done.4.rest_5_
  24.1 0.2 collective-permute-done.5.rest_6_
  24.3 0.2 collective-permute-done.6.rest_7_
  24.5 0.0 copy-done.4
  24.5 0.0 copy-done.1
  24.6 0.0 copy-done.3
  24.6 21.2 %attend.1 = bf16[128,4096]{1,0:T(8,128)(2,1)} custom-call(s32[8]{0:T(128)S(1)} %copy-done.4, s32[1]{0:T(128)S(6)} %copy.9.prefix_ref, bf16[128,6144]{1,0:T(8,128)(2,1)S(1)} %copy-done.3, bf16[4096,512]{1,0:T(8,128)(2,1)} %get-tuple-element.14.wkt_ref, bf16[4096,256]{1,0:T(8,128)(2,1)} %copy-done.2, bf16[512,4096]{1,0:T(8,128)(2,1)} %wv_ref.1, ...), custom_call_target="tpu_custom_call" | custom-call | flops 12079595520 | bytes 8388608 | tf_op jit(solution)/shard_map/attend/pallas_call | solution.py:207
Async XLA Ops:
  0.0 24.5 %copy-start.4 = (s32[8]{0:T(128)S(1)}, s32[8]{0:T(128)}, u32[]{:S(2)}) copy-start(s32[8]{0:T(128)} %order_ref.1) | copy-start | bytes 100
  1.8 8.7 %collective-permute-start.3 = (bf16[656,128]{1,0:T(8,128)(2,1)}, bf16[656,128]{1,0:T(8,128)(2,1)S(1)}, u32[]{:S(2)}, u32[]{:S(2)}) collective-permute-start(bf16[656,128]{1,0:T(8,128)(2,1)} %pack_rows.1.rest_0_), channel_id=1, source_target_pairs={{0,2},{1,3},{2,0},{3,1},{4,6},{5,7},{6,4},{7,5},{8,10},{9,11},{10,... | collective-permute-start | bytes 503816 | tf_op jit(solution)/shard_map/ppermute | solution.py:246
  4.8 15.4 %collective-permute-start.2 = (bf16[656,128]{1,0:T(8,128)(2,1)}, bf16[656,128]{1,0:T(8,128)(2,1)S(1)}, u32[]{:S(2)}, u32[]{:S(2)}) collective-permute-start(bf16[656,128]{1,0:T(8,128)(2,1)} %pack_rows.1.rest_0_), channel_id=1, source_target_pairs={{0,12},{1,15},{2,14},{3,13},{4,0},{5,3},{6,2},{7,1},{8,4},{9,7},{1... | collective-permute-start | bytes 503816 | tf_op jit(solution)/shard_map/ppermute | solution.py:246
  8.4 14.2 %collective-permute-start.1 = (bf16[656,128]{1,0:T(8,128)(2,1)}, bf16[656,128]{1,0:T(8,128)(2,1)S(1)}, u32[]{:S(2)}, u32[]{:S(2)}) collective-permute-start(bf16[656,128]{1,0:T(8,128)(2,1)} %pack_rows.1.rest_0_), channel_id=1, source_target_pairs={{0,8},{1,11},{2,10},{3,9},{4,12},{5,15},{6,14},{7,13},{8,0},{9,3},... | collective-permute-start | bytes 503816 | tf_op jit(solution)/shard_map/ppermute | solution.py:246
  8.4 14.2 %collective-permute-start = (bf16[656,128]{1,0:T(8,128)(2,1)}, bf16[656,128]{1,0:T(8,128)(2,1)S(1)}, u32[]{:S(2)}, u32[]{:S(2)}) collective-permute-start(bf16[656,128]{1,0:T(8,128)(2,1)} %pack_rows.1.rest_0_), channel_id=1, source_target_pairs={{0,4},{1,7},{2,6},{3,5},{4,8},{5,11},{6,10},{7,9},{8,12},{9,15},{1... | collective-permute-start | bytes 503816 | tf_op jit(solution)/shard_map/ppermute | solution.py:246
  10.6 0.9 %copy-start = (bf16[656,128]{1,0:T(8,128)(2,1)S(1)}, bf16[656,128]{1,0:T(8,128)(2,1)}, u32[]{:S(2)}) copy-start(bf16[656,128]{1,0:T(8,128)(2,1)} %pack_rows.1.rest_0_) | copy-start | bytes 503812
  11.5 13.1 %copy-start.1 = (bf16[656,128]{1,0:T(8,128)(2,1)S(1)}, bf16[656,128]{1,0:T(8,128)(2,1)}, u32[]{:S(2)}) copy-start(bf16[656,128]{1,0:T(8,128)(2,1)} %pack_rows.1.rest_0_) | copy-start | bytes 503812
  11.5 13.1 %copy-start.3 = (bf16[128,6144]{1,0:T(8,128)(2,1)S(1)}, bf16[128,6144]{1,0:T(8,128)(2,1)}, u32[]{:S(2)}) copy-start(bf16[128,6144]{1,0:T(8,128)(2,1)} %q_ref.1) | copy-start | bytes 4718596
  18.9 1.3 %copy-start.2 = (bf16[4096,256]{1,0:T(8,128)(2,1)}, bf16[4096,256]{1,0:T(8,128)(2,1)S(1)}, u32[]{:S(2)}) copy-start(bf16[4096,256]{1,0:T(8,128)(2,1)S(1)} %get-tuple-element.15.keys_ref) | copy-start | bytes 6291460
  22.6 1.5 %collective-permute-start.4 = (bf16[656,128]{1,0:T(8,128)(2,1)S(1)}, bf16[656,128]{1,0:T(8,128)(2,1)S(1)}, u32[]{:S(2)}, u32[]{:S(2)}) collective-permute-start(bf16[656,128]{1,0:T(8,128)(2,1)S(1)} %collective-permute-done.rest_2_), channel_id=1, source_target_pairs={{0,1},{1,0},{2,3},{3,2},{4,5},{5,4},{6,7},{7,6},{8,9},{9,8},{10,11... | collective-permute-start | bytes 503816 | tf_op jit(solution)/shard_map/ppermute | solution.py:246
  22.9 1.4 %collective-permute-start.5 = (bf16[656,128]{1,0:T(8,128)(2,1)S(1)}, bf16[656,128]{1,0:T(8,128)(2,1)S(1)}, u32[]{:S(2)}, u32[]{:S(2)}) collective-permute-start(bf16[656,128]{1,0:T(8,128)(2,1)S(1)} %collective-permute-done.1.rest_3_), channel_id=1, source_target_pairs={{0,1},{1,0},{2,3},{3,2},{4,5},{5,4},{6,7},{7,6},{8,9},{9,8},{10,11... | collective-permute-start | bytes 503816 | tf_op jit(solution)/shard_map/ppermute | solution.py:246
  23.1 1.5 %collective-permute-start.6 = (bf16[656,128]{1,0:T(8,128)(2,1)S(1)}, bf16[656,128]{1,0:T(8,128)(2,1)S(1)}, u32[]{:S(2)}, u32[]{:S(2)}) collective-permute-start(bf16[656,128]{1,0:T(8,128)(2,1)S(1)} %collective-permute-done.2.rest_4_), channel_id=1, source_target_pairs={{0,1},{1,0},{2,3},{3,2},{4,5},{5,4},{6,7},{7,6},{8,9},{9,8},{10,11... | collective-permute-start | bytes 503816 | tf_op jit(solution)/shard_map/ppermute | solution.py:246

commit v8 on v7

v8 whole, which is shorter than its diff:
```python
import functools
import math

import jax
import jax.numpy as jnp
from jax import lax
from jax.experimental import pallas as pl
from jax.experimental.pallas import tpu as pltpu
from jax.sharding import PartitionSpec as P

LATENT = 512
ROPE = 64
NOPE = 128
VDIM = 128
PACKED = 640
QK = 256
NEG = -1e30
VMEM_BYTES = 50 * 1024 * 1024
AXES = ("ctx", "head")
BF = jnp.bfloat16
F32 = jnp.float32


def vmem_spec():
    return pl.BlockSpec(memory_space=pltpu.VMEM)


def smem_spec():
    return pl.BlockSpec(memory_space=pltpu.SMEM)


def pack_kernel(span_ref, cache_ref, gain_ref, out_ref):
    tok_rows = span_ref.shape[1]
    cache_rows = cache_ref.shape[0]
    latent = span_ref[:LATENT, :].astype(F32)
    mean_square = jnp.mean(latent * latent, axis=0, keepdims=True)
    normed = ((latent * lax.rsqrt(mean_square + 1e-06)).T * gain_ref[...]).astype(BF)
    tiles = LATENT // 128
    for tile in range(tiles):
        out_ref[tile * tok_rows : (tile + 1) * tok_rows, :] = normed[:, tile * 128 : (tile + 1) * 128]
    at = tiles * tok_rows
    out_ref[at : at + ROPE, :] = span_ref[LATENT:, :]
    at += ROPE
    for tile in range(tiles):
        out_ref[at : at + cache_rows, :] = cache_ref[:, tile * 128 : (tile + 1) * 128]
        at += cache_rows
    out_ref[at:, :] = jnp.zeros((cache_rows, 128), BF)
    out_ref[at:, :ROPE] = cache_ref[:, LATENT:]


def pack(span_latents, cache_latents, gain):
    tok_rows = span_latents.shape[0]
    cache_rows = cache_latents.shape[0]
    rows = (LATENT // 128) * (tok_rows + cache_rows) + ROPE + cache_rows
    return pl.pallas_call(
        pack_kernel,
        out_shape=jax.ShapeDtypeStruct((rows, 128), BF),
        in_specs=[vmem_spec(), vmem_spec(), vmem_spec()],
        out_specs=vmem_spec(),
        name="pack_rows",
    )(span_latents.T, cache_latents, gain.reshape(1, LATENT))


def origin(route, place, side, core, line):
    kind, step = route
    if kind == "own":
        return place * 2 + side
    if kind == "across":
        return place * 2 + 1 - side
    came = lax.rem(place + line - step, line)
    lane_side = lax.rem(side + core, 2) if kind == "along" else lax.rem(side + 1 - core, 2)
    return came * 2 + lane_side


def prepare_kernel(heads, q_ref, wk_ref, wv_ref, latent_ref, wvt_ref):
    rows = q_ref.shape[0]
    turned = q_ref[...].T
    ids = lax.broadcasted_iota(jnp.int32, (PACKED - LATENT - ROPE, rows), 0)
    flags = jnp.where(ids == 0, NEG, 0.0).astype(BF)
    for head in range(heads):
        at = head * (NOPE + ROPE)
        here = slice(head * rows, (head + 1) * rows)
        wk = wk_ref[:, head * NOPE : (head + 1) * NOPE]
        latent_ref[:LATENT, here] = jnp.dot(wk, turned[at : at + NOPE], preferred_element_type=F32).astype(BF)
        latent_ref[LATENT : LATENT + ROPE, here] = turned[at + NOPE : at + NOPE + ROPE]
        latent_ref[LATENT + ROPE :, here] = flags
    wvt_ref[...] = wv_ref[...].T


def prepare(queries, key_weight, value_weight, heads):
    rows = queries.shape[0]
    depth, width = key_weight.shape
    steps = width // (heads * NOPE)
    return pl.pallas_call(
        functools.partial(prepare_kernel, heads),
        out_shape=(
            jax.ShapeDtypeStruct((steps * PACKED, heads * rows), BF),
            jax.ShapeDtypeStruct((steps * heads * VDIM, depth), BF),
        ),
        grid=(steps,),
        in_specs=[
            pl.BlockSpec((rows, heads * (NOPE + ROPE)), lambda i: (0, i)),
            pl.BlockSpec((depth, heads * NOPE), lambda i: (0, i)),
            pl.BlockSpec((depth, heads * VDIM), lambda i: (0, i)),
        ],
        out_specs=(
            pl.BlockSpec((PACKED, heads * rows), lambda i: (i, 0)),
            pl.BlockSpec((heads * VDIM, depth), lambda i: (i, 0)),
        ),
        compiler_params=pltpu.CompilerParams(vmem_limit_bytes=VMEM_BYTES),
        cost_estimate=pl.CostEstimate(
            flops=2 * rows * depth * width, bytes_accessed=depth * width * 8, transcendentals=0
        ),
        name="prepare",
    )(queries, key_weight, value_weight)


def gather_rows(cfg, order_ref, prefix_ref, blocks, rows_ref, turned_ref):
    routes, line, cache_rows, tok_rows = cfg
    tiles = LATENT // 128
    me = lax.axis_index("ctx")
    core = lax.axis_index("head")
    place = lax.div(me, 2)
    side = lax.rem(me, 2)
    lanes = lax.broadcasted_iota(jnp.int32, (tok_rows, ROPE), 1)
    slots = lax.broadcasted_iota(jnp.int32, (cache_rows, 128), 0)
    flag_lane = lax.broadcasted_iota(jnp.int32, (cache_rows, 128), 1) == ROPE
    base = tiles * tok_rows + ROPE
    for slot, route in enumerate(routes):
        block = blocks[slot]
        to = slice(slot * tok_rows, (slot + 1) * tok_rows)
        for tile in range(tiles):
            part = block[tile * tok_rows : (tile + 1) * tok_rows, :]
            rows_ref[to, tile * 128 : (tile + 1) * 128] = part
            turned_ref[tile * 128 : (tile + 1) * 128, to] = part.T
        source = origin(route, place, side, core, line)
        hidden = jnp.where(order_ref[source] > order_ref[me], 1.0, 0.0)
        flags = jnp.where(lanes == 0, hidden, 0.0)
        rotary = block[tiles * tok_rows : base, :].astype(F32).T
        rows_ref[to, LATENT:] = jnp.concatenate([rotary, flags], axis=1).astype(BF)
        at = len(routes) * tok_rows + slot * cache_rows
        to = slice(at, at + cache_rows)
        for tile in range(tiles):
            begin = base + tile * cache_rows
            rows_ref[to, tile * 128 : (tile + 1) * 128] = block[begin : begin + cache_rows, :]
        unused = jnp.logical_and(flag_lane, slots + source * cache_rows >= prefix_ref[0])
        rotary = block[base + tiles * cache_rows :, :].astype(F32)
        rows_ref[to, LATENT:] = jnp.where(unused, 1.0, rotary).astype(BF)
    at = len(routes) * tok_rows
    turned_ref[:, at:] = rows_ref[at:, :LATENT].T


def attend_kernel(cfg, heads, order_ref, prefix_ref, latent_ref, wvt_ref, *rest):
    routes = cfg[0]
    tok_rows = cfg[3]
    blocks = rest[: len(routes)]
    out_ref, rows_ref, turned_ref = rest[len(routes) :]
    scale = math.log2(math.e) / math.sqrt(NOPE + ROPE)

    @pl.when(pl.program_id(0) == 0)
    def _():
        gather_rows(cfg, order_ref, prefix_ref, blocks, rows_ref, turned_ref)

    key_ids = lax.broadcasted_iota(jnp.int32, (tok_rows, heads * tok_rows), 0)
    query_ids = lax.broadcasted_iota(jnp.int32, (tok_rows, heads * tok_rows), 1) % tok_rows
    causal = jnp.where(key_ids <= query_ids, 0.0, NEG)
    scores = jnp.dot(rows_ref[...], latent_ref[...], preferred_element_type=F32)
    scores = jnp.concatenate([scores[:tok_rows] + causal, scores[tok_rows:]], axis=0)
    peak = jnp.max(scores, axis=0, keepdims=True)
    exponent = jnp.exp2((scores - peak) * scale)
    total = jnp.sum(exponent, axis=0, keepdims=True)
    mixed = jnp.dot(turned_ref[...], exponent.astype(BF), preferred_element_type=F32).astype(BF)
    for head in range(heads):
        here = slice(head * tok_rows, (head + 1) * tok_rows)
        wvt = wvt_ref[head * VDIM : (head + 1) * VDIM, :]
        out = jnp.dot(wvt, mixed[:, here], preferred_element_type=F32) / total[:, here]
        out_ref[:, head * VDIM : (head + 1) * VDIM] = out.astype(BF).T


def attend(scalars, latent_queries, wvt, blocks, line, cache_rows, heads):
    tok_rows = latent_queries.shape[1] // heads
    all_heads = wvt.shape[0] // VDIM
    routes = tuple(route for route, _ in blocks)
    keys = len(routes) * (tok_rows + cache_rows)
    cfg = (routes, line, cache_rows, tok_rows)
    return pl.pallas_call(
        functools.partial(attend_kernel, cfg, heads),
        out_shape=jax.ShapeDtypeStruct((tok_rows, all_heads * VDIM), BF),
        grid=(all_heads // heads,),
        in_specs=[
            smem_spec(),
            smem_spec(),
            pl.BlockSpec((PACKED, heads * tok_rows), lambda i: (i, 0)),
            pl.BlockSpec((heads * VDIM, LATENT), lambda i: (i, 0)),
        ]
        + [vmem_spec()] * len(blocks),
        out_specs=pl.BlockSpec((tok_rows, heads * VDIM), lambda i: (0, i)),
        scratch_shapes=[pltpu.VMEM((keys, PACKED), BF), pltpu.VMEM((LATENT, keys), BF)],
        compiler_params=pltpu.CompilerParams(vmem_limit_bytes=VMEM_BYTES),
        cost_estimate=pl.CostEstimate(
            flops=2 * keys * all_heads * tok_rows * (PACKED + LATENT),
            bytes_accessed=LATENT * all_heads * 512,
            transcendentals=keys * tok_rows * all_heads,
        ),
        name="attend",
    )(*scalars, latent_queries, wvt, *[x for _, x in blocks])


def mover(line):
    def move(value, route):
        pairs = []
        for place in range(line):
            for side in range(2):
                for core in range(2):
                    to_place, to_side, to_core = route(place, side, core)
                    source = (place * 2 + side) * 2 + core
                    target = ((to_place % line) * 2 + to_side) * 2 + to_core
                    pairs.append((source, target))
        return lax.ppermute(value, AXES, pairs)

    return move


def per_device(
    queries,
    span_latents,
    cache_latents,
    latent_gain,
    key_weight,
    value_weight,
    prefix_length,
    block_order,
):
    line = lax.axis_size("ctx") // 2
    cache_rows = cache_latents.shape[0]
    move = mover(line)
    own = pack(span_latents, cache_latents, latent_gain)
    heads = 4 if line <= 8 else 2
    across = move(own, lambda p, s, c: (p, 1 - s, c))
    along = [move(own, lambda p, s, c, k=k: (p + k, s ^ c, c)) for k in range(1, line)]
    latent_queries, wvt = prepare(queries, key_weight, value_weight, heads)
    along, latent_queries, wvt = lax.optimization_barrier((along, latent_queries, wvt))
    swapped = [move(a, lambda p, s, c: (p, s, 1 - c)) for a in along]
    blocks = [(("own", 0), own), (("across", 0), across)]
    blocks += [(("along", k + 1), a) for k, a in enumerate(along)]
    blocks += [(("swapped", k + 1), w) for k, w in enumerate(swapped)]
    return attend((block_order, prefix_length), latent_queries, wvt, blocks, line, cache_rows, heads)


def solution(mesh):
    return jax.shard_map(
        per_device,
        mesh=mesh,
        in_specs=(
            P(("groups", "ctx"), "head"),
            P(("groups", "ctx"), None),
            P(("groups", "ctx"), None),
            P(),
            P(None, "head"),
            P(None, "head"),
            P("groups"),
            P("groups"),
        ),
        out_specs=P(("groups", "ctx"), "head"),
        check_vma=False,
    )
```

time: 46.1 us -> 46 us (level)
  Pallas kernels: 30.4 us -> 33.4 us
  waiting for transfers between devices: 3.99 us -> 2.05 us
  local copies, waits for them, and re-layouts: 2.25 us -> 1.41 us
    pallas_call x2, Pallas kernels: 28.6 us -> 31.6 us  [the longest x1 21.4 us: attend(): pl.pallas_call(functools.partial(attend_kernel, cfg, heads), out_shape=ja...]
    ppermute x7, waiting for transfers between devices: 3.99 us -> 2.05 us  [move(): return lax.ppermute(value, AXES, pairs)]
    unnamed x10 -> x6, local copies, waits for them, and re-layouts: 2.25 us -> 1.41 us
  transfers between devices with their start and end apart: 7 -> 7, of which waited for: 4 -> 4; matrix products, arithmetic and copies ran while one was open for 0% -> 0% of each run, Pallas kernels for 16% -> 22%
where the time goes in v8:
time: 46 us; the launch traced here: 45.6 us
  Pallas kernels  33.4 us (73%)
  starting transfers between devices  8.1 us (18%)
  waiting for transfers between devices  2.05 us (4%)
  local copies, waits for them, and re-layouts  1.41 us (3%)
  between operations  0.67 us (1%)
    pallas_call x1, Pallas kernels, attend(): pl.pallas_call(functools.partial(attend_kernel, cfg, heads), out_shape=ja...  21.4 us
    pallas_call x1, Pallas kernels, prepare(): pl.pallas_call(functools.partial(prepare_kernel, heads), out_shape=(jax.S...  10.1 us
    ppermute x7, starting transfers between devices, move(): return lax.ppermute(value, AXES, pairs)  8.1 us
    ppermute x7, waiting for transfers between devices, move(): return lax.ppermute(value, AXES, pairs)  2.05 us
    pallas_call x1, Pallas kernels, pack(): pl.pallas_call(pack_kernel, out_shape=jax.ShapeDtypeStruct((rows, 128), B...  1.83 us
    unnamed x6, local copies, waits for them, and re-layouts  1.41 us
  transfers between devices with their start and end apart: 7, of which 4 were waited for; matrix products, arithmetic and copies ran while one was open for 0% of the time, Pallas kernels for 22%

profile of v8, /device:TPU:0, one launch (start us, length us, event | category | flops | bytes accessed | tf_op | source)
XLA Modules:
  0.0 45.6 jit_solution(12572775043273970393)
XLA Ops:
  0.0 0.0 copy-start.2
  0.0 1.8 %pack_rows.1.rest_0_ = bf16[656,128]{1,0:T(8,128)(2,1)} custom-call(bf16[576,128]{1,0:T(8,128)(2,1)} %bitcast.2, bf16[16,576]{1,0:T(8,128)(2,1)} %cache_ref.1, f32[1,512]{1,0:T(1,128)} %bitcast.3), custom_call_target="tpu_custom_call" | custom-call | tf_op jit(solution)/shard_map/pack_rows/pallas_call | solution.py:55
  1.8 5.0 %collective-permute-start.2 = (bf16[656,128]{1,0:T(8,128)(2,1)}, bf16[656,128]{1,0:T(8,128)(2,1)S(1)}, u32[]{:S(2)}, u32[]{:S(2)}) collective-permute-start(bf16[656,128]{1,0:T(8,128)(2,1)} %pack_rows.1.rest_0_), channel_id=1, source_target_pairs={{0,12},{1,15},{2,14},{3,13},{4,0},{5,3},{6,2},{7,1},{8,4},{9,7},{1... | collective-permute-start | bytes 503816 | tf_op jit(solution)/shard_map/ppermute | solution.py:219
  6.9 0.0 collective-permute-start.1
  6.9 1.0 %collective-permute-start = (bf16[656,128]{1,0:T(8,128)(2,1)}, bf16[656,128]{1,0:T(8,128)(2,1)S(1)}, u32[]{:S(2)}, u32[]{:S(2)}) collective-permute-start(bf16[656,128]{1,0:T(8,128)(2,1)} %pack_rows.1.rest_0_), channel_id=1, source_target_pairs={{0,4},{1,7},{2,6},{3,5},{4,8},{5,11},{6,10},{7,9},{8,12},{9,15},{1... | collective-permute-start | bytes 503816 | tf_op jit(solution)/shard_map/ppermute | solution.py:219
  7.9 1.5 %collective-permute-start.3 = (bf16[656,128]{1,0:T(8,128)(2,1)}, bf16[656,128]{1,0:T(8,128)(2,1)S(1)}, u32[]{:S(2)}, u32[]{:S(2)}) collective-permute-start(bf16[656,128]{1,0:T(8,128)(2,1)} %pack_rows.1.rest_0_), channel_id=1, source_target_pairs={{0,2},{1,3},{2,0},{3,1},{4,6},{5,7},{6,4},{7,5},{8,10},{9,11},{10,... | collective-permute-start | bytes 503816 | tf_op jit(solution)/shard_map/ppermute | solution.py:219
  9.4 0.0 copy-start
  9.4 1.4 %copy-done = bf16[128,6144]{1,0:T(8,128)(2,1)S(1)} copy-done((bf16[128,6144]{1,0:T(8,128)(2,1)S(1)}, bf16[128,6144]{1,0:T(8,128)(2,1)}, u32[]{:S(2)}) %copy-start) | copy-done | bytes 1572888
  10.8 0.0 copy-start.1
  10.8 10.1 %prepare.1 = (bf16[5120,512]{1,0:T(8,128)(2,1)}, bf16[4096,512]{1,0:T(8,128)(2,1)}) custom-call(bf16[128,6144]{1,0:T(8,128)(2,1)S(1)} %copy-done, bf16[512,4096]{1,0:T(8,128)(2,1)} %wk_ref.1, bf16[512,4096]{1,0:T(8,128)(2,1)} %wv_ref.1), custom_call_target="tpu_custom_call" | custom-call | flops 536870912 | bytes 16777216 | tf_op jit(solution)/shard_map/prepare/pallas_call | solution.py:94
  21.0 0.0 collective-permute-done.2.rest_4_
  21.0 1.3 %collective-permute-done.1.rest_3_ = bf16[656,128]{1,0:T(8,128)(2,1)S(1)} collective-permute-done((bf16[656,128]{1,0:T(8,128)(2,1)}, bf16[656,128]{1,0:T(8,128)(2,1)S(1)}, u32[]{:S(2)}, u32[]{:S(2)}) %collective-permute-start.1) | collective-permute-done | bytes 167968 | tf_op jit(solution)/shard_map/ppermute | solution.py:219
  22.3 0.0 collective-permute-done.rest_2_
  22.3 0.0 collective-permute-start.4
  22.3 0.5 %collective-permute-start.5 = (bf16[656,128]{1,0:T(8,128)(2,1)S(1)}, bf16[656,128]{1,0:T(8,128)(2,1)S(1)}, u32[]{:S(2)}, u32[]{:S(2)}) collective-permute-start(bf16[656,128]{1,0:T(8,128)(2,1)S(1)} %collective-permute-done.1.rest_3_), channel_id=1, source_target_pairs={{0,1},{1,0},{2,3},{3,2},{4,5},{5,4},{6,7},{7,6},{8,9},{9,8},{10,11... | collective-permute-start | bytes 503816 | tf_op jit(solution)/shard_map/ppermute | solution.py:219
  22.8 0.0 collective-permute-start.6
  23.5 0.0 collective-permute-done.3.rest_1_
  23.5 0.2 collective-permute-done.4.rest_5_
  23.7 0.2 collective-permute-done.5.rest_6_
  23.9 0.3 collective-permute-done.6.rest_7_
  24.2 0.0 copy-done.2
  24.2 0.0 copy-done.1
  24.2 21.4 %attend.1 = bf16[128,4096]{1,0:T(8,128)(2,1)} custom-call(s32[8]{0:T(128)S(1)} %copy-done.2, s32[1]{0:T(128)S(6)} %copy.9.prefix_ref, bf16[5120,512]{1,0:T(8,128)(2,1)} %get-tuple-element.14.latent_ref, bf16[4096,512]{1,0:T(8,128)(2,1)} %get-tuple-element.15.wvt_ref, bf16[656,128]{1,0:T(8,128)(2,1)S(1)} %copy-done.1, ...), custom_call_target="tpu_custom_call" | custom-call | flops 10871635968 | bytes 8388608 | tf_op jit(solution)/shard_map/attend/pallas_call | solution.py:186
Async XLA Ops:
  0.0 24.2 %copy-start.2 = (s32[8]{0:T(128)S(1)}, s32[8]{0:T(128)}, u32[]{:S(2)}) copy-start(s32[8]{0:T(128)} %order_ref.1) | copy-start | bytes 100
  1.8 19.1 %collective-permute-start.2 = (bf16[656,128]{1,0:T(8,128)(2,1)}, bf16[656,128]{1,0:T(8,128)(2,1)S(1)}, u32[]{:S(2)}, u32[]{:S(2)}) collective-permute-start(bf16[656,128]{1,0:T(8,128)(2,1)} %pack_rows.1.rest_0_), channel_id=1, source_target_pairs={{0,12},{1,15},{2,14},{3,13},{4,0},{5,3},{6,2},{7,1},{8,4},{9,7},{1... | collective-permute-start | bytes 503816 | tf_op jit(solution)/shard_map/ppermute | solution.py:219
  6.9 15.4 %collective-permute-start.1 = (bf16[656,128]{1,0:T(8,128)(2,1)}, bf16[656,128]{1,0:T(8,128)(2,1)S(1)}, u32[]{:S(2)}, u32[]{:S(2)}) collective-permute-start(bf16[656,128]{1,0:T(8,128)(2,1)} %pack_rows.1.rest_0_), channel_id=1, source_target_pairs={{0,8},{1,11},{2,10},{3,9},{4,12},{5,15},{6,14},{7,13},{8,0},{9,3},... | collective-permute-start | bytes 503816 | tf_op jit(solution)/shard_map/ppermute | solution.py:219
  6.9 15.4 %collective-permute-start = (bf16[656,128]{1,0:T(8,128)(2,1)}, bf16[656,128]{1,0:T(8,128)(2,1)S(1)}, u32[]{:S(2)}, u32[]{:S(2)}) collective-permute-start(bf16[656,128]{1,0:T(8,128)(2,1)} %pack_rows.1.rest_0_), channel_id=1, source_target_pairs={{0,4},{1,7},{2,6},{3,5},{4,8},{5,11},{6,10},{7,9},{8,12},{9,15},{1... | collective-permute-start | bytes 503816 | tf_op jit(solution)/shard_map/ppermute | solution.py:219
  7.9 15.6 %collective-permute-start.3 = (bf16[656,128]{1,0:T(8,128)(2,1)}, bf16[656,128]{1,0:T(8,128)(2,1)S(1)}, u32[]{:S(2)}, u32[]{:S(2)}) collective-permute-start(bf16[656,128]{1,0:T(8,128)(2,1)} %pack_rows.1.rest_0_), channel_id=1, source_target_pairs={{0,2},{1,3},{2,0},{3,1},{4,6},{5,7},{6,4},{7,5},{8,10},{9,11},{10,... | collective-permute-start | bytes 503816 | tf_op jit(solution)/shard_map/ppermute | solution.py:219
  9.4 1.4 %copy-start = (bf16[128,6144]{1,0:T(8,128)(2,1)S(1)}, bf16[128,6144]{1,0:T(8,128)(2,1)}, u32[]{:S(2)}) copy-start(bf16[128,6144]{1,0:T(8,128)(2,1)} %q_ref.1) | copy-start | bytes 4718596
  10.8 13.4 %copy-start.1 = (bf16[656,128]{1,0:T(8,128)(2,1)S(1)}, bf16[656,128]{1,0:T(8,128)(2,1)}, u32[]{:S(2)}) copy-start(bf16[656,128]{1,0:T(8,128)(2,1)} %pack_rows.1.rest_0_) | copy-start | bytes 503812
  22.3 1.4 %collective-permute-start.4 = (bf16[656,128]{1,0:T(8,128)(2,1)S(1)}, bf16[656,128]{1,0:T(8,128)(2,1)S(1)}, u32[]{:S(2)}, u32[]{:S(2)}) collective-permute-start(bf16[656,128]{1,0:T(8,128)(2,1)S(1)} %collective-permute-done.rest_2_), channel_id=1, source_target_pairs={{0,1},{1,0},{2,3},{3,2},{4,5},{5,4},{6,7},{7,6},{8,9},{9,8},{10,11... | collective-permute-start | bytes 503816 | tf_op jit(solution)/shard_map/ppermute | solution.py:219
  22.3 1.6 %collective-permute-start.5 = (bf16[656,128]{1,0:T(8,128)(2,1)S(1)}, bf16[656,128]{1,0:T(8,128)(2,1)S(1)}, u32[]{:S(2)}, u32[]{:S(2)}) collective-permute-start(bf16[656,128]{1,0:T(8,128)(2,1)S(1)} %collective-permute-done.1.rest_3_), channel_id=1, source_target_pairs={{0,1},{1,0},{2,3},{3,2},{4,5},{5,4},{6,7},{7,6},{8,9},{9,8},{10,11... | collective-permute-start | bytes 503816 | tf_op jit(solution)/shard_map/ppermute | solution.py:219
  22.8 1.4 %collective-permute-start.6 = (bf16[656,128]{1,0:T(8,128)(2,1)S(1)}, bf16[656,128]{1,0:T(8,128)(2,1)S(1)}, u32[]{:S(2)}, u32[]{:S(2)}) collective-permute-start(bf16[656,128]{1,0:T(8,128)(2,1)S(1)} %collective-permute-done.2.rest_4_), channel_id=1, source_target_pairs={{0,1},{1,0},{2,3},{3,2},{4,5},{5,4},{6,7},{7,6},{8,9},{9,8},{10,11... | collective-permute-start | bytes 503816 | tf_op jit(solution)/shard_map/ppermute | solution.py:219

commit v9 on v8

--- a/solution.py
+++ b/solution.py
@@ -107,7 +107,7 @@
             pl.BlockSpec((PACKED, heads * rows), lambda i: (i, 0)),
             pl.BlockSpec((heads * VDIM, depth), lambda i: (i, 0)),
         ),
-        compiler_params=pltpu.CompilerParams(vmem_limit_bytes=VMEM_BYTES),
+        compiler_params=pltpu.CompilerParams(vmem_limit_bytes=58 * 1024 * 1024),
         cost_estimate=pl.CostEstimate(
             flops=2 * rows * depth * width, bytes_accessed=depth * width * 8, transcendentals=0
         ),
@@ -132,7 +132,6 @@
         for tile in range(tiles):
             part = block[tile * tok_rows : (tile + 1) * tok_rows, :]
             rows_ref[to, tile * 128 : (tile + 1) * 128] = part
-            turned_ref[tile * 128 : (tile + 1) * 128, to] = part.T
         source = origin(route, place, side, core, line)
         hidden = jnp.where(order_ref[source] > order_ref[me], 1.0, 0.0)
         flags = jnp.where(lanes == 0, hidden, 0.0)
@@ -146,35 +145,106 @@
         unused = jnp.logical_and(flag_lane, slots + source * cache_rows >= prefix_ref[0])
         rotary = block[base + tiles * cache_rows :, :].astype(F32)
         rows_ref[to, LATENT:] = jnp.where(unused, 1.0, rotary).astype(BF)
-    at = len(routes) * tok_rows
-    turned_ref[:, at:] = rows_ref[at:, :LATENT].T
-
-
-def attend_kernel(cfg, heads, order_ref, prefix_ref, latent_ref, wvt_ref, *rest):
+
+    def turn(here):
+        turned_ref[:, here] = rows_ref[here, :LATENT].T
+
+    total = rows_ref.shape[0]
+    return [functools.partial(turn, slice(at, at + 128)) for at in range(0, total, 128)]
+
+
+def weave(*lanes):
+    longest = max(len(lane) for lane in lanes)
+    done = [0] * len(lanes)
+    for turn in range(1, longest + 1):
+        for index, lane in enumerate(lanes):
+            while done[index] < len(lane) and done[index] * longest < turn * len(lane):
+                lane[done[index]]()
+                done[index] += 1
+
+
+def attend_kernel(cfg, heads, steps, order_ref, prefix_ref, latent_ref, wvt_ref, *rest):
     routes = cfg[0]
     tok_rows = cfg[3]
     blocks = rest[: len(routes)]
-    out_ref, rows_ref, turned_ref = rest[len(routes) :]
+    out_ref, rows_ref, turned_ref = rest[len(routes) : len(routes) + 3]
+    scratch = rest[len(routes) + 3 :]
+    score_refs, weight_refs, peak_refs, total_refs = (scratch[at : at + 2] for at in (0, 2, 4, 6))
+    keys = rows_ref.shape[0]
+    width = heads * tok_rows
     scale = math.log2(math.e) / math.sqrt(NOPE + ROPE)
-
-    @pl.when(pl.program_id(0) == 0)
+    step = pl.program_id(0)
+    pieces = [slice(at, min(at + 256, keys)) for at in range(0, keys, 256)]
+
+    def by_eights(value):
+        return value.reshape(-1, 8, width)
+
+    def scores(buffer):
+        def piece(index):
+            here = pieces[index]
+            query = latent_ref[buffer * PACKED : (buffer + 1) * PACKED, :]
+            result = jnp.dot(rows_ref[here, :], query, preferred_element_type=F32)
+            if index == 0:
+                key_ids = lax.broadcasted_iota(jnp.int32, (tok_rows, width), 0)
+                query_ids = lax.broadcasted_iota(jnp.int32, (tok_rows, width), 1) % tok_rows
+                causal = jnp.where(key_ids <= query_ids, 0.0, NEG)
+                result = jnp.concatenate([result[:tok_rows] + causal, result[tok_rows:]], axis=0)
+            score_refs[buffer][here, :] = result
+            peak = jnp.max(by_eights(result), axis=0)
+            if index:
+                peak = jnp.maximum(peak, peak_refs[buffer][...])
+            peak_refs[buffer][...] = peak
+
+        return [functools.partial(piece, index) for index in range(len(pieces))]
+
+    def weights(buffer):
+        def piece(index):
+            here = pieces[index]
+            peak = jnp.max(peak_refs[buffer][...], axis=0, keepdims=True)
+            exponent = jnp.exp2((score_refs[buffer][here, :] - peak) * scale)
+            total = jnp.sum(by_eights(exponent), axis=0)
+            if index:
+                total = total + total_refs[buffer][...]
+            total_refs[buffer][...] = total
+            weight_refs[buffer][here, :] = exponent.astype(BF)
+
+        return [functools.partial(piece, index) for index in range(len(pieces))]
+
+    def outputs(buffer):
+        total = jnp.sum(total_refs[buffer][...], axis=0, keepdims=True)
+        parts = []
+
+        def mix(index):
+            here = slice(index * 256, (index + 1) * 256)
+            mixed = jnp.dot(turned_ref[here, :], weight_refs[buffer][...], preferred_element_type=F32)
+            parts.append(mixed.astype(BF))
+
+        def finish():
+            mixed = jnp.concatenate(parts, axis=0)
+            for head in range(heads):
+                here = slice(head * tok_rows, (head + 1) * tok_rows)
+                place = buffer * heads + head
+                wvt = wvt_ref[place * VDIM : (place + 1) * VDIM, :]
+                out = jnp.dot(wvt, mixed[:, here], preferred_element_type=F32) / total[:, here]
+                out_ref[:, place * VDIM : (place + 1) * VDIM] = out.astype(BF).T
+
+        return [functools.partial(mix, index) for index in range(LATENT // 256)] + [finish]
+
+    @pl.when(step == 0)
     def _():
-        gather_rows(cfg, order_ref, prefix_ref, blocks, rows_ref, turned_ref)
-
-    key_ids = lax.broadcasted_iota(jnp.int32, (tok_rows, heads * tok_rows), 0)
-    query_ids = lax.broadcasted_iota(jnp.int32, (tok_rows, heads * tok_rows), 1) % tok_rows
-    causal = jnp.where(key_ids <= query_ids, 0.0, NEG)
-    scores = jnp.dot(rows_ref[...], latent_ref[...], preferred_element_type=F32)
-    scores = jnp.concatenate([scores[:tok_rows] + causal, scores[tok_rows:]], axis=0)
-    peak = jnp.max(scores, axis=0, keepdims=True)
-    exponent = jnp.exp2((scores - peak) * scale)
-    total = jnp.sum(exponent, axis=0, keepdims=True)
-    mixed = jnp.dot(turned_ref[...], exponent.astype(BF), preferred_element_type=F32).astype(BF)
-    for head in range(heads):
-        here = slice(head * tok_rows, (head + 1) * tok_rows)
-        wvt = wvt_ref[head * VDIM : (head + 1) * VDIM, :]
-        out = jnp.dot(wvt, mixed[:, here], preferred_element_type=F32) / total[:, here]
-        out_ref[:, head * VDIM : (head + 1) * VDIM] = out.astype(BF).T
+        turns = gather_rows(cfg, order_ref, prefix_ref, blocks, rows_ref, turned_ref)
+        weave(scores(0), turns)
+        weave(scores(1), weights(0))
+
+    @pl.when(jnp.logical_and(step > 0, step < steps))
+    def _():
+        weave(scores(0), weights(1), outputs(0))
+        weave(scores(1), weights(0), outputs(1))
+
+    @pl.when(step == steps)
+    def _():
+        weave(weights(1), outputs(0))
+        weave(outputs(1))
 
 
 def attend(scalars, latent_queries, wvt, blocks, line, cache_rows, heads):
@@ -183,19 +253,24 @@
     routes = tuple(route for route, _ in blocks)
     keys = len(routes) * (tok_rows + cache_rows)
     cfg = (routes, line, cache_rows, tok_rows)
+    steps = all_heads // (2 * heads)
+    width = heads * tok_rows
     return pl.pallas_call(
-        functools.partial(attend_kernel, cfg, heads),
+        functools.partial(attend_kernel, cfg, heads, steps),
         out_shape=jax.ShapeDtypeStruct((tok_rows, all_heads * VDIM), BF),
-        grid=(all_heads // heads,),
+        grid=(steps + 1,),
         in_specs=[
             smem_spec(),
             smem_spec(),
-            pl.BlockSpec((PACKED, heads * tok_rows), lambda i: (i, 0)),
-            pl.BlockSpec((heads * VDIM, LATENT), lambda i: (i, 0)),
+            pl.BlockSpec((2 * PACKED, width), lambda i: (jnp.minimum(i, steps - 1), 0)),
+            pl.BlockSpec((2 * heads * VDIM, LATENT), lambda i: (jnp.maximum(i - 1, 0), 0)),
         ]
         + [vmem_spec()] * len(blocks),
-        out_specs=pl.BlockSpec((tok_rows, heads * VDIM), lambda i: (0, i)),
-        scratch_shapes=[pltpu.VMEM((keys, PACKED), BF), pltpu.VMEM((LATENT, keys), BF)],
+        out_specs=pl.BlockSpec((tok_rows, 2 * heads * VDIM), lambda i: (0, jnp.maximum(i - 1, 0))),
+        scratch_shapes=[pltpu.VMEM((keys, PACKED), BF), pltpu.VMEM((LATENT, keys), BF)]
+        + [pltpu.VMEM((keys, width), F32)] * 2
+        + [pltpu.VMEM((keys, width), BF)] * 2
+        + [pltpu.VMEM((8, width), F32)] * 4,
         compiler_params=pltpu.CompilerParams(vmem_limit_bytes=VMEM_BYTES),
         cost_estimate=pl.CostEstimate(
             flops=2 * keys * all_heads * tok_rows * (PACKED + LATENT),

time: 46 us -> 44.4 us (0.965)
  local copies, waits for them, and re-layouts: 1.41 us -> 0.01 us
  Pallas kernels: 33.4 us -> 32.1 us
  waiting for transfers between devices: 2.05 us -> 3.17 us
    pallas_call x1, Pallas kernels: 21.4 us -> 19.9 us  [attend(): pl.pallas_call(functools.partial(attend_kernel, cfg, heads, steps), out_s...]
    unnamed x6 -> x4, local copies, waits for them, and re-layouts: 1.41 us -> 0.01 us
    ppermute x7, waiting for transfers between devices: 2.05 us -> 3.17 us  [move(): return lax.ppermute(value, AXES, pairs)]
  transfers between devices with their start and end apart: 7 -> 7, of which waited for: 4 -> 4; matrix products, arithmetic and copies ran while one was open for 0% -> 0% of each run, Pallas kernels for 22% -> 24%
where the time goes in v9:
time: 44.4 us; the launch traced here: 44.1 us
  Pallas kernels  32.1 us (72%)
  starting transfers between devices  8.1 us (18%)
  waiting for transfers between devices  3.17 us (7%)
  between operations  0.67 us (2%)
    pallas_call x1, Pallas kernels, attend(): pl.pallas_call(functools.partial(attend_kernel, cfg, heads, steps), out_s...  19.9 us
    pallas_call x1, Pallas kernels, prepare(): pl.pallas_call(functools.partial(prepare_kernel, heads), out_shape=(jax.S...  10.4 us
    ppermute x7, starting transfers between devices, move(): return lax.ppermute(value, AXES, pairs)  8.1 us
    ppermute x7, waiting for transfers between devices, move(): return lax.ppermute(value, AXES, pairs)  3.17 us
    pallas_call x1, Pallas kernels, pack(): pl.pallas_call(pack_kernel, out_shape=jax.ShapeDtypeStruct((rows, 128), B...  1.81 us
  transfers between devices with their start and end apart: 7, of which 4 were waited for; matrix products, arithmetic and copies ran while one was open for 0% of the time, Pallas kernels for 24%

profile of v9, /device:TPU:0, one launch (start us, length us, event | category | flops | bytes accessed | tf_op | source)
XLA Modules:
  0.0 44.1 jit_solution(387856841038368591)
XLA Ops:
  0.0 1.8 %pack_rows.1.rest_0_ = bf16[656,128]{1,0:T(8,128)(2,1)} custom-call(bf16[576,128]{1,0:T(8,128)(2,1)} %bitcast.2, bf16[16,576]{1,0:T(8,128)(2,1)} %cache_ref.1, f32[1,512]{1,0:T(1,128)} %bitcast.3), custom_call_target="tpu_custom_call" | custom-call | tf_op jit(solution)/shard_map/pack_rows/pallas_call | solution.py:55
  1.8 0.0 copy-start
  1.8 0.0 copy-start.1
  1.8 5.0 %collective-permute-start.2 = (bf16[656,128]{1,0:T(8,128)(2,1)}, bf16[656,128]{1,0:T(8,128)(2,1)S(1)}, u32[]{:S(2)}, u32[]{:S(2)}) collective-permute-start(bf16[656,128]{1,0:T(8,128)(2,1)} %pack_rows.1.rest_0_), channel_id=1, source_target_pairs={{0,12},{1,15},{2,14},{3,13},{4,0},{5,3},{6,2},{7,1},{8,4},{9,7},{1... | collective-permute-start | bytes 503816 | tf_op jit(solution)/shard_map/ppermute | solution.py:294
  6.9 0.0 collective-permute-start.1
  6.9 1.0 %collective-permute-start = (bf16[656,128]{1,0:T(8,128)(2,1)}, bf16[656,128]{1,0:T(8,128)(2,1)S(1)}, u32[]{:S(2)}, u32[]{:S(2)}) collective-permute-start(bf16[656,128]{1,0:T(8,128)(2,1)} %pack_rows.1.rest_0_), channel_id=1, source_target_pairs={{0,4},{1,7},{2,6},{3,5},{4,8},{5,11},{6,10},{7,9},{8,12},{9,15},{1... | collective-permute-start | bytes 503816 | tf_op jit(solution)/shard_map/ppermute | solution.py:294
  7.9 1.5 %collective-permute-start.3 = (bf16[656,128]{1,0:T(8,128)(2,1)}, bf16[656,128]{1,0:T(8,128)(2,1)S(1)}, u32[]{:S(2)}, u32[]{:S(2)}) collective-permute-start(bf16[656,128]{1,0:T(8,128)(2,1)} %pack_rows.1.rest_0_), channel_id=1, source_target_pairs={{0,2},{1,3},{2,0},{3,1},{4,6},{5,7},{6,4},{7,5},{8,10},{9,11},{10,... | collective-permute-start | bytes 503816 | tf_op jit(solution)/shard_map/ppermute | solution.py:294
  9.4 10.4 %prepare.1 = (bf16[5120,512]{1,0:T(8,128)(2,1)}, bf16[4096,512]{1,0:T(8,128)(2,1)}) custom-call(bf16[128,6144]{1,0:T(8,128)(2,1)} %q_ref.1, bf16[512,4096]{1,0:T(8,128)(2,1)} %wk_ref.1, bf16[512,4096]{1,0:T(8,128)(2,1)} %wv_ref.1), custom_call_target="tpu_custom_call" | custom-call | flops 536870912 | bytes 16777216 | tf_op jit(solution)/shard_map/prepare/pallas_call | solution.py:94
  19.8 0.0 collective-permute-done.2.rest_4_
  19.8 2.4 %collective-permute-done.1.rest_3_ = bf16[656,128]{1,0:T(8,128)(2,1)S(1)} collective-permute-done((bf16[656,128]{1,0:T(8,128)(2,1)}, bf16[656,128]{1,0:T(8,128)(2,1)S(1)}, u32[]{:S(2)}, u32[]{:S(2)}) %collective-permute-start.1) | collective-permute-done | bytes 167968 | tf_op jit(solution)/shard_map/ppermute | solution.py:294
  22.3 0.0 collective-permute-done.rest_2_
  22.3 0.0 collective-permute-start.4
  22.3 0.5 %collective-permute-start.5 = (bf16[656,128]{1,0:T(8,128)(2,1)S(1)}, bf16[656,128]{1,0:T(8,128)(2,1)S(1)}, u32[]{:S(2)}, u32[]{:S(2)}) collective-permute-start(bf16[656,128]{1,0:T(8,128)(2,1)S(1)} %collective-permute-done.1.rest_3_), channel_id=1, source_target_pairs={{0,1},{1,0},{2,3},{3,2},{4,5},{5,4},{6,7},{7,6},{8,9},{9,8},{10,11... | collective-permute-start | bytes 503816 | tf_op jit(solution)/shard_map/ppermute | solution.py:294
  22.8 0.0 collective-permute-start.6
  23.4 0.0 collective-permute-done.3.rest_1_
  23.5 0.2 collective-permute-done.4.rest_5_
  23.7 0.2 collective-permute-done.5.rest_6_
  23.9 0.3 collective-permute-done.6.rest_7_
  24.2 0.0 copy-done
  24.2 0.0 copy-done.1
  24.2 19.9 %attend.1 = bf16[128,4096]{1,0:T(8,128)(2,1)} custom-call(s32[8]{0:T(128)S(1)} %copy-done.1, s32[1]{0:T(128)S(6)} %copy.9.prefix_ref, bf16[5120,512]{1,0:T(8,128)(2,1)} %get-tuple-element.14.latent_ref, bf16[4096,512]{1,0:T(8,128)(2,1)} %get-tuple-element.15.wvt_ref, bf16[656,128]{1,0:T(8,128)(2,1)S(1)} %copy-done, ...), custom_call_target="tpu_custom_call" | custom-call | flops 10871635968 | bytes 8388608 | tf_op jit(solution)/shard_map/attend/pallas_call | solution.py:258
Async XLA Ops:
  1.8 22.4 %copy-start = (bf16[656,128]{1,0:T(8,128)(2,1)S(1)}, bf16[656,128]{1,0:T(8,128)(2,1)}, u32[]{:S(2)}) copy-start(bf16[656,128]{1,0:T(8,128)(2,1)} %pack_rows.1.rest_0_) | copy-start | bytes 503812
  1.8 22.4 %copy-start.1 = (s32[8]{0:T(128)S(1)}, s32[8]{0:T(128)}, u32[]{:S(2)}) copy-start(s32[8]{0:T(128)} %order_ref.1) | copy-start | bytes 100
  1.8 18.0 %collective-permute-start.2 = (bf16[656,128]{1,0:T(8,128)(2,1)}, bf16[656,128]{1,0:T(8,128)(2,1)S(1)}, u32[]{:S(2)}, u32[]{:S(2)}) collective-permute-start(bf16[656,128]{1,0:T(8,128)(2,1)} %pack_rows.1.rest_0_), channel_id=1, source_target_pairs={{0,12},{1,15},{2,14},{3,13},{4,0},{5,3},{6,2},{7,1},{8,4},{9,7},{1... | collective-permute-start | bytes 503816 | tf_op jit(solution)/shard_map/ppermute | solution.py:294
  6.9 15.4 %collective-permute-start.1 = (bf16[656,128]{1,0:T(8,128)(2,1)}, bf16[656,128]{1,0:T(8,128)(2,1)S(1)}, u32[]{:S(2)}, u32[]{:S(2)}) collective-permute-start(bf16[656,128]{1,0:T(8,128)(2,1)} %pack_rows.1.rest_0_), channel_id=1, source_target_pairs={{0,8},{1,11},{2,10},{3,9},{4,12},{5,15},{6,14},{7,13},{8,0},{9,3},... | collective-permute-start | bytes 503816 | tf_op jit(solution)/shard_map/ppermute | solution.py:294
  6.9 15.4 %collective-permute-start = (bf16[656,128]{1,0:T(8,128)(2,1)}, bf16[656,128]{1,0:T(8,128)(2,1)S(1)}, u32[]{:S(2)}, u32[]{:S(2)}) collective-permute-start(bf16[656,128]{1,0:T(8,128)(2,1)} %pack_rows.1.rest_0_), channel_id=1, source_target_pairs={{0,4},{1,7},{2,6},{3,5},{4,8},{5,11},{6,10},{7,9},{8,12},{9,15},{1... | collective-permute-start | bytes 503816 | tf_op jit(solution)/shard_map/ppermute | solution.py:294
  7.9 15.6 %collective-permute-start.3 = (bf16[656,128]{1,0:T(8,128)(2,1)}, bf16[656,128]{1,0:T(8,128)(2,1)S(1)}, u32[]{:S(2)}, u32[]{:S(2)}) collective-permute-start(bf16[656,128]{1,0:T(8,128)(2,1)} %pack_rows.1.rest_0_), channel_id=1, source_target_pairs={{0,2},{1,3},{2,0},{3,1},{4,6},{5,7},{6,4},{7,5},{8,10},{9,11},{10,... | collective-permute-start | bytes 503816 | tf_op jit(solution)/shard_map/ppermute | solution.py:294
  22.3 1.4 %collective-permute-start.4 = (bf16[656,128]{1,0:T(8,128)(2,1)S(1)}, bf16[656,128]{1,0:T(8,128)(2,1)S(1)}, u32[]{:S(2)}, u32[]{:S(2)}) collective-permute-start(bf16[656,128]{1,0:T(8,128)(2,1)S(1)} %collective-permute-done.rest_2_), channel_id=1, source_target_pairs={{0,1},{1,0},{2,3},{3,2},{4,5},{5,4},{6,7},{7,6},{8,9},{9,8},{10,11... | collective-permute-start | bytes 503816 | tf_op jit(solution)/shard_map/ppermute | solution.py:294
  22.3 1.6 %collective-permute-start.5 = (bf16[656,128]{1,0:T(8,128)(2,1)S(1)}, bf16[656,128]{1,0:T(8,128)(2,1)S(1)}, u32[]{:S(2)}, u32[]{:S(2)}) collective-permute-start(bf16[656,128]{1,0:T(8,128)(2,1)S(1)} %collective-permute-done.1.rest_3_), channel_id=1, source_target_pairs={{0,1},{1,0},{2,3},{3,2},{4,5},{5,4},{6,7},{7,6},{8,9},{9,8},{10,11... | collective-permute-start | bytes 503816 | tf_op jit(solution)/shard_map/ppermute | solution.py:294
  22.8 1.4 %collective-permute-start.6 = (bf16[656,128]{1,0:T(8,128)(2,1)S(1)}, bf16[656,128]{1,0:T(8,128)(2,1)S(1)}, u32[]{:S(2)}, u32[]{:S(2)}) collective-permute-start(bf16[656,128]{1,0:T(8,128)(2,1)S(1)} %collective-permute-done.2.rest_4_), channel_id=1, source_target_pairs={{0,1},{1,0},{2,3},{3,2},{4,5},{5,4},{6,7},{7,6},{8,9},{9,8},{10,11... | collective-permute-start | bytes 503816 | tf_op jit(solution)/shard_map/ppermute | solution.py:294

commit v10 on v9

--- a/solution.py
+++ b/solution.py
@@ -172,7 +172,7 @@
     score_refs, weight_refs, peak_refs, total_refs = (scratch[at : at + 2] for at in (0, 2, 4, 6))
     keys = rows_ref.shape[0]
     width = heads * tok_rows
-    scale = math.log2(math.e) / math.sqrt(NOPE + ROPE)
+    scale = 1.0 / math.sqrt(NOPE + ROPE)
     step = pl.program_id(0)
     pieces = [slice(at, min(at + 256, keys)) for at in range(0, keys, 256)]
 
@@ -201,7 +201,7 @@
         def piece(index):
             here = pieces[index]
             peak = jnp.max(peak_refs[buffer][...], axis=0, keepdims=True)
-            exponent = jnp.exp2((score_refs[buffer][here, :] - peak) * scale)
+            exponent = jnp.exp((score_refs[buffer][here, :] - peak) * scale)
             total = jnp.sum(by_eights(exponent), axis=0)
             if index:
                 total = total + total_refs[buffer][...]
@@ -233,8 +233,9 @@
     @pl.when(step == 0)
     def _():
         turns = gather_rows(cfg, order_ref, prefix_ref, blocks, rows_ref, turned_ref)
-        weave(scores(0), turns)
-        weave(scores(1), weights(0))
+        cut = len(turns) // 3
+        weave(scores(0), turns[:cut])
+        weave(scores(1), weights(0), turns[cut:])
 
     @pl.when(jnp.logical_and(step > 0, step < steps))
     def _():

time: 44.4 us -> 45.1 us (1.016)
  Pallas kernels: 32.1 us -> 32.8 us
    pallas_call x1, Pallas kernels: 19.9 us -> 20.5 us  [attend(): pl.pallas_call(functools.partial(attend_kernel, cfg, heads, steps), out_s...]
  transfers between devices with their start and end apart: 7 -> 7, of which waited for: 4 -> 4; matrix products, arithmetic and copies ran while one was open for 0% -> 0% of each run, Pallas kernels for 24% -> 23%
where the time goes in v10:
time: 45.1 us; the launch traced here: 44.7 us
  Pallas kernels  32.8 us (73%)
  starting transfers between devices  8.1 us (18%)
  waiting for transfers between devices  3.17 us (7%)
  between operations  0.67 us (1%)
    pallas_call x1, Pallas kernels, attend(): pl.pallas_call(functools.partial(attend_kernel, cfg, heads, steps), out_s...  20.5 us
    pallas_call x1, Pallas kernels, prepare(): pl.pallas_call(functools.partial(prepare_kernel, heads), out_shape=(jax.S...  10.4 us
    ppermute x7, starting transfers between devices, move(): return lax.ppermute(value, AXES, pairs)  8.1 us
    ppermute x7, waiting for transfers between devices, move(): return lax.ppermute(value, AXES, pairs)  3.17 us
    pallas_call x1, Pallas kernels, pack(): pl.pallas_call(pack_kernel, out_shape=jax.ShapeDtypeStruct((rows, 128), B...  1.81 us
  transfers between devices with their start and end apart: 7, of which 4 were waited for; matrix products, arithmetic and copies ran while one was open for 0% of the time, Pallas kernels for 23%

profile of v10, /device:TPU:0, one launch (start us, length us, event | category | flops | bytes accessed | tf_op | source)
XLA Modules:
  0.0 44.7 jit_solution(8286814540096031211)
XLA Ops:
  0.0 1.8 %pack_rows.1.rest_0_ = bf16[656,128]{1,0:T(8,128)(2,1)} custom-call(bf16[576,128]{1,0:T(8,128)(2,1)} %bitcast.2, bf16[16,576]{1,0:T(8,128)(2,1)} %cache_ref.1, f32[1,512]{1,0:T(1,128)} %bitcast.3), custom_call_target="tpu_custom_call" | custom-call | tf_op jit(solution)/shard_map/pack_rows/pallas_call | solution.py:55
  1.8 0.0 copy-start
  1.8 0.0 copy-start.1
  1.8 5.0 %collective-permute-start.2 = (bf16[656,128]{1,0:T(8,128)(2,1)}, bf16[656,128]{1,0:T(8,128)(2,1)S(1)}, u32[]{:S(2)}, u32[]{:S(2)}) collective-permute-start(bf16[656,128]{1,0:T(8,128)(2,1)} %pack_rows.1.rest_0_), channel_id=1, source_target_pairs={{0,12},{1,15},{2,14},{3,13},{4,0},{5,3},{6,2},{7,1},{8,4},{9,7},{1... | collective-permute-start | bytes 503816 | tf_op jit(solution)/shard_map/ppermute | solution.py:295
  6.9 0.0 collective-permute-start.1
  6.9 1.0 %collective-permute-start = (bf16[656,128]{1,0:T(8,128)(2,1)}, bf16[656,128]{1,0:T(8,128)(2,1)S(1)}, u32[]{:S(2)}, u32[]{:S(2)}) collective-permute-start(bf16[656,128]{1,0:T(8,128)(2,1)} %pack_rows.1.rest_0_), channel_id=1, source_target_pairs={{0,4},{1,7},{2,6},{3,5},{4,8},{5,11},{6,10},{7,9},{8,12},{9,15},{1... | collective-permute-start | bytes 503816 | tf_op jit(solution)/shard_map/ppermute | solution.py:295
  7.9 1.5 %collective-permute-start.3 = (bf16[656,128]{1,0:T(8,128)(2,1)}, bf16[656,128]{1,0:T(8,128)(2,1)S(1)}, u32[]{:S(2)}, u32[]{:S(2)}) collective-permute-start(bf16[656,128]{1,0:T(8,128)(2,1)} %pack_rows.1.rest_0_), channel_id=1, source_target_pairs={{0,2},{1,3},{2,0},{3,1},{4,6},{5,7},{6,4},{7,5},{8,10},{9,11},{10,... | collective-permute-start | bytes 503816 | tf_op jit(solution)/shard_map/ppermute | solution.py:295
  9.4 10.4 %prepare.1 = (bf16[5120,512]{1,0:T(8,128)(2,1)}, bf16[4096,512]{1,0:T(8,128)(2,1)}) custom-call(bf16[128,6144]{1,0:T(8,128)(2,1)} %q_ref.1, bf16[512,4096]{1,0:T(8,128)(2,1)} %wk_ref.1, bf16[512,4096]{1,0:T(8,128)(2,1)} %wv_ref.1), custom_call_target="tpu_custom_call" | custom-call | flops 536870912 | bytes 16777216 | tf_op jit(solution)/shard_map/prepare/pallas_call | solution.py:94
  19.8 0.0 collective-permute-done.2.rest_4_
  19.8 2.4 %collective-permute-done.1.rest_3_ = bf16[656,128]{1,0:T(8,128)(2,1)S(1)} collective-permute-done((bf16[656,128]{1,0:T(8,128)(2,1)}, bf16[656,128]{1,0:T(8,128)(2,1)S(1)}, u32[]{:S(2)}, u32[]{:S(2)}) %collective-permute-start.1) | collective-permute-done | bytes 167968 | tf_op jit(solution)/shard_map/ppermute | solution.py:295
  22.3 0.0 collective-permute-done.rest_2_
  22.3 0.0 collective-permute-start.4
  22.3 0.5 %collective-permute-start.5 = (bf16[656,128]{1,0:T(8,128)(2,1)S(1)}, bf16[656,128]{1,0:T(8,128)(2,1)S(1)}, u32[]{:S(2)}, u32[]{:S(2)}) collective-permute-start(bf16[656,128]{1,0:T(8,128)(2,1)S(1)} %collective-permute-done.1.rest_3_), channel_id=1, source_target_pairs={{0,1},{1,0},{2,3},{3,2},{4,5},{5,4},{6,7},{7,6},{8,9},{9,8},{10,11... | collective-permute-start | bytes 503816 | tf_op jit(solution)/shard_map/ppermute | solution.py:295
  22.8 0.0 collective-permute-start.6
  23.4 0.0 collective-permute-done.3.rest_1_
  23.5 0.2 collective-permute-done.4.rest_5_
  23.7 0.2 collective-permute-done.5.rest_6_
  23.9 0.3 collective-permute-done.6.rest_7_
  24.2 0.0 copy-done
  24.2 0.0 copy-done.1
  24.2 20.5 %attend.1 = bf16[128,4096]{1,0:T(8,128)(2,1)} custom-call(s32[8]{0:T(128)S(1)} %copy-done.1, s32[1]{0:T(128)S(6)} %copy.9.prefix_ref, bf16[5120,512]{1,0:T(8,128)(2,1)} %get-tuple-element.14.latent_ref, bf16[4096,512]{1,0:T(8,128)(2,1)} %get-tuple-element.15.wvt_ref, bf16[656,128]{1,0:T(8,128)(2,1)S(1)} %copy-done, ...), custom_call_target="tpu_custom_call" | custom-call | flops 10871635968 | bytes 8388608 | tf_op jit(solution)/shard_map/attend/pallas_call | solution.py:259
Async XLA Ops:
  1.8 22.4 %copy-start = (bf16[656,128]{1,0:T(8,128)(2,1)S(1)}, bf16[656,128]{1,0:T(8,128)(2,1)}, u32[]{:S(2)}) copy-start(bf16[656,128]{1,0:T(8,128)(2,1)} %pack_rows.1.rest_0_) | copy-start | bytes 503812
  1.8 22.4 %copy-start.1 = (s32[8]{0:T(128)S(1)}, s32[8]{0:T(128)}, u32[]{:S(2)}) copy-start(s32[8]{0:T(128)} %order_ref.1) | copy-start | bytes 100
  1.8 18.0 %collective-permute-start.2 = (bf16[656,128]{1,0:T(8,128)(2,1)}, bf16[656,128]{1,0:T(8,128)(2,1)S(1)}, u32[]{:S(2)}, u32[]{:S(2)}) collective-permute-start(bf16[656,128]{1,0:T(8,128)(2,1)} %pack_rows.1.rest_0_), channel_id=1, source_target_pairs={{0,12},{1,15},{2,14},{3,13},{4,0},{5,3},{6,2},{7,1},{8,4},{9,7},{1... | collective-permute-start | bytes 503816 | tf_op jit(solution)/shard_map/ppermute | solution.py:295
  6.9 15.4 %collective-permute-start.1 = (bf16[656,128]{1,0:T(8,128)(2,1)}, bf16[656,128]{1,0:T(8,128)(2,1)S(1)}, u32[]{:S(2)}, u32[]{:S(2)}) collective-permute-start(bf16[656,128]{1,0:T(8,128)(2,1)} %pack_rows.1.rest_0_), channel_id=1, source_target_pairs={{0,8},{1,11},{2,10},{3,9},{4,12},{5,15},{6,14},{7,13},{8,0},{9,3},... | collective-permute-start | bytes 503816 | tf_op jit(solution)/shard_map/ppermute | solution.py:295
  6.9 15.4 %collective-permute-start = (bf16[656,128]{1,0:T(8,128)(2,1)}, bf16[656,128]{1,0:T(8,128)(2,1)S(1)}, u32[]{:S(2)}, u32[]{:S(2)}) collective-permute-start(bf16[656,128]{1,0:T(8,128)(2,1)} %pack_rows.1.rest_0_), channel_id=1, source_target_pairs={{0,4},{1,7},{2,6},{3,5},{4,8},{5,11},{6,10},{7,9},{8,12},{9,15},{1... | collective-permute-start | bytes 503816 | tf_op jit(solution)/shard_map/ppermute | solution.py:295
  7.9 15.6 %collective-permute-start.3 = (bf16[656,128]{1,0:T(8,128)(2,1)}, bf16[656,128]{1,0:T(8,128)(2,1)S(1)}, u32[]{:S(2)}, u32[]{:S(2)}) collective-permute-start(bf16[656,128]{1,0:T(8,128)(2,1)} %pack_rows.1.rest_0_), channel_id=1, source_target_pairs={{0,2},{1,3},{2,0},{3,1},{4,6},{5,7},{6,4},{7,5},{8,10},{9,11},{10,... | collective-permute-start | bytes 503816 | tf_op jit(solution)/shard_map/ppermute | solution.py:295
  22.3 1.4 %collective-permute-start.4 = (bf16[656,128]{1,0:T(8,128)(2,1)S(1)}, bf16[656,128]{1,0:T(8,128)(2,1)S(1)}, u32[]{:S(2)}, u32[]{:S(2)}) collective-permute-start(bf16[656,128]{1,0:T(8,128)(2,1)S(1)} %collective-permute-done.rest_2_), channel_id=1, source_target_pairs={{0,1},{1,0},{2,3},{3,2},{4,5},{5,4},{6,7},{7,6},{8,9},{9,8},{10,11... | collective-permute-start | bytes 503816 | tf_op jit(solution)/shard_map/ppermute | solution.py:295
  22.3 1.6 %collective-permute-start.5 = (bf16[656,128]{1,0:T(8,128)(2,1)S(1)}, bf16[656,128]{1,0:T(8,128)(2,1)S(1)}, u32[]{:S(2)}, u32[]{:S(2)}) collective-permute-start(bf16[656,128]{1,0:T(8,128)(2,1)S(1)} %collective-permute-done.1.rest_3_), channel_id=1, source_target_pairs={{0,1},{1,0},{2,3},{3,2},{4,5},{5,4},{6,7},{7,6},{8,9},{9,8},{10,11... | collective-permute-start | bytes 503816 | tf_op jit(solution)/shard_map/ppermute | solution.py:295
  22.8 1.4 %collective-permute-start.6 = (bf16[656,128]{1,0:T(8,128)(2,1)S(1)}, bf16[656,128]{1,0:T(8,128)(2,1)S(1)}, u32[]{:S(2)}, u32[]{:S(2)}) collective-permute-start(bf16[656,128]{1,0:T(8,128)(2,1)S(1)} %collective-permute-done.2.rest_4_), channel_id=1, source_target_pairs={{0,1},{1,0},{2,3},{3,2},{4,5},{5,4},{6,7},{7,6},{8,9},{9,8},{10,11... | collective-permute-start | bytes 503816 | tf_op jit(solution)/shard_map/ppermute | solution.py:295

commit v11 on v10

--- a/solution.py
+++ b/solution.py
@@ -12,7 +12,8 @@
 ROPE = 64
 NOPE = 128
 VDIM = 128
-PACKED = 640
+PACKED = 768
+ONES = 16
 QK = 256
 NEG = -1e30
 VMEM_BYTES = 50 * 1024 * 1024
@@ -44,8 +45,8 @@
     for tile in range(tiles):
         out_ref[at : at + cache_rows, :] = cache_ref[:, tile * 128 : (tile + 1) * 128]
         at += cache_rows
-    out_ref[at:, :] = jnp.zeros((cache_rows, 128), BF)
     out_ref[at:, :ROPE] = cache_ref[:, LATENT:]
+    out_ref[at:, ROPE:] = cache_ref[:, LATENT:]
 
 
 def pack(span_latents, cache_latents, gain):
@@ -73,17 +74,22 @@
 
 
 def prepare_kernel(heads, q_ref, wk_ref, wv_ref, latent_ref, wvt_ref):
+    scale = math.log2(math.e) / math.sqrt(NOPE + ROPE)
     rows = q_ref.shape[0]
     turned = q_ref[...].T
-    ids = lax.broadcasted_iota(jnp.int32, (PACKED - LATENT - ROPE, rows), 0)
+    ids = lax.broadcasted_iota(jnp.int32, (PACKED - LATENT - 2 * ROPE, rows), 0)
     flags = jnp.where(ids == 0, NEG, 0.0).astype(BF)
     for head in range(heads):
         at = head * (NOPE + ROPE)
         here = slice(head * rows, (head + 1) * rows)
         wk = wk_ref[:, head * NOPE : (head + 1) * NOPE]
-        latent_ref[:LATENT, here] = jnp.dot(wk, turned[at : at + NOPE], preferred_element_type=F32).astype(BF)
-        latent_ref[LATENT : LATENT + ROPE, here] = turned[at + NOPE : at + NOPE + ROPE]
-        latent_ref[LATENT + ROPE :, here] = flags
+        latent = jnp.dot(wk, turned[at : at + NOPE], preferred_element_type=F32)
+        latent_ref[:LATENT, here] = (latent * scale).astype(BF)
+        rotary = turned[at + NOPE : at + NOPE + ROPE].astype(F32) * scale
+        rounded = rotary.astype(BF)
+        latent_ref[LATENT : LATENT + ROPE, here] = rounded
+        latent_ref[LATENT + ROPE : LATENT + 2 * ROPE, here] = (rotary - rounded.astype(F32)).astype(BF)
+        latent_ref[LATENT + 2 * ROPE :, here] = flags
     wvt_ref[...] = wv_ref[...].T
 
 
@@ -122,9 +128,9 @@
     core = lax.axis_index("head")
     place = lax.div(me, 2)
     side = lax.rem(me, 2)
-    lanes = lax.broadcasted_iota(jnp.int32, (tok_rows, ROPE), 1)
+    lanes = lax.broadcasted_iota(jnp.int32, (tok_rows, 128), 1)
     slots = lax.broadcasted_iota(jnp.int32, (cache_rows, 128), 0)
-    flag_lane = lax.broadcasted_iota(jnp.int32, (cache_rows, 128), 1) == ROPE
+    flag_lane = lax.broadcasted_iota(jnp.int32, (cache_rows, 128), 1) == 0
     base = tiles * tok_rows + ROPE
     for slot, route in enumerate(routes):
         block = blocks[slot]
@@ -135,21 +141,23 @@
         source = origin(route, place, side, core, line)
         hidden = jnp.where(order_ref[source] > order_ref[me], 1.0, 0.0)
         flags = jnp.where(lanes == 0, hidden, 0.0)
-        rotary = block[tiles * tok_rows : base, :].astype(F32).T
-        rows_ref[to, LATENT:] = jnp.concatenate([rotary, flags], axis=1).astype(BF)
+        rotary = block[tiles * tok_rows : base, :]
+        rows_ref[to, LATENT : LATENT + 128] = jnp.concatenate([rotary, rotary], axis=0).T
+        rows_ref[to, LATENT + 128 :] = flags.astype(BF)
         at = len(routes) * tok_rows + slot * cache_rows
         to = slice(at, at + cache_rows)
         for tile in range(tiles):
             begin = base + tile * cache_rows
             rows_ref[to, tile * 128 : (tile + 1) * 128] = block[begin : begin + cache_rows, :]
         unused = jnp.logical_and(flag_lane, slots + source * cache_rows >= prefix_ref[0])
-        rotary = block[base + tiles * cache_rows :, :].astype(F32)
-        rows_ref[to, LATENT:] = jnp.where(unused, 1.0, rotary).astype(BF)
+        rows_ref[to, LATENT : LATENT + 128] = block[base + tiles * cache_rows :, :]
+        rows_ref[to, LATENT + 128 :] = jnp.where(unused, 1.0, 0.0).astype(BF)
 
     def turn(here):
-        turned_ref[:, here] = rows_ref[here, :LATENT].T
+        turned_ref[:LATENT, here] = rows_ref[here, :LATENT].T
 
     total = rows_ref.shape[0]
+    turned_ref[LATENT:, :] = jnp.ones((ONES, total), BF)
     return [functools.partial(turn, slice(at, at + 128)) for at in range(0, total, 128)]
 
 
@@ -169,10 +177,9 @@
     blocks = rest[: len(routes)]
     out_ref, rows_ref, turned_ref = rest[len(routes) : len(routes) + 3]
     scratch = rest[len(routes) + 3 :]
-    score_refs, weight_refs, peak_refs, total_refs = (scratch[at : at + 2] for at in (0, 2, 4, 6))
+    score_refs, weight_refs, peak_refs = (scratch[at : at + 2] for at in (0, 2, 4))
     keys = rows_ref.shape[0]
     width = heads * tok_rows
-    scale = 1.0 / math.sqrt(NOPE + ROPE)
     step = pl.program_id(0)
     pieces = [slice(at, min(at + 256, keys)) for at in range(0, keys, 256)]
 
@@ -201,25 +208,25 @@
         def piece(index):
             here = pieces[index]
             peak = jnp.max(peak_refs[buffer][...], axis=0, keepdims=True)
-            exponent = jnp.exp((score_refs[buffer][here, :] - peak) * scale)
-            total = jnp.sum(by_eights(exponent), axis=0)
-            if index:
-                total = total + total_refs[buffer][...]
-            total_refs[buffer][...] = total
-            weight_refs[buffer][here, :] = exponent.astype(BF)
+            weight_refs[buffer][here, :] = jnp.exp2(score_refs[buffer][here, :] - peak).astype(BF)
 
         return [functools.partial(piece, index) for index in range(len(pieces))]
 
     def outputs(buffer):
-        total = jnp.sum(total_refs[buffer][...], axis=0, keepdims=True)
         parts = []
+        totals = []
 
         def mix(index):
-            here = slice(index * 256, (index + 1) * 256)
+            first = index * 256
+            final = index == LATENT // 256 - 1
+            here = slice(first, LATENT + ONES if final else first + 256)
             mixed = jnp.dot(turned_ref[here, :], weight_refs[buffer][...], preferred_element_type=F32)
-            parts.append(mixed.astype(BF))
+            parts.append(mixed[:256].astype(BF))
+            if final:
+                totals.append(mixed[256:257])
 
         def finish():
+            total = totals[0]
             mixed = jnp.concatenate(parts, axis=0)
             for head in range(heads):
                 here = slice(head * tok_rows, (head + 1) * tok_rows)
@@ -268,10 +275,10 @@
         ]
         + [vmem_spec()] * len(blocks),
         out_specs=pl.BlockSpec((tok_rows, 2 * heads * VDIM), lambda i: (0, jnp.maximum(i - 1, 0))),
-        scratch_shapes=[pltpu.VMEM((keys, PACKED), BF), pltpu.VMEM((LATENT, keys), BF)]
+        scratch_shapes=[pltpu.VMEM((keys, PACKED), BF), pltpu.VMEM((LATENT + ONES, keys), BF)]
         + [pltpu.VMEM((keys, width), F32)] * 2
         + [pltpu.VMEM((keys, width), BF)] * 2
-        + [pltpu.VMEM((8, width), F32)] * 4,
+        + [pltpu.VMEM((8, width), F32)] * 2,
         compiler_params=pltpu.CompilerParams(vmem_limit_bytes=VMEM_BYTES),
         cost_estimate=pl.CostEstimate(
             flops=2 * keys * all_heads * tok_rows * (PACKED + LATENT),

time: 45.1 us -> 44 us (0.976)
  Pallas kernels: 32.8 us -> 32 us
    pallas_call x1, Pallas kernels: 20.5 us -> 19.4 us  [attend(): pl.pallas_call(functools.partial(attend_kernel, cfg, heads, steps), out_s...]
  transfers between devices with their start and end apart: 7 -> 7, of which waited for: 4 -> 4; matrix products, arithmetic and copies ran while one was open for 0% -> 0% of each run, Pallas kernels for 23% -> 25%
where the time goes in v11:
time: 44 us; the launch traced here: 43.6 us
  Pallas kernels  32 us (73%)
  starting transfers between devices  8.1 us (18%)
  waiting for transfers between devices  2.83 us (6%)
  between operations  0.67 us (2%)
    pallas_call x1, Pallas kernels, attend(): pl.pallas_call(functools.partial(attend_kernel, cfg, heads, steps), out_s...  19.4 us
    pallas_call x1, Pallas kernels, prepare(): pl.pallas_call(functools.partial(prepare_kernel, heads), out_shape=(jax.S...  10.8 us
    ppermute x7, starting transfers between devices, move(): return lax.ppermute(value, AXES, pairs)  8.1 us
    ppermute x7, waiting for transfers between devices, move(): return lax.ppermute(value, AXES, pairs)  2.83 us
    pallas_call x1, Pallas kernels, pack(): pl.pallas_call(pack_kernel, out_shape=jax.ShapeDtypeStruct((rows, 128), B...  1.83 us
  transfers between devices with their start and end apart: 7, of which 4 were waited for; matrix products, arithmetic and copies ran while one was open for 0% of the time, Pallas kernels for 25%

profile of v11, /device:TPU:0, one launch (start us, length us, event | category | flops | bytes accessed | tf_op | source)
XLA Modules:
  0.0 43.6 jit_solution(7799318097263225048)
XLA Ops:
  0.0 1.8 %pack_rows.1.rest_0_ = bf16[656,128]{1,0:T(8,128)(2,1)} custom-call(bf16[576,128]{1,0:T(8,128)(2,1)} %bitcast.2, bf16[16,576]{1,0:T(8,128)(2,1)} %cache_ref.1, f32[1,512]{1,0:T(1,128)} %bitcast.3), custom_call_target="tpu_custom_call" | custom-call | tf_op jit(solution)/shard_map/pack_rows/pallas_call | solution.py:56
  1.8 0.0 copy-start
  1.8 0.0 copy-start.1
  1.8 5.0 %collective-permute-start.2 = (bf16[656,128]{1,0:T(8,128)(2,1)}, bf16[656,128]{1,0:T(8,128)(2,1)S(1)}, u32[]{:S(2)}, u32[]{:S(2)}) collective-permute-start(bf16[656,128]{1,0:T(8,128)(2,1)} %pack_rows.1.rest_0_), channel_id=1, source_target_pairs={{0,12},{1,15},{2,14},{3,13},{4,0},{5,3},{6,2},{7,1},{8,4},{9,7},{1... | collective-permute-start | bytes 503816 | tf_op jit(solution)/shard_map/ppermute | solution.py:302
  6.9 0.0 collective-permute-start.1
  6.9 1.0 %collective-permute-start = (bf16[656,128]{1,0:T(8,128)(2,1)}, bf16[656,128]{1,0:T(8,128)(2,1)S(1)}, u32[]{:S(2)}, u32[]{:S(2)}) collective-permute-start(bf16[656,128]{1,0:T(8,128)(2,1)} %pack_rows.1.rest_0_), channel_id=1, source_target_pairs={{0,4},{1,7},{2,6},{3,5},{4,8},{5,11},{6,10},{7,9},{8,12},{9,15},{1... | collective-permute-start | bytes 503816 | tf_op jit(solution)/shard_map/ppermute | solution.py:302
  7.9 1.5 %collective-permute-start.3 = (bf16[656,128]{1,0:T(8,128)(2,1)}, bf16[656,128]{1,0:T(8,128)(2,1)S(1)}, u32[]{:S(2)}, u32[]{:S(2)}) collective-permute-start(bf16[656,128]{1,0:T(8,128)(2,1)} %pack_rows.1.rest_0_), channel_id=1, source_target_pairs={{0,2},{1,3},{2,0},{3,1},{4,6},{5,7},{6,4},{7,5},{8,10},{9,11},{10,... | collective-permute-start | bytes 503816 | tf_op jit(solution)/shard_map/ppermute | solution.py:302
  9.4 10.8 %prepare.1 = (bf16[6144,512]{1,0:T(8,128)(2,1)}, bf16[4096,512]{1,0:T(8,128)(2,1)}) custom-call(bf16[128,6144]{1,0:T(8,128)(2,1)} %q_ref.1, bf16[512,4096]{1,0:T(8,128)(2,1)} %wk_ref.1, bf16[512,4096]{1,0:T(8,128)(2,1)} %wv_ref.1), custom_call_target="tpu_custom_call" | custom-call | flops 536870912 | bytes 16777216 | tf_op jit(solution)/shard_map/prepare/pallas_call | solution.py:100
  20.2 0.0 collective-permute-done.2.rest_4_
  20.2 2.1 %collective-permute-done.1.rest_3_ = bf16[656,128]{1,0:T(8,128)(2,1)S(1)} collective-permute-done((bf16[656,128]{1,0:T(8,128)(2,1)}, bf16[656,128]{1,0:T(8,128)(2,1)S(1)}, u32[]{:S(2)}, u32[]{:S(2)}) %collective-permute-start.1) | collective-permute-done | bytes 167968 | tf_op jit(solution)/shard_map/ppermute | solution.py:302
  22.3 0.0 collective-permute-done.rest_2_
  22.3 0.0 collective-permute-start.4
  22.3 0.5 %collective-permute-start.5 = (bf16[656,128]{1,0:T(8,128)(2,1)S(1)}, bf16[656,128]{1,0:T(8,128)(2,1)S(1)}, u32[]{:S(2)}, u32[]{:S(2)}) collective-permute-start(bf16[656,128]{1,0:T(8,128)(2,1)S(1)} %collective-permute-done.1.rest_3_), channel_id=1, source_target_pairs={{0,1},{1,0},{2,3},{3,2},{4,5},{5,4},{6,7},{7,6},{8,9},{9,8},{10,11... | collective-permute-start | bytes 503816 | tf_op jit(solution)/shard_map/ppermute | solution.py:302
  22.8 0.0 collective-permute-start.6
  23.5 0.0 collective-permute-done.3.rest_1_
  23.5 0.2 collective-permute-done.4.rest_5_
  23.7 0.2 collective-permute-done.5.rest_6_
  23.9 0.3 collective-permute-done.6.rest_7_
  24.2 0.0 copy-done
  24.2 0.0 copy-done.1
  24.2 19.4 %attend.1 = bf16[128,4096]{1,0:T(8,128)(2,1)} custom-call(s32[8]{0:T(128)S(1)} %copy-done.1, s32[1]{0:T(128)S(6)} %copy.9.prefix_ref, bf16[6144,512]{1,0:T(8,128)(2,1)} %get-tuple-element.14.latent_ref, bf16[4096,512]{1,0:T(8,128)(2,1)} %get-tuple-element.15.wvt_ref, bf16[656,128]{1,0:T(8,128)(2,1)S(1)} %copy-done, ...), custom_call_target="tpu_custom_call" | custom-call | flops 12079595520 | bytes 8388608 | tf_op jit(solution)/shard_map/attend/pallas_call | solution.py:266
Async XLA Ops:
  1.8 22.4 %copy-start = (bf16[656,128]{1,0:T(8,128)(2,1)S(1)}, bf16[656,128]{1,0:T(8,128)(2,1)}, u32[]{:S(2)}) copy-start(bf16[656,128]{1,0:T(8,128)(2,1)} %pack_rows.1.rest_0_) | copy-start | bytes 503812
  1.8 22.4 %copy-start.1 = (s32[8]{0:T(128)S(1)}, s32[8]{0:T(128)}, u32[]{:S(2)}) copy-start(s32[8]{0:T(128)} %order_ref.1) | copy-start | bytes 100
  1.8 18.4 %collective-permute-start.2 = (bf16[656,128]{1,0:T(8,128)(2,1)}, bf16[656,128]{1,0:T(8,128)(2,1)S(1)}, u32[]{:S(2)}, u32[]{:S(2)}) collective-permute-start(bf16[656,128]{1,0:T(8,128)(2,1)} %pack_rows.1.rest_0_), channel_id=1, source_target_pairs={{0,12},{1,15},{2,14},{3,13},{4,0},{5,3},{6,2},{7,1},{8,4},{9,7},{1... | collective-permute-start | bytes 503816 | tf_op jit(solution)/shard_map/ppermute | solution.py:302
  6.9 15.4 %collective-permute-start.1 = (bf16[656,128]{1,0:T(8,128)(2,1)}, bf16[656,128]{1,0:T(8,128)(2,1)S(1)}, u32[]{:S(2)}, u32[]{:S(2)}) collective-permute-start(bf16[656,128]{1,0:T(8,128)(2,1)} %pack_rows.1.rest_0_), channel_id=1, source_target_pairs={{0,8},{1,11},{2,10},{3,9},{4,12},{5,15},{6,14},{7,13},{8,0},{9,3},... | collective-permute-start | bytes 503816 | tf_op jit(solution)/shard_map/ppermute | solution.py:302
  6.9 15.4 %collective-permute-start = (bf16[656,128]{1,0:T(8,128)(2,1)}, bf16[656,128]{1,0:T(8,128)(2,1)S(1)}, u32[]{:S(2)}, u32[]{:S(2)}) collective-permute-start(bf16[656,128]{1,0:T(8,128)(2,1)} %pack_rows.1.rest_0_), channel_id=1, source_target_pairs={{0,4},{1,7},{2,6},{3,5},{4,8},{5,11},{6,10},{7,9},{8,12},{9,15},{1... | collective-permute-start | bytes 503816 | tf_op jit(solution)/shard_map/ppermute | solution.py:302
  7.9 15.6 %collective-permute-start.3 = (bf16[656,128]{1,0:T(8,128)(2,1)}, bf16[656,128]{1,0:T(8,128)(2,1)S(1)}, u32[]{:S(2)}, u32[]{:S(2)}) collective-permute-start(bf16[656,128]{1,0:T(8,128)(2,1)} %pack_rows.1.rest_0_), channel_id=1, source_target_pairs={{0,2},{1,3},{2,0},{3,1},{4,6},{5,7},{6,4},{7,5},{8,10},{9,11},{10,... | collective-permute-start | bytes 503816 | tf_op jit(solution)/shard_map/ppermute | solution.py:302
  22.3 1.4 %collective-permute-start.4 = (bf16[656,128]{1,0:T(8,128)(2,1)S(1)}, bf16[656,128]{1,0:T(8,128)(2,1)S(1)}, u32[]{:S(2)}, u32[]{:S(2)}) collective-permute-start(bf16[656,128]{1,0:T(8,128)(2,1)S(1)} %collective-permute-done.rest_2_), channel_id=1, source_target_pairs={{0,1},{1,0},{2,3},{3,2},{4,5},{5,4},{6,7},{7,6},{8,9},{9,8},{10,11... | collective-permute-start | bytes 503816 | tf_op jit(solution)/shard_map/ppermute | solution.py:302
  22.3 1.6 %collective-permute-start.5 = (bf16[656,128]{1,0:T(8,128)(2,1)S(1)}, bf16[656,128]{1,0:T(8,128)(2,1)S(1)}, u32[]{:S(2)}, u32[]{:S(2)}) collective-permute-start(bf16[656,128]{1,0:T(8,128)(2,1)S(1)} %collective-permute-done.1.rest_3_), channel_id=1, source_target_pairs={{0,1},{1,0},{2,3},{3,2},{4,5},{5,4},{6,7},{7,6},{8,9},{9,8},{10,11... | collective-permute-start | bytes 503816 | tf_op jit(solution)/shard_map/ppermute | solution.py:302
  22.8 1.4 %collective-permute-start.6 = (bf16[656,128]{1,0:T(8,128)(2,1)S(1)}, bf16[656,128]{1,0:T(8,128)(2,1)S(1)}, u32[]{:S(2)}, u32[]{:S(2)}) collective-permute-start(bf16[656,128]{1,0:T(8,128)(2,1)S(1)} %collective-permute-done.2.rest_4_), channel_id=1, source_target_pairs={{0,1},{1,0},{2,3},{3,2},{4,5},{5,4},{6,7},{7,6},{8,9},{9,8},{10,11... | collective-permute-start | bytes 503816 | tf_op jit(solution)/shard_map/ppermute | solution.py:302

commit v12 on v11

--- a/solution.py
+++ b/solution.py
@@ -73,7 +73,7 @@
     return came * 2 + lane_side
 
 
-def prepare_kernel(heads, q_ref, wk_ref, wv_ref, latent_ref, wvt_ref):
+def prepare_kernel(heads, q_ref, wk_ref, latent_ref):
     scale = math.log2(math.e) / math.sqrt(NOPE + ROPE)
     rows = q_ref.shape[0]
     turned = q_ref[...].T
@@ -90,35 +90,27 @@
         latent_ref[LATENT : LATENT + ROPE, here] = rounded
         latent_ref[LATENT + ROPE : LATENT + 2 * ROPE, here] = (rotary - rounded.astype(F32)).astype(BF)
         latent_ref[LATENT + 2 * ROPE :, here] = flags
-    wvt_ref[...] = wv_ref[...].T
-
-
-def prepare(queries, key_weight, value_weight, heads):
+
+
+def prepare(queries, key_weight, heads):
     rows = queries.shape[0]
     depth, width = key_weight.shape
     steps = width // (heads * NOPE)
     return pl.pallas_call(
         functools.partial(prepare_kernel, heads),
-        out_shape=(
-            jax.ShapeDtypeStruct((steps * PACKED, heads * rows), BF),
-            jax.ShapeDtypeStruct((steps * heads * VDIM, depth), BF),
-        ),
+        out_shape=jax.ShapeDtypeStruct((steps * PACKED, heads * rows), BF),
         grid=(steps,),
         in_specs=[
             pl.BlockSpec((rows, heads * (NOPE + ROPE)), lambda i: (0, i)),
             pl.BlockSpec((depth, heads * NOPE), lambda i: (0, i)),
-            pl.BlockSpec((depth, heads * VDIM), lambda i: (0, i)),
         ],
-        out_specs=(
-            pl.BlockSpec((PACKED, heads * rows), lambda i: (i, 0)),
-            pl.BlockSpec((heads * VDIM, depth), lambda i: (i, 0)),
-        ),
+        out_specs=pl.BlockSpec((PACKED, heads * rows), lambda i: (i, 0)),
         compiler_params=pltpu.CompilerParams(vmem_limit_bytes=58 * 1024 * 1024),
         cost_estimate=pl.CostEstimate(
             flops=2 * rows * depth * width, bytes_accessed=depth * width * 8, transcendentals=0
         ),
         name="prepare",
-    )(queries, key_weight, value_weight)
+    )(queries, key_weight)
 
 
 def gather_rows(cfg, order_ref, prefix_ref, blocks, rows_ref, turned_ref):
@@ -132,8 +124,8 @@
     slots = lax.broadcasted_iota(jnp.int32, (cache_rows, 128), 0)
     flag_lane = lax.broadcasted_iota(jnp.int32, (cache_rows, 128), 1) == 0
     base = tiles * tok_rows + ROPE
-    for slot, route in enumerate(routes):
-        block = blocks[slot]
+
+    def take(slot, route, block):
         to = slice(slot * tok_rows, (slot + 1) * tok_rows)
         for tile in range(tiles):
             part = block[tile * tok_rows : (tile + 1) * tok_rows, :]
@@ -153,6 +145,13 @@
         rows_ref[to, LATENT : LATENT + 128] = block[base + tiles * cache_rows :, :]
         rows_ref[to, LATENT + 128 :] = jnp.where(unused, 1.0, 0.0).astype(BF)
 
+    for slot, route in enumerate(routes):
+        if len(blocks[slot]) == 1:
+            take(slot, route, blocks[slot][0])
+        else:
+            for which in range(2):
+                pl.when(core == which)(functools.partial(take, slot, route, blocks[slot][which]))
+
     def turn(here):
         turned_ref[:LATENT, here] = rows_ref[here, :LATENT].T
 
@@ -171,13 +170,17 @@
                 done[index] += 1
 
 
-def attend_kernel(cfg, heads, steps, order_ref, prefix_ref, latent_ref, wvt_ref, *rest):
+def attend_kernel(cfg, heads, steps, counts, order_ref, prefix_ref, latent_ref, wv_ref, *rest):
     routes = cfg[0]
     tok_rows = cfg[3]
-    blocks = rest[: len(routes)]
-    out_ref, rows_ref, turned_ref = rest[len(routes) : len(routes) + 3]
-    scratch = rest[len(routes) + 3 :]
+    blocks = []
+    for count in counts:
+        blocks.append(rest[:count])
+        rest = rest[count:]
+    out_ref, rows_ref, turned_ref = rest[:3]
+    scratch = rest[3:]
     score_refs, weight_refs, peak_refs = (scratch[at : at + 2] for at in (0, 2, 4))
+    wvt_refs = scratch[6:8]
     keys = rows_ref.shape[0]
     width = heads * tok_rows
     step = pl.program_id(0)
@@ -225,17 +228,24 @@
             if final:
                 totals.append(mixed[256:257])
 
+        def turn(head):
+            place = buffer * heads + head
+            to = slice(head * VDIM, (head + 1) * VDIM)
+            wvt_refs[buffer][to, :] = wv_ref[:, place * VDIM : (place + 1) * VDIM].T
+
         def finish():
             total = totals[0]
             mixed = jnp.concatenate(parts, axis=0)
             for head in range(heads):
                 here = slice(head * tok_rows, (head + 1) * tok_rows)
                 place = buffer * heads + head
-                wvt = wvt_ref[place * VDIM : (place + 1) * VDIM, :]
+                wvt = wvt_refs[buffer][head * VDIM : (head + 1) * VDIM, :]
                 out = jnp.dot(wvt, mixed[:, here], preferred_element_type=F32) / total[:, here]
                 out_ref[:, place * VDIM : (place + 1) * VDIM] = out.astype(BF).T
 
-        return [functools.partial(mix, index) for index in range(LATENT // 256)] + [finish]
+        turns = [functools.partial(turn, head) for head in range(heads)]
+        mixes = [functools.partial(mix, index) for index in range(LATENT // 256)]
+        return turns[: heads // 2] + mixes[:-1] + turns[heads // 2 :] + [mixes[-1], finish]
 
     @pl.when(step == 0)
     def _():
@@ -255,30 +265,31 @@
         weave(outputs(1))
 
 
-def attend(scalars, latent_queries, wvt, blocks, line, cache_rows, heads):
+def attend(scalars, latent_queries, wv, blocks, line, cache_rows, heads):
     tok_rows = latent_queries.shape[1] // heads
-    all_heads = wvt.shape[0] // VDIM
+    all_heads = wv.shape[1] // VDIM
     routes = tuple(route for route, _ in blocks)
     keys = len(routes) * (tok_rows + cache_rows)
     cfg = (routes, line, cache_rows, tok_rows)
     steps = all_heads // (2 * heads)
     width = heads * tok_rows
     return pl.pallas_call(
-        functools.partial(attend_kernel, cfg, heads, steps),
+        functools.partial(attend_kernel, cfg, heads, steps, tuple(len(x) for _, x in blocks)),
         out_shape=jax.ShapeDtypeStruct((tok_rows, all_heads * VDIM), BF),
         grid=(steps + 1,),
         in_specs=[
             smem_spec(),
             smem_spec(),
             pl.BlockSpec((2 * PACKED, width), lambda i: (jnp.minimum(i, steps - 1), 0)),
-            pl.BlockSpec((2 * heads * VDIM, LATENT), lambda i: (jnp.maximum(i - 1, 0), 0)),
+            pl.BlockSpec((LATENT, 2 * heads * VDIM), lambda i: (0, jnp.maximum(i - 1, 0))),
         ]
-        + [vmem_spec()] * len(blocks),
+        + [vmem_spec()] * sum(len(x) for _, x in blocks),
         out_specs=pl.BlockSpec((tok_rows, 2 * heads * VDIM), lambda i: (0, jnp.maximum(i - 1, 0))),
         scratch_shapes=[pltpu.VMEM((keys, PACKED), BF), pltpu.VMEM((LATENT + ONES, keys), BF)]
         + [pltpu.VMEM((keys, width), F32)] * 2
         + [pltpu.VMEM((keys, width), BF)] * 2
-        + [pltpu.VMEM((8, width), F32)] * 2,
+        + [pltpu.VMEM((8, width), F32)] * 2
+        + [pltpu.VMEM((heads * VDIM, LATENT), BF)] * 2,
         compiler_params=pltpu.CompilerParams(vmem_limit_bytes=VMEM_BYTES),
         cost_estimate=pl.CostEstimate(
             flops=2 * keys * all_heads * tok_rows * (PACKED + LATENT),
@@ -286,7 +297,7 @@
             transcendentals=keys * tok_rows * all_heads,
         ),
         name="attend",
-    )(*scalars, latent_queries, wvt, *[x for _, x in blocks])
+    )(*scalars, latent_queries, wv, *[x for _, group in blocks for x in group])
 
 
 def mover(line):
@@ -319,15 +330,25 @@
     move = mover(line)
     own = pack(span_latents, cache_latents, latent_gain)
     heads = 4 if line <= 8 else 2
+    half = line // 2
+
+    def swap(value):
+        return move(value, lambda p, s, c: (p, s, 1 - c))
+
     across = move(own, lambda p, s, c: (p, 1 - s, c))
-    along = [move(own, lambda p, s, c, k=k: (p + k, s ^ c, c)) for k in range(1, line)]
-    latent_queries, wvt = prepare(queries, key_weight, value_weight, heads)
-    along, latent_queries, wvt = lax.optimization_barrier((along, latent_queries, wvt))
-    swapped = [move(a, lambda p, s, c: (p, s, 1 - c)) for a in along]
-    blocks = [(("own", 0), own), (("across", 0), across)]
-    blocks += [(("along", k + 1), a) for k, a in enumerate(along)]
-    blocks += [(("swapped", k + 1), w) for k, w in enumerate(swapped)]
-    return attend((block_order, prefix_length), latent_queries, wvt, blocks, line, cache_rows, heads)
+    along = [move(own, lambda p, s, c, k=k: (p + k, s ^ c, c)) for k in range(1, line) if k != half]
+    far = move(own, lambda p, s, c: (p + half * (1 - c), s, c))
+    latent_queries = prepare(queries, key_weight, heads)
+    across, along, far, latent_queries = lax.optimization_barrier((across, along, far, latent_queries))
+    crossed = move(far, lambda p, s, c: (p, s, 0) if c else (p, 1 - s, 1))
+    swapped = [swap(a) for a in along]
+    shared = swap(far)
+    steps = [k for k in range(1, line) if k != half]
+    blocks = [(("own", 0), (own,)), (("across", 0), (across,))]
+    blocks += [(("along", k), (a,)) for k, a in zip(steps, along)]
+    blocks += [(("swapped", k), (w,)) for k, w in zip(steps, swapped)]
+    blocks += [(("along", half), (far, crossed)), (("swapped", half), (swap(crossed), shared))]
+    return attend((block_order, prefix_length), latent_queries, value_weight, blocks, line, cache_rows, heads)
 
 
 def solution(mesh):

time: 44 us -> 45.2 us (1.027)
  starting transfers between devices: 8.1 us -> 11.5 us
  Pallas kernels: 32 us -> 30.3 us
  waiting for transfers between devices: 2.83 us -> 2.23 us
    ppermute x7 -> x9, starting transfers between devices: 8.1 us -> 11.5 us  [move(): return lax.ppermute(value, AXES, pairs)]
    pallas_call x2, Pallas kernels: 30.2 us -> 28.5 us  [the longest x1 19.5 us: attend(): pl.pallas_call(functools.partial(attend_kernel, cfg, heads, steps, tuple(...]
    ppermute x7 -> x9, waiting for transfers between devices: 2.83 us -> 2.23 us  [move(): return lax.ppermute(value, AXES, pairs)]
  transfers between devices with their start and end apart: 7 -> 9, of which waited for: 4 -> 2; matrix products, arithmetic and copies ran while one was open for 0% -> 0% of each run, Pallas kernels for 25% -> 20%
where the time goes in v12:
time: 45.2 us; the launch traced here: 44.8 us
  Pallas kernels  30.3 us (67%)
  starting transfers between devices  11.5 us (25%)
  waiting for transfers between devices  2.23 us (5%)
  between operations  0.72 us (2%)
    pallas_call x1, Pallas kernels, attend(): pl.pallas_call(functools.partial(attend_kernel, cfg, heads, steps, tuple(...  19.5 us
    ppermute x9, starting transfers between devices, move(): return lax.ppermute(value, AXES, pairs)  11.5 us
    pallas_call x1, Pallas kernels, prepare(): pl.pallas_call(functools.partial(prepare_kernel, heads), out_shape=jax.Sh...  8.97 us
    ppermute x9, waiting for transfers between devices, move(): return lax.ppermute(value, AXES, pairs)  2.23 us
    pallas_call x1, Pallas kernels, pack(): pl.pallas_call(pack_kernel, out_shape=jax.ShapeDtypeStruct((rows, 128), B...  1.83 us
  transfers between devices with their start and end apart: 9, of which 2 were waited for; matrix products, arithmetic and copies ran while one was open for 0% of the time, Pallas kernels for 20%

profile of v12, /device:TPU:0, one launch (start us, length us, event | category | flops | bytes accessed | tf_op | source)
XLA Modules:
  0.0 44.8 jit_solution(15870886193695006663)
XLA Ops:
  0.0 1.8 %pack_rows.1.rest_0_ = bf16[656,128]{1,0:T(8,128)(2,1)} custom-call(bf16[576,128]{1,0:T(8,128)(2,1)} %bitcast.2, bf16[16,576]{1,0:T(8,128)(2,1)} %cache_ref.1, f32[1,512]{1,0:T(1,128)} %bitcast.3), custom_call_target="tpu_custom_call" | custom-call | tf_op jit(solution)/shard_map/pack_rows/pallas_call | solution.py:56
  1.8 0.0 copy-start
  1.8 0.0 copy-start.1
  1.8 6.1 %collective-permute-start.3 = (bf16[656,128]{1,0:T(8,128)(2,1)}, bf16[656,128]{1,0:T(8,128)(2,1)S(1)}, u32[]{:S(2)}, u32[]{:S(2)}) collective-permute-start(bf16[656,128]{1,0:T(8,128)(2,1)} %pack_rows.1.rest_0_), channel_id=1, source_target_pairs={{0,8},{1,1},{2,10},{3,3},{4,12},{5,5},{6,14},{7,7},{8,0},{9,9},{10... | collective-permute-start | bytes 503816 | tf_op jit(solution)/shard_map/ppermute | solution.py:313
  7.9 1.4 %collective-permute-start.2 = (bf16[656,128]{1,0:T(8,128)(2,1)}, bf16[656,128]{1,0:T(8,128)(2,1)S(1)}, u32[]{:S(2)}, u32[]{:S(2)}) collective-permute-start(bf16[656,128]{1,0:T(8,128)(2,1)} %pack_rows.1.rest_0_), channel_id=1, source_target_pairs={{0,12},{1,15},{2,14},{3,13},{4,0},{5,3},{6,2},{7,1},{8,4},{9,7},{1... | collective-permute-start | bytes 503816 | tf_op jit(solution)/shard_map/ppermute | solution.py:313
  9.3 0.7 %collective-permute-start.1 = (bf16[656,128]{1,0:T(8,128)(2,1)}, bf16[656,128]{1,0:T(8,128)(2,1)S(1)}, u32[]{:S(2)}, u32[]{:S(2)}) collective-permute-start(bf16[656,128]{1,0:T(8,128)(2,1)} %pack_rows.1.rest_0_), channel_id=1, source_target_pairs={{0,4},{1,7},{2,6},{3,5},{4,8},{5,11},{6,10},{7,9},{8,12},{9,15},{1... | collective-permute-start | bytes 503816 | tf_op jit(solution)/shard_map/ppermute | solution.py:313
  10.0 1.5 %collective-permute-start = (bf16[656,128]{1,0:T(8,128)(2,1)}, bf16[656,128]{1,0:T(8,128)(2,1)S(1)}, u32[]{:S(2)}, u32[]{:S(2)}) collective-permute-start(bf16[656,128]{1,0:T(8,128)(2,1)} %pack_rows.1.rest_0_), channel_id=1, source_target_pairs={{0,2},{1,3},{2,0},{3,1},{4,6},{5,7},{6,4},{7,5},{8,10},{9,11},{10,... | collective-permute-start | bytes 503816 | tf_op jit(solution)/shard_map/ppermute | solution.py:313
  11.5 9.0 %prepare.1.latent_ref = bf16[6144,512]{1,0:T(8,128)(2,1)} custom-call(bf16[128,6144]{1,0:T(8,128)(2,1)} %q_ref.1, bf16[512,4096]{1,0:T(8,128)(2,1)} %wk_ref.1), custom_call_target="tpu_custom_call" | custom-call | flops 536870912 | bytes 16777216 | tf_op jit(solution)/shard_map/prepare/pallas_call | solution.py:99
  20.5 0.0 collective-permute-done.3.rest_6_
  20.5 0.0 collective-permute-done.2.rest_3_
  20.5 0.0 collective-permute-done.1.rest_2_
  20.5 0.0 collective-permute-done.rest_1_
  20.5 0.1 collective-permute-start.6
  20.6 0.5 %collective-permute-start.8 = (bf16[656,128]{1,0:T(8,128)(2,1)S(1)}, bf16[656,128]{1,0:T(8,128)(2,1)S(1)}, u32[]{:S(2)}, u32[]{:S(2)}) collective-permute-start(bf16[656,128]{1,0:T(8,128)(2,1)S(1)} %collective-permute-done.3.rest_6_), channel_id=1, source_target_pairs={{0,1},{1,0},{2,3},{3,2},{4,5},{5,4},{6,7},{7,6},{8,9},{9,8},{10,11... | collective-permute-start | bytes 503816 | tf_op jit(solution)/shard_map/ppermute | solution.py:313
  21.1 0.1 collective-permute-start.4
  21.1 0.4 collective-permute-start.5
  21.6 1.9 %collective-permute-done.6.rest_7_ = bf16[656,128]{1,0:T(8,128)(2,1)S(1)} collective-permute-done((bf16[656,128]{1,0:T(8,128)(2,1)S(1)}, bf16[656,128]{1,0:T(8,128)(2,1)S(1)}, u32[]{:S(2)}, u32[]{:S(2)}) %collective-permute-start.6) | collective-permute-done | bytes 167968 | tf_op jit(solution)/shard_map/ppermute | solution.py:313
  23.4 0.8 %collective-permute-start.7 = (bf16[656,128]{1,0:T(8,128)(2,1)S(1)}, bf16[656,128]{1,0:T(8,128)(2,1)S(1)}, u32[]{:S(2)}, u32[]{:S(2)}) collective-permute-start(bf16[656,128]{1,0:T(8,128)(2,1)S(1)} %collective-permute-done.6.rest_7_), channel_id=1, source_target_pairs={{0,1},{1,0},{2,3},{3,2},{4,5},{5,4},{6,7},{7,6},{8,9},{9,8},{10,11... | collective-permute-start | bytes 503816 | tf_op jit(solution)/shard_map/ppermute | solution.py:313
  24.9 0.0 collective-permute-done.4.rest_4_
  24.9 0.0 collective-permute-done.5.rest_5_
  24.9 0.0 collective-permute-done.8.rest_9_
  24.9 0.4 collective-permute-done.7.rest_8_
  25.3 0.0 copy-done
  25.3 0.0 copy-done.1
  25.3 19.5 %attend.1 = bf16[128,4096]{1,0:T(8,128)(2,1)} custom-call(s32[8]{0:T(128)S(1)} %copy-done.1, s32[1]{0:T(128)S(6)} %copy.9.prefix_ref, bf16[6144,512]{1,0:T(8,128)(2,1)} %prepare.1.latent_ref, bf16[512,4096]{1,0:T(8,128)(2,1)} %wv_ref.1, bf16[656,128]{1,0:T(8,128)(2,1)S(1)} %copy-done, bf16[656,128]{1,0:T(8,128)(2,1)S(1)} %collective-permute-done.rest_1_, ...), custom_call_target="tpu_custom_call" | custom-call | flops 12079595520 | bytes 8388608 | tf_op jit(solution)/shard_map/attend/pallas_call | solution.py:276
Async XLA Ops:
  1.8 23.4 %copy-start = (bf16[656,128]{1,0:T(8,128)(2,1)S(1)}, bf16[656,128]{1,0:T(8,128)(2,1)}, u32[]{:S(2)}) copy-start(bf16[656,128]{1,0:T(8,128)(2,1)} %pack_rows.1.rest_0_) | copy-start | bytes 503812
  1.8 23.4 %copy-start.1 = (s32[8]{0:T(128)S(1)}, s32[8]{0:T(128)}, u32[]{:S(2)}) copy-start(s32[8]{0:T(128)} %order_ref.1) | copy-start | bytes 100
  1.8 18.6 %collective-permute-start.3 = (bf16[656,128]{1,0:T(8,128)(2,1)}, bf16[656,128]{1,0:T(8,128)(2,1)S(1)}, u32[]{:S(2)}, u32[]{:S(2)}) collective-permute-start(bf16[656,128]{1,0:T(8,128)(2,1)} %pack_rows.1.rest_0_), channel_id=1, source_target_pairs={{0,8},{1,1},{2,10},{3,3},{4,12},{5,5},{6,14},{7,7},{8,0},{9,9},{10... | collective-permute-start | bytes 503816 | tf_op jit(solution)/shard_map/ppermute | solution.py:313
  7.9 12.6 %collective-permute-start.2 = (bf16[656,128]{1,0:T(8,128)(2,1)}, bf16[656,128]{1,0:T(8,128)(2,1)S(1)}, u32[]{:S(2)}, u32[]{:S(2)}) collective-permute-start(bf16[656,128]{1,0:T(8,128)(2,1)} %pack_rows.1.rest_0_), channel_id=1, source_target_pairs={{0,12},{1,15},{2,14},{3,13},{4,0},{5,3},{6,2},{7,1},{8,4},{9,7},{1... | collective-permute-start | bytes 503816 | tf_op jit(solution)/shard_map/ppermute | solution.py:313
  9.3 11.2 %collective-permute-start.1 = (bf16[656,128]{1,0:T(8,128)(2,1)}, bf16[656,128]{1,0:T(8,128)(2,1)S(1)}, u32[]{:S(2)}, u32[]{:S(2)}) collective-permute-start(bf16[656,128]{1,0:T(8,128)(2,1)} %pack_rows.1.rest_0_), channel_id=1, source_target_pairs={{0,4},{1,7},{2,6},{3,5},{4,8},{5,11},{6,10},{7,9},{8,12},{9,15},{1... | collective-permute-start | bytes 503816 | tf_op jit(solution)/shard_map/ppermute | solution.py:313
  10.0 10.5 %collective-permute-start = (bf16[656,128]{1,0:T(8,128)(2,1)}, bf16[656,128]{1,0:T(8,128)(2,1)S(1)}, u32[]{:S(2)}, u32[]{:S(2)}) collective-permute-start(bf16[656,128]{1,0:T(8,128)(2,1)} %pack_rows.1.rest_0_), channel_id=1, source_target_pairs={{0,2},{1,3},{2,0},{3,1},{4,6},{5,7},{6,4},{7,5},{8,10},{9,11},{10,... | collective-permute-start | bytes 503816 | tf_op jit(solution)/shard_map/ppermute | solution.py:313
  20.5 2.9 %collective-permute-start.6 = (bf16[656,128]{1,0:T(8,128)(2,1)S(1)}, bf16[656,128]{1,0:T(8,128)(2,1)S(1)}, u32[]{:S(2)}, u32[]{:S(2)}) collective-permute-start(bf16[656,128]{1,0:T(8,128)(2,1)S(1)} %collective-permute-done.3.rest_6_), channel_id=1, source_target_pairs={{0,3},{1,0},{2,1},{3,2},{4,7},{5,4},{6,5},{7,6},{8,11},{9,8},{10,9... | collective-permute-start | bytes 503816 | tf_op jit(solution)/shard_map/ppermute | solution.py:313
  20.6 4.3 %collective-permute-start.8 = (bf16[656,128]{1,0:T(8,128)(2,1)S(1)}, bf16[656,128]{1,0:T(8,128)(2,1)S(1)}, u32[]{:S(2)}, u32[]{:S(2)}) collective-permute-start(bf16[656,128]{1,0:T(8,128)(2,1)S(1)} %collective-permute-done.3.rest_6_), channel_id=1, source_target_pairs={{0,1},{1,0},{2,3},{3,2},{4,5},{5,4},{6,7},{7,6},{8,9},{9,8},{10,11... | collective-permute-start | bytes 503816 | tf_op jit(solution)/shard_map/ppermute | solution.py:313
  21.1 3.8 %collective-permute-start.4 = (bf16[656,128]{1,0:T(8,128)(2,1)S(1)}, bf16[656,128]{1,0:T(8,128)(2,1)S(1)}, u32[]{:S(2)}, u32[]{:S(2)}) collective-permute-start(bf16[656,128]{1,0:T(8,128)(2,1)S(1)} %collective-permute-done.1.rest_2_), channel_id=1, source_target_pairs={{0,1},{1,0},{2,3},{3,2},{4,5},{5,4},{6,7},{7,6},{8,9},{9,8},{10,11... | collective-permute-start | bytes 503816 | tf_op jit(solution)/shard_map/ppermute | solution.py:313
  21.1 3.7 %collective-permute-start.5 = (bf16[656,128]{1,0:T(8,128)(2,1)S(1)}, bf16[656,128]{1,0:T(8,128)(2,1)S(1)}, u32[]{:S(2)}, u32[]{:S(2)}) collective-permute-start(bf16[656,128]{1,0:T(8,128)(2,1)S(1)} %collective-permute-done.2.rest_3_), channel_id=1, source_target_pairs={{0,1},{1,0},{2,3},{3,2},{4,5},{5,4},{6,7},{7,6},{8,9},{9,8},{10,11... | collective-permute-start | bytes 503816 | tf_op jit(solution)/shard_map/ppermute | solution.py:313
  23.4 1.8 %collective-permute-start.7 = (bf16[656,128]{1,0:T(8,128)(2,1)S(1)}, bf16[656,128]{1,0:T(8,128)(2,1)S(1)}, u32[]{:S(2)}, u32[]{:S(2)}) collective-permute-start(bf16[656,128]{1,0:T(8,128)(2,1)S(1)} %collective-permute-done.6.rest_7_), channel_id=1, source_target_pairs={{0,1},{1,0},{2,3},{3,2},{4,5},{5,4},{6,7},{7,6},{8,9},{9,8},{10,11... | collective-permute-start | bytes 503816 | tf_op jit(solution)/shard_map/ppermute | solution.py:313

commit v13 on v11

--- a/solution.py
+++ b/solution.py
@@ -181,7 +181,7 @@
     keys = rows_ref.shape[0]
     width = heads * tok_rows
     step = pl.program_id(0)
-    pieces = [slice(at, min(at + 256, keys)) for at in range(0, keys, 256)]
+    pieces = [slice(at, min(at + 384, keys)) for at in range(0, keys, 384)]
 
     def by_eights(value):
         return value.reshape(-1, 8, width)
@@ -213,21 +213,15 @@
         return [functools.partial(piece, index) for index in range(len(pieces))]
 
     def outputs(buffer):
-        parts = []
-        totals = []
-
-        def mix(index):
-            first = index * 256
-            final = index == LATENT // 256 - 1
-            here = slice(first, LATENT + ONES if final else first + 256)
-            mixed = jnp.dot(turned_ref[here, :], weight_refs[buffer][...], preferred_element_type=F32)
-            parts.append(mixed[:256].astype(BF))
-            if final:
-                totals.append(mixed[256:257])
+        held = []
+
+        def mix():
+            mixed = jnp.dot(turned_ref[...], weight_refs[buffer][...], preferred_element_type=F32)
+            held.append(mixed[:LATENT].astype(BF))
+            held.append(mixed[LATENT : LATENT + 1])
 
         def finish():
-            total = totals[0]
-            mixed = jnp.concatenate(parts, axis=0)
+            mixed, total = held
             for head in range(heads):
                 here = slice(head * tok_rows, (head + 1) * tok_rows)
                 place = buffer * heads + head
@@ -235,7 +229,7 @@
                 out = jnp.dot(wvt, mixed[:, here], preferred_element_type=F32) / total[:, here]
                 out_ref[:, place * VDIM : (place + 1) * VDIM] = out.astype(BF).T
 
-        return [functools.partial(mix, index) for index in range(LATENT // 256)] + [finish]
+        return [mix, finish]
 
     @pl.when(step == 0)
     def _():

time: 44 us -> 43.6 us (level)
  no operation moved by 1% of the time
where the time goes in v13:
time: 43.6 us; the launch traced here: 43.2 us
  Pallas kernels  31.6 us (72%)
  starting transfers between devices  8.1 us (19%)
  waiting for transfers between devices  2.83 us (6%)
  between operations  0.67 us (2%)
    pallas_call x1, Pallas kernels, attend(): pl.pallas_call(functools.partial(attend_kernel, cfg, heads, steps), out_s...  19 us
    pallas_call x1, Pallas kernels, prepare(): pl.pallas_call(functools.partial(prepare_kernel, heads), out_shape=(jax.S...  10.8 us
    ppermute x7, starting transfers between devices, move(): return lax.ppermute(value, AXES, pairs)  8.1 us
    ppermute x7, waiting for transfers between devices, move(): return lax.ppermute(value, AXES, pairs)  2.83 us
    pallas_call x1, Pallas kernels, pack(): pl.pallas_call(pack_kernel, out_shape=jax.ShapeDtypeStruct((rows, 128), B...  1.83 us
  transfers between devices with their start and end apart: 7, of which 4 were waited for; matrix products, arithmetic and copies ran while one was open for 0% of the time, Pallas kernels for 25%

profile of v13, /device:TPU:0, one launch (start us, length us, event | category | flops | bytes accessed | tf_op | source)
XLA Modules:
  0.0 43.2 jit_solution(6377426995954726142)
XLA Ops:
  0.0 1.8 %pack_rows.1.rest_0_ = bf16[656,128]{1,0:T(8,128)(2,1)} custom-call(bf16[576,128]{1,0:T(8,128)(2,1)} %bitcast.2, bf16[16,576]{1,0:T(8,128)(2,1)} %cache_ref.1, f32[1,512]{1,0:T(1,128)} %bitcast.3), custom_call_target="tpu_custom_call" | custom-call | tf_op jit(solution)/shard_map/pack_rows/pallas_call | solution.py:56
  1.8 0.0 copy-start
  1.8 0.0 copy-start.1
  1.8 5.0 %collective-permute-start.2 = (bf16[656,128]{1,0:T(8,128)(2,1)}, bf16[656,128]{1,0:T(8,128)(2,1)S(1)}, u32[]{:S(2)}, u32[]{:S(2)}) collective-permute-start(bf16[656,128]{1,0:T(8,128)(2,1)} %pack_rows.1.rest_0_), channel_id=1, source_target_pairs={{0,12},{1,15},{2,14},{3,13},{4,0},{5,3},{6,2},{7,1},{8,4},{9,7},{1... | collective-permute-start | bytes 503816 | tf_op jit(solution)/shard_map/ppermute | solution.py:296
  6.9 0.0 collective-permute-start.1
  6.9 1.0 %collective-permute-start = (bf16[656,128]{1,0:T(8,128)(2,1)}, bf16[656,128]{1,0:T(8,128)(2,1)S(1)}, u32[]{:S(2)}, u32[]{:S(2)}) collective-permute-start(bf16[656,128]{1,0:T(8,128)(2,1)} %pack_rows.1.rest_0_), channel_id=1, source_target_pairs={{0,4},{1,7},{2,6},{3,5},{4,8},{5,11},{6,10},{7,9},{8,12},{9,15},{1... | collective-permute-start | bytes 503816 | tf_op jit(solution)/shard_map/ppermute | solution.py:296
  7.9 1.5 %collective-permute-start.3 = (bf16[656,128]{1,0:T(8,128)(2,1)}, bf16[656,128]{1,0:T(8,128)(2,1)S(1)}, u32[]{:S(2)}, u32[]{:S(2)}) collective-permute-start(bf16[656,128]{1,0:T(8,128)(2,1)} %pack_rows.1.rest_0_), channel_id=1, source_target_pairs={{0,2},{1,3},{2,0},{3,1},{4,6},{5,7},{6,4},{7,5},{8,10},{9,11},{10,... | collective-permute-start | bytes 503816 | tf_op jit(solution)/shard_map/ppermute | solution.py:296
  9.4 10.8 %prepare.1 = (bf16[6144,512]{1,0:T(8,128)(2,1)}, bf16[4096,512]{1,0:T(8,128)(2,1)}) custom-call(bf16[128,6144]{1,0:T(8,128)(2,1)} %q_ref.1, bf16[512,4096]{1,0:T(8,128)(2,1)} %wk_ref.1, bf16[512,4096]{1,0:T(8,128)(2,1)} %wv_ref.1), custom_call_target="tpu_custom_call" | custom-call | flops 536870912 | bytes 16777216 | tf_op jit(solution)/shard_map/prepare/pallas_call | solution.py:100
  20.2 0.0 collective-permute-done.2.rest_4_
  20.2 2.1 %collective-permute-done.1.rest_3_ = bf16[656,128]{1,0:T(8,128)(2,1)S(1)} collective-permute-done((bf16[656,128]{1,0:T(8,128)(2,1)}, bf16[656,128]{1,0:T(8,128)(2,1)S(1)}, u32[]{:S(2)}, u32[]{:S(2)}) %collective-permute-start.1) | collective-permute-done | bytes 167968 | tf_op jit(solution)/shard_map/ppermute | solution.py:296
  22.3 0.0 collective-permute-done.rest_2_
  22.3 0.0 collective-permute-start.4
  22.3 0.5 %collective-permute-start.5 = (bf16[656,128]{1,0:T(8,128)(2,1)S(1)}, bf16[656,128]{1,0:T(8,128)(2,1)S(1)}, u32[]{:S(2)}, u32[]{:S(2)}) collective-permute-start(bf16[656,128]{1,0:T(8,128)(2,1)S(1)} %collective-permute-done.1.rest_3_), channel_id=1, source_target_pairs={{0,1},{1,0},{2,3},{3,2},{4,5},{5,4},{6,7},{7,6},{8,9},{9,8},{10,11... | collective-permute-start | bytes 503816 | tf_op jit(solution)/shard_map/ppermute | solution.py:296
  22.8 0.0 collective-permute-start.6
  23.5 0.0 collective-permute-done.3.rest_1_
  23.5 0.2 collective-permute-done.4.rest_5_
  23.7 0.2 collective-permute-done.5.rest_6_
  23.9 0.3 collective-permute-done.6.rest_7_
  24.2 0.0 copy-done
  24.2 0.0 copy-done.1
  24.2 19.0 %attend.1 = bf16[128,4096]{1,0:T(8,128)(2,1)} custom-call(s32[8]{0:T(128)S(1)} %copy-done.1, s32[1]{0:T(128)S(6)} %copy.9.prefix_ref, bf16[6144,512]{1,0:T(8,128)(2,1)} %get-tuple-element.14.latent_ref, bf16[4096,512]{1,0:T(8,128)(2,1)} %get-tuple-element.15.wvt_ref, bf16[656,128]{1,0:T(8,128)(2,1)S(1)} %copy-done, ...), custom_call_target="tpu_custom_call" | custom-call | flops 12079595520 | bytes 8388608 | tf_op jit(solution)/shard_map/attend/pallas_call | solution.py:260
Async XLA Ops:
  1.8 22.4 %copy-start = (bf16[656,128]{1,0:T(8,128)(2,1)S(1)}, bf16[656,128]{1,0:T(8,128)(2,1)}, u32[]{:S(2)}) copy-start(bf16[656,128]{1,0:T(8,128)(2,1)} %pack_rows.1.rest_0_) | copy-start | bytes 503812
  1.8 22.4 %copy-start.1 = (s32[8]{0:T(128)S(1)}, s32[8]{0:T(128)}, u32[]{:S(2)}) copy-start(s32[8]{0:T(128)} %order_ref.1) | copy-start | bytes 100
  1.8 18.4 %collective-permute-start.2 = (bf16[656,128]{1,0:T(8,128)(2,1)}, bf16[656,128]{1,0:T(8,128)(2,1)S(1)}, u32[]{:S(2)}, u32[]{:S(2)}) collective-permute-start(bf16[656,128]{1,0:T(8,128)(2,1)} %pack_rows.1.rest_0_), channel_id=1, source_target_pairs={{0,12},{1,15},{2,14},{3,13},{4,0},{5,3},{6,2},{7,1},{8,4},{9,7},{1... | collective-permute-start | bytes 503816 | tf_op jit(solution)/shard_map/ppermute | solution.py:296
  6.9 15.4 %collective-permute-start.1 = (bf16[656,128]{1,0:T(8,128)(2,1)}, bf16[656,128]{1,0:T(8,128)(2,1)S(1)}, u32[]{:S(2)}, u32[]{:S(2)}) collective-permute-start(bf16[656,128]{1,0:T(8,128)(2,1)} %pack_rows.1.rest_0_), channel_id=1, source_target_pairs={{0,8},{1,11},{2,10},{3,9},{4,12},{5,15},{6,14},{7,13},{8,0},{9,3},... | collective-permute-start | bytes 503816 | tf_op jit(solution)/shard_map/ppermute | solution.py:296
  6.9 15.4 %collective-permute-start = (bf16[656,128]{1,0:T(8,128)(2,1)}, bf16[656,128]{1,0:T(8,128)(2,1)S(1)}, u32[]{:S(2)}, u32[]{:S(2)}) collective-permute-start(bf16[656,128]{1,0:T(8,128)(2,1)} %pack_rows.1.rest_0_), channel_id=1, source_target_pairs={{0,4},{1,7},{2,6},{3,5},{4,8},{5,11},{6,10},{7,9},{8,12},{9,15},{1... | collective-permute-start | bytes 503816 | tf_op jit(solution)/shard_map/ppermute | solution.py:296
  7.9 15.6 %collective-permute-start.3 = (bf16[656,128]{1,0:T(8,128)(2,1)}, bf16[656,128]{1,0:T(8,128)(2,1)S(1)}, u32[]{:S(2)}, u32[]{:S(2)}) collective-permute-start(bf16[656,128]{1,0:T(8,128)(2,1)} %pack_rows.1.rest_0_), channel_id=1, source_target_pairs={{0,2},{1,3},{2,0},{3,1},{4,6},{5,7},{6,4},{7,5},{8,10},{9,11},{10,... | collective-permute-start | bytes 503816 | tf_op jit(solution)/shard_map/ppermute | solution.py:296
  22.3 1.4 %collective-permute-start.4 = (bf16[656,128]{1,0:T(8,128)(2,1)S(1)}, bf16[656,128]{1,0:T(8,128)(2,1)S(1)}, u32[]{:S(2)}, u32[]{:S(2)}) collective-permute-start(bf16[656,128]{1,0:T(8,128)(2,1)S(1)} %collective-permute-done.rest_2_), channel_id=1, source_target_pairs={{0,1},{1,0},{2,3},{3,2},{4,5},{5,4},{6,7},{7,6},{8,9},{9,8},{10,11... | collective-permute-start | bytes 503816 | tf_op jit(solution)/shard_map/ppermute | solution.py:296
  22.3 1.6 %collective-permute-start.5 = (bf16[656,128]{1,0:T(8,128)(2,1)S(1)}, bf16[656,128]{1,0:T(8,128)(2,1)S(1)}, u32[]{:S(2)}, u32[]{:S(2)}) collective-permute-start(bf16[656,128]{1,0:T(8,128)(2,1)S(1)} %collective-permute-done.1.rest_3_), channel_id=1, source_target_pairs={{0,1},{1,0},{2,3},{3,2},{4,5},{5,4},{6,7},{7,6},{8,9},{9,8},{10,11... | collective-permute-start | bytes 503816 | tf_op jit(solution)/shard_map/ppermute | solution.py:296
  22.8 1.4 %collective-permute-start.6 = (bf16[656,128]{1,0:T(8,128)(2,1)S(1)}, bf16[656,128]{1,0:T(8,128)(2,1)S(1)}, u32[]{:S(2)}, u32[]{:S(2)}) collective-permute-start(bf16[656,128]{1,0:T(8,128)(2,1)S(1)} %collective-permute-done.2.rest_4_), channel_id=1, source_target_pairs={{0,1},{1,0},{2,3},{3,2},{4,5},{5,4},{6,7},{7,6},{8,9},{9,8},{10,11... | collective-permute-start | bytes 503816 | tf_op jit(solution)/shard_map/ppermute | solution.py:296

commit v14 on v12

--- a/solution.py
+++ b/solution.py
@@ -76,20 +76,28 @@
 def prepare_kernel(heads, q_ref, wk_ref, latent_ref):
     scale = math.log2(math.e) / math.sqrt(NOPE + ROPE)
     rows = q_ref.shape[0]
-    turned = q_ref[...].T
     ids = lax.broadcasted_iota(jnp.int32, (PACKED - LATENT - 2 * ROPE, rows), 0)
     flags = jnp.where(ids == 0, NEG, 0.0).astype(BF)
-    for head in range(heads):
-        at = head * (NOPE + ROPE)
-        here = slice(head * rows, (head + 1) * rows)
-        wk = wk_ref[:, head * NOPE : (head + 1) * NOPE]
-        latent = jnp.dot(wk, turned[at : at + NOPE], preferred_element_type=F32)
-        latent_ref[:LATENT, here] = (latent * scale).astype(BF)
-        rotary = turned[at + NOPE : at + NOPE + ROPE].astype(F32) * scale
-        rounded = rotary.astype(BF)
-        latent_ref[LATENT : LATENT + ROPE, here] = rounded
-        latent_ref[LATENT + ROPE : LATENT + 2 * ROPE, here] = (rotary - rounded.astype(F32)).astype(BF)
-        latent_ref[LATENT + 2 * ROPE :, here] = flags
+    nothing = jnp.zeros((NOPE, rows), BF)
+    for pair in range(q_ref.shape[1] // (2 * (NOPE + ROPE))):
+        turned = q_ref[:, pair * 384 : pair * 384 + 384].T
+        left = jnp.concatenate([turned[:NOPE], nothing], axis=0)
+        right = jnp.concatenate([nothing, turned[192 : 192 + NOPE]], axis=0)
+        both = jnp.concatenate([left, right], axis=1)
+        wk = wk_ref[:, pair * 2 * NOPE : (pair + 1) * 2 * NOPE]
+        latent = (jnp.dot(wk, both, preferred_element_type=F32) * scale).astype(BF)
+        group, head = divmod(2 * pair, heads)
+        at = group * PACKED
+        latent_ref[at : at + LATENT, head * rows : (head + 2) * rows] = latent
+        for side in range(2):
+            here = slice((head + side) * rows, (head + side + 1) * rows)
+            begin = side * 192 + NOPE
+            rotary = turned[begin : begin + ROPE].astype(F32) * scale
+            rounded = rotary.astype(BF)
+            latent_ref[at + LATENT : at + LATENT + ROPE, here] = rounded
+            rest = (rotary - rounded.astype(F32)).astype(BF)
+            latent_ref[at + LATENT + ROPE : at + LATENT + 2 * ROPE, here] = rest
+            latent_ref[at + LATENT + 2 * ROPE : at + PACKED, here] = flags
 
 
 def prepare(queries, key_weight, heads):
@@ -99,12 +107,12 @@
     return pl.pallas_call(
         functools.partial(prepare_kernel, heads),
         out_shape=jax.ShapeDtypeStruct((steps * PACKED, heads * rows), BF),
-        grid=(steps,),
+        grid=(steps // 2,),
         in_specs=[
-            pl.BlockSpec((rows, heads * (NOPE + ROPE)), lambda i: (0, i)),
-            pl.BlockSpec((depth, heads * NOPE), lambda i: (0, i)),
+            pl.BlockSpec((rows, 2 * heads * (NOPE + ROPE)), lambda i: (0, i)),
+            pl.BlockSpec((depth, 2 * heads * NOPE), lambda i: (0, i)),
         ],
-        out_specs=pl.BlockSpec((PACKED, heads * rows), lambda i: (i, 0)),
+        out_specs=pl.BlockSpec((2 * PACKED, heads * rows), lambda i: (i, 0)),
         compiler_params=pltpu.CompilerParams(vmem_limit_bytes=58 * 1024 * 1024),
         cost_estimate=pl.CostEstimate(
             flops=2 * rows * depth * width, bytes_accessed=depth * width * 8, transcendentals=0
@@ -184,7 +192,7 @@
     keys = rows_ref.shape[0]
     width = heads * tok_rows
     step = pl.program_id(0)
-    pieces = [slice(at, min(at + 256, keys)) for at in range(0, keys, 256)]
+    pieces = [slice(at, min(at + 384, keys)) for at in range(0, keys, 384)]
 
     def by_eights(value):
         return value.reshape(-1, 8, width)
@@ -216,26 +224,21 @@
         return [functools.partial(piece, index) for index in range(len(pieces))]
 
     def outputs(buffer):
-        parts = []
-        totals = []
-
-        def mix(index):
-            first = index * 256
-            final = index == LATENT // 256 - 1
-            here = slice(first, LATENT + ONES if final else first + 256)
-            mixed = jnp.dot(turned_ref[here, :], weight_refs[buffer][...], preferred_element_type=F32)
-            parts.append(mixed[:256].astype(BF))
-            if final:
-                totals.append(mixed[256:257])
-
-        def turn(head):
-            place = buffer * heads + head
-            to = slice(head * VDIM, (head + 1) * VDIM)
-            wvt_refs[buffer][to, :] = wv_ref[:, place * VDIM : (place + 1) * VDIM].T
+        held = []
+
+        def mix():
+            mixed = jnp.dot(turned_ref[...], weight_refs[buffer][...], preferred_element_type=F32)
+            held.append(mixed[:LATENT].astype(BF))
+            held.append(mixed[LATENT : LATENT + 1])
+
+        def turn(part):
+            for head in range(part * heads // 2, (part + 1) * heads // 2):
+                place = buffer * heads + head
+                to = slice(head * VDIM, (head + 1) * VDIM)
+                wvt_refs[buffer][to, :] = wv_ref[:, place * VDIM : (place + 1) * VDIM].T
 
         def finish():
-            total = totals[0]
-            mixed = jnp.concatenate(parts, axis=0)
+            mixed, total = held
             for head in range(heads):
                 here = slice(head * tok_rows, (head + 1) * tok_rows)
                 place = buffer * heads + head
@@ -243,9 +246,7 @@
                 out = jnp.dot(wvt, mixed[:, here], preferred_element_type=F32) / total[:, here]
                 out_ref[:, place * VDIM : (place + 1) * VDIM] = out.astype(BF).T
 
-        turns = [functools.partial(turn, head) for head in range(heads)]
-        mixes = [functools.partial(mix, index) for index in range(LATENT // 256)]
-        return turns[: heads // 2] + mixes[:-1] + turns[heads // 2 :] + [mixes[-1], finish]
+        return [functools.partial(turn, 0), mix, functools.partial(turn, 1), finish]
 
     @pl.when(step == 0)
     def _():

time: 45.2 us -> 44.4 us (0.982)
  Pallas kernels: 30.3 us -> 28.1 us
  waiting for transfers between devices: 2.23 us -> 3.81 us
    pallas_call x1, Pallas kernels: 8.97 us -> 6.55 us  [prepare(): pl.pallas_call(functools.partial(prepare_kernel, heads), out_shape=jax.Sh...]
    ppermute x9, waiting for transfers between devices: 2.23 us -> 3.81 us  [move(): return lax.ppermute(value, AXES, pairs)]
  transfers between devices with their start and end apart: 9 -> 9, of which waited for: 2 -> 3; matrix products, arithmetic and copies ran while one was open for 0% -> 0% of each run, Pallas kernels for 20% -> 15%
where the time goes in v14:
time: 44.4 us; the launch traced here: 44.2 us
  Pallas kernels  28.1 us (63%)
  starting transfers between devices  11.5 us (26%)
  waiting for transfers between devices  3.81 us (9%)
  between operations  0.7 us (2%)
    pallas_call x1, Pallas kernels, attend(): pl.pallas_call(functools.partial(attend_kernel, cfg, heads, steps, tuple(...  19.7 us
    ppermute x9, starting transfers between devices, move(): return lax.ppermute(value, AXES, pairs)  11.5 us
    pallas_call x1, Pallas kernels, prepare(): pl.pallas_call(functools.partial(prepare_kernel, heads), out_shape=jax.Sh...  6.55 us
    ppermute x9, waiting for transfers between devices, move(): return lax.ppermute(value, AXES, pairs)  3.81 us
    pallas_call x1, Pallas kernels, pack(): pl.pallas_call(pack_kernel, out_shape=jax.ShapeDtypeStruct((rows, 128), B...  1.83 us
  transfers between devices with their start and end apart: 9, of which 3 were waited for; matrix products, arithmetic and copies ran while one was open for 0% of the time, Pallas kernels for 15%

profile of v14, /device:TPU:0, one launch (start us, length us, event | category | flops | bytes accessed | tf_op | source)
XLA Modules:
  0.0 44.2 jit_solution(3027588139832773282)
XLA Ops:
  0.0 1.8 %pack_rows.1.rest_0_ = bf16[656,128]{1,0:T(8,128)(2,1)} custom-call(bf16[576,128]{1,0:T(8,128)(2,1)} %bitcast.2, bf16[16,576]{1,0:T(8,128)(2,1)} %cache_ref.1, f32[1,512]{1,0:T(1,128)} %bitcast.3), custom_call_target="tpu_custom_call" | custom-call | tf_op jit(solution)/shard_map/pack_rows/pallas_call | solution.py:56
  1.8 0.0 copy-start
  1.8 0.0 copy-start.1
  1.8 6.1 %collective-permute-start.3 = (bf16[656,128]{1,0:T(8,128)(2,1)}, bf16[656,128]{1,0:T(8,128)(2,1)S(1)}, u32[]{:S(2)}, u32[]{:S(2)}) collective-permute-start(bf16[656,128]{1,0:T(8,128)(2,1)} %pack_rows.1.rest_0_), channel_id=1, source_target_pairs={{0,8},{1,1},{2,10},{3,3},{4,12},{5,5},{6,14},{7,7},{8,0},{9,9},{10... | collective-permute-start | bytes 503816 | tf_op jit(solution)/shard_map/ppermute | solution.py:314
  7.9 1.4 %collective-permute-start.2 = (bf16[656,128]{1,0:T(8,128)(2,1)}, bf16[656,128]{1,0:T(8,128)(2,1)S(1)}, u32[]{:S(2)}, u32[]{:S(2)}) collective-permute-start(bf16[656,128]{1,0:T(8,128)(2,1)} %pack_rows.1.rest_0_), channel_id=1, source_target_pairs={{0,12},{1,15},{2,14},{3,13},{4,0},{5,3},{6,2},{7,1},{8,4},{9,7},{1... | collective-permute-start | bytes 503816 | tf_op jit(solution)/shard_map/ppermute | solution.py:314
  9.3 0.7 %collective-permute-start.1 = (bf16[656,128]{1,0:T(8,128)(2,1)}, bf16[656,128]{1,0:T(8,128)(2,1)S(1)}, u32[]{:S(2)}, u32[]{:S(2)}) collective-permute-start(bf16[656,128]{1,0:T(8,128)(2,1)} %pack_rows.1.rest_0_), channel_id=1, source_target_pairs={{0,4},{1,7},{2,6},{3,5},{4,8},{5,11},{6,10},{7,9},{8,12},{9,15},{1... | collective-permute-start | bytes 503816 | tf_op jit(solution)/shard_map/ppermute | solution.py:314
  10.0 1.5 %collective-permute-start = (bf16[656,128]{1,0:T(8,128)(2,1)}, bf16[656,128]{1,0:T(8,128)(2,1)S(1)}, u32[]{:S(2)}, u32[]{:S(2)}) collective-permute-start(bf16[656,128]{1,0:T(8,128)(2,1)} %pack_rows.1.rest_0_), channel_id=1, source_target_pairs={{0,2},{1,3},{2,0},{3,1},{4,6},{5,7},{6,4},{7,5},{8,10},{9,11},{10,... | collective-permute-start | bytes 503816 | tf_op jit(solution)/shard_map/ppermute | solution.py:314
  11.5 6.6 %prepare.1.latent_ref = bf16[6144,512]{1,0:T(8,128)(2,1)} custom-call(bf16[128,6144]{1,0:T(8,128)(2,1)} %q_ref.1, bf16[512,4096]{1,0:T(8,128)(2,1)} %wk_ref.1), custom_call_target="tpu_custom_call" | custom-call | flops 536870912 | bytes 16777216 | tf_op jit(solution)/shard_map/prepare/pallas_call | solution.py:107
  18.1 0.0 collective-permute-done.3.rest_6_
  18.1 0.0 collective-permute-done.2.rest_3_
  18.1 1.6 %collective-permute-done.1.rest_2_ = bf16[656,128]{1,0:T(8,128)(2,1)S(1)} collective-permute-done((bf16[656,128]{1,0:T(8,128)(2,1)}, bf16[656,128]{1,0:T(8,128)(2,1)S(1)}, u32[]{:S(2)}, u32[]{:S(2)}) %collective-permute-start.1) | collective-permute-done | bytes 167968 | tf_op jit(solution)/shard_map/ppermute | solution.py:314
  19.7 0.0 collective-permute-done.rest_1_
  19.7 0.0 collective-permute-start.6
  19.7 0.5 %collective-permute-start.8 = (bf16[656,128]{1,0:T(8,128)(2,1)S(1)}, bf16[656,128]{1,0:T(8,128)(2,1)S(1)}, u32[]{:S(2)}, u32[]{:S(2)}) collective-permute-start(bf16[656,128]{1,0:T(8,128)(2,1)S(1)} %collective-permute-done.3.rest_6_), channel_id=1, source_target_pairs={{0,1},{1,0},{2,3},{3,2},{4,5},{5,4},{6,7},{7,6},{8,9},{9,8},{10,11... | collective-permute-start | bytes 503816 | tf_op jit(solution)/shard_map/ppermute | solution.py:314
  20.2 0.0 collective-permute-start.4
  20.2 0.5 %collective-permute-start.5 = (bf16[656,128]{1,0:T(8,128)(2,1)S(1)}, bf16[656,128]{1,0:T(8,128)(2,1)S(1)}, u32[]{:S(2)}, u32[]{:S(2)}) collective-permute-start(bf16[656,128]{1,0:T(8,128)(2,1)S(1)} %collective-permute-done.2.rest_3_), channel_id=1, source_target_pairs={{0,1},{1,0},{2,3},{3,2},{4,5},{5,4},{6,7},{7,6},{8,9},{9,8},{10,11... | collective-permute-start | bytes 503816 | tf_op jit(solution)/shard_map/ppermute | solution.py:314
  20.7 1.9 %collective-permute-done.6.rest_7_ = bf16[656,128]{1,0:T(8,128)(2,1)S(1)} collective-permute-done((bf16[656,128]{1,0:T(8,128)(2,1)S(1)}, bf16[656,128]{1,0:T(8,128)(2,1)S(1)}, u32[]{:S(2)}, u32[]{:S(2)}) %collective-permute-start.6) | collective-permute-done | bytes 167968 | tf_op jit(solution)/shard_map/ppermute | solution.py:314
  22.5 0.8 %collective-permute-start.7 = (bf16[656,128]{1,0:T(8,128)(2,1)S(1)}, bf16[656,128]{1,0:T(8,128)(2,1)S(1)}, u32[]{:S(2)}, u32[]{:S(2)}) collective-permute-start(bf16[656,128]{1,0:T(8,128)(2,1)S(1)} %collective-permute-done.6.rest_7_), channel_id=1, source_target_pairs={{0,1},{1,0},{2,3},{3,2},{4,5},{5,4},{6,7},{7,6},{8,9},{9,8},{10,11... | collective-permute-start | bytes 503816 | tf_op jit(solution)/shard_map/ppermute | solution.py:314
  24.0 0.0 collective-permute-done.4.rest_4_
  24.0 0.0 collective-permute-done.5.rest_5_
  24.0 0.0 collective-permute-done.8.rest_9_
  24.1 0.4 collective-permute-done.7.rest_8_
  24.4 0.0 copy-done
  24.4 0.0 copy-done.1
  24.4 19.7 %attend.1 = bf16[128,4096]{1,0:T(8,128)(2,1)} custom-call(s32[8]{0:T(128)S(1)} %copy-done.1, s32[1]{0:T(128)S(6)} %copy.9.prefix_ref, bf16[6144,512]{1,0:T(8,128)(2,1)} %prepare.1.latent_ref, bf16[512,4096]{1,0:T(8,128)(2,1)} %wv_ref.1, bf16[656,128]{1,0:T(8,128)(2,1)S(1)} %copy-done, bf16[656,128]{1,0:T(8,128)(2,1)S(1)} %collective-permute-done.rest_1_, ...), custom_call_target="tpu_custom_call" | custom-call | flops 12079595520 | bytes 8388608 | tf_op jit(solution)/shard_map/attend/pallas_call | solution.py:277
Async XLA Ops:
  1.8 22.6 %copy-start = (bf16[656,128]{1,0:T(8,128)(2,1)S(1)}, bf16[656,128]{1,0:T(8,128)(2,1)}, u32[]{:S(2)}) copy-start(bf16[656,128]{1,0:T(8,128)(2,1)} %pack_rows.1.rest_0_) | copy-start | bytes 503812
  1.8 22.6 %copy-start.1 = (s32[8]{0:T(128)S(1)}, s32[8]{0:T(128)}, u32[]{:S(2)}) copy-start(s32[8]{0:T(128)} %order_ref.1) | copy-start | bytes 100
  1.8 16.2 %collective-permute-start.3 = (bf16[656,128]{1,0:T(8,128)(2,1)}, bf16[656,128]{1,0:T(8,128)(2,1)S(1)}, u32[]{:S(2)}, u32[]{:S(2)}) collective-permute-start(bf16[656,128]{1,0:T(8,128)(2,1)} %pack_rows.1.rest_0_), channel_id=1, source_target_pairs={{0,8},{1,1},{2,10},{3,3},{4,12},{5,5},{6,14},{7,7},{8,0},{9,9},{10... | collective-permute-start | bytes 503816 | tf_op jit(solution)/shard_map/ppermute | solution.py:314
  7.9 10.2 %collective-permute-start.2 = (bf16[656,128]{1,0:T(8,128)(2,1)}, bf16[656,128]{1,0:T(8,128)(2,1)S(1)}, u32[]{:S(2)}, u32[]{:S(2)}) collective-permute-start(bf16[656,128]{1,0:T(8,128)(2,1)} %pack_rows.1.rest_0_), channel_id=1, source_target_pairs={{0,12},{1,15},{2,14},{3,13},{4,0},{5,3},{6,2},{7,1},{8,4},{9,7},{1... | collective-permute-start | bytes 503816 | tf_op jit(solution)/shard_map/ppermute | solution.py:314
  9.3 10.3 %collective-permute-start.1 = (bf16[656,128]{1,0:T(8,128)(2,1)}, bf16[656,128]{1,0:T(8,128)(2,1)S(1)}, u32[]{:S(2)}, u32[]{:S(2)}) collective-permute-start(bf16[656,128]{1,0:T(8,128)(2,1)} %pack_rows.1.rest_0_), channel_id=1, source_target_pairs={{0,4},{1,7},{2,6},{3,5},{4,8},{5,11},{6,10},{7,9},{8,12},{9,15},{1... | collective-permute-start | bytes 503816 | tf_op jit(solution)/shard_map/ppermute | solution.py:314
  10.0 9.7 %collective-permute-start = (bf16[656,128]{1,0:T(8,128)(2,1)}, bf16[656,128]{1,0:T(8,128)(2,1)S(1)}, u32[]{:S(2)}, u32[]{:S(2)}) collective-permute-start(bf16[656,128]{1,0:T(8,128)(2,1)} %pack_rows.1.rest_0_), channel_id=1, source_target_pairs={{0,2},{1,3},{2,0},{3,1},{4,6},{5,7},{6,4},{7,5},{8,10},{9,11},{10,... | collective-permute-start | bytes 503816 | tf_op jit(solution)/shard_map/ppermute | solution.py:314
  19.7 2.9 %collective-permute-start.6 = (bf16[656,128]{1,0:T(8,128)(2,1)S(1)}, bf16[656,128]{1,0:T(8,128)(2,1)S(1)}, u32[]{:S(2)}, u32[]{:S(2)}) collective-permute-start(bf16[656,128]{1,0:T(8,128)(2,1)S(1)} %collective-permute-done.3.rest_6_), channel_id=1, source_target_pairs={{0,3},{1,0},{2,1},{3,2},{4,7},{5,4},{6,5},{7,6},{8,11},{9,8},{10,9... | collective-permute-start | bytes 503816 | tf_op jit(solution)/shard_map/ppermute | solution.py:314
  19.7 4.4 %collective-permute-start.8 = (bf16[656,128]{1,0:T(8,128)(2,1)S(1)}, bf16[656,128]{1,0:T(8,128)(2,1)S(1)}, u32[]{:S(2)}, u32[]{:S(2)}) collective-permute-start(bf16[656,128]{1,0:T(8,128)(2,1)S(1)} %collective-permute-done.3.rest_6_), channel_id=1, source_target_pairs={{0,1},{1,0},{2,3},{3,2},{4,5},{5,4},{6,7},{7,6},{8,9},{9,8},{10,11... | collective-permute-start | bytes 503816 | tf_op jit(solution)/shard_map/ppermute | solution.py:314
  20.2 3.9 %collective-permute-start.4 = (bf16[656,128]{1,0:T(8,128)(2,1)S(1)}, bf16[656,128]{1,0:T(8,128)(2,1)S(1)}, u32[]{:S(2)}, u32[]{:S(2)}) collective-permute-start(bf16[656,128]{1,0:T(8,128)(2,1)S(1)} %collective-permute-done.1.rest_2_), channel_id=1, source_target_pairs={{0,1},{1,0},{2,3},{3,2},{4,5},{5,4},{6,7},{7,6},{8,9},{9,8},{10,11... | collective-permute-start | bytes 503816 | tf_op jit(solution)/shard_map/ppermute | solution.py:314
  20.2 3.9 %collective-permute-start.5 = (bf16[656,128]{1,0:T(8,128)(2,1)S(1)}, bf16[656,128]{1,0:T(8,128)(2,1)S(1)}, u32[]{:S(2)}, u32[]{:S(2)}) collective-permute-start(bf16[656,128]{1,0:T(8,128)(2,1)S(1)} %collective-permute-done.2.rest_3_), channel_id=1, source_target_pairs={{0,1},{1,0},{2,3},{3,2},{4,5},{5,4},{6,7},{7,6},{8,9},{9,8},{10,11... | collective-permute-start | bytes 503816 | tf_op jit(solution)/shard_map/ppermute | solution.py:314
  22.5 1.9 %collective-permute-start.7 = (bf16[656,128]{1,0:T(8,128)(2,1)S(1)}, bf16[656,128]{1,0:T(8,128)(2,1)S(1)}, u32[]{:S(2)}, u32[]{:S(2)}) collective-permute-start(bf16[656,128]{1,0:T(8,128)(2,1)S(1)} %collective-permute-done.6.rest_7_), channel_id=1, source_target_pairs={{0,1},{1,0},{2,3},{3,2},{4,5},{5,4},{6,7},{7,6},{8,9},{9,8},{10,11... | collective-permute-start | bytes 503816 | tf_op jit(solution)/shard_map/ppermute | solution.py:314

commit v15 on v13

--- a/solution.py
+++ b/solution.py
@@ -76,21 +76,30 @@
 def prepare_kernel(heads, q_ref, wk_ref, wv_ref, latent_ref, wvt_ref):
     scale = math.log2(math.e) / math.sqrt(NOPE + ROPE)
     rows = q_ref.shape[0]
-    turned = q_ref[...].T
     ids = lax.broadcasted_iota(jnp.int32, (PACKED - LATENT - 2 * ROPE, rows), 0)
     flags = jnp.where(ids == 0, NEG, 0.0).astype(BF)
-    for head in range(heads):
-        at = head * (NOPE + ROPE)
-        here = slice(head * rows, (head + 1) * rows)
-        wk = wk_ref[:, head * NOPE : (head + 1) * NOPE]
-        latent = jnp.dot(wk, turned[at : at + NOPE], preferred_element_type=F32)
-        latent_ref[:LATENT, here] = (latent * scale).astype(BF)
-        rotary = turned[at + NOPE : at + NOPE + ROPE].astype(F32) * scale
-        rounded = rotary.astype(BF)
-        latent_ref[LATENT : LATENT + ROPE, here] = rounded
-        latent_ref[LATENT + ROPE : LATENT + 2 * ROPE, here] = (rotary - rounded.astype(F32)).astype(BF)
-        latent_ref[LATENT + 2 * ROPE :, here] = flags
-    wvt_ref[...] = wv_ref[...].T
+    nothing = jnp.zeros((NOPE, rows), BF)
+    for pair in range(q_ref.shape[1] // (2 * (NOPE + ROPE))):
+        turned = q_ref[:, pair * 384 : pair * 384 + 384].T
+        left = jnp.concatenate([turned[:NOPE], nothing], axis=0)
+        right = jnp.concatenate([nothing, turned[192 : 192 + NOPE]], axis=0)
+        both = jnp.concatenate([left, right], axis=1)
+        wk = wk_ref[:, pair * 2 * NOPE : (pair + 1) * 2 * NOPE]
+        latent = (jnp.dot(wk, both, preferred_element_type=F32) * scale).astype(BF)
+        group, head = divmod(2 * pair, heads)
+        at = group * PACKED
+        latent_ref[at : at + LATENT, head * rows : (head + 2) * rows] = latent
+        for side in range(2):
+            here = slice((head + side) * rows, (head + side + 1) * rows)
+            begin = side * 192 + NOPE
+            rotary = turned[begin : begin + ROPE].astype(F32) * scale
+            rounded = rotary.astype(BF)
+            latent_ref[at + LATENT : at + LATENT + ROPE, here] = rounded
+            rest = (rotary - rounded.astype(F32)).astype(BF)
+            latent_ref[at + LATENT + ROPE : at + LATENT + 2 * ROPE, here] = rest
+            latent_ref[at + LATENT + 2 * ROPE : at + PACKED, here] = flags
+        own = slice(pair * 2 * VDIM, (pair + 1) * 2 * VDIM)
+        wvt_ref[own, :] = wv_ref[:, own].T
 
 
 def prepare(queries, key_weight, value_weight, heads):
@@ -103,15 +112,15 @@
             jax.ShapeDtypeStruct((steps * PACKED, heads * rows), BF),
             jax.ShapeDtypeStruct((steps * heads * VDIM, depth), BF),
         ),
-        grid=(steps,),
+        grid=(steps // 2,),
         in_specs=[
-            pl.BlockSpec((rows, heads * (NOPE + ROPE)), lambda i: (0, i)),
-            pl.BlockSpec((depth, heads * NOPE), lambda i: (0, i)),
-            pl.BlockSpec((depth, heads * VDIM), lambda i: (0, i)),
+            pl.BlockSpec((rows, 2 * heads * (NOPE + ROPE)), lambda i: (0, i)),
+            pl.BlockSpec((depth, 2 * heads * NOPE), lambda i: (0, i)),
+            pl.BlockSpec((depth, 2 * heads * VDIM), lambda i: (0, i)),
         ],
         out_specs=(
-            pl.BlockSpec((PACKED, heads * rows), lambda i: (i, 0)),
-            pl.BlockSpec((heads * VDIM, depth), lambda i: (i, 0)),
+            pl.BlockSpec((2 * PACKED, heads * rows), lambda i: (i, 0)),
+            pl.BlockSpec((2 * heads * VDIM, depth), lambda i: (i, 0)),
         ),
         compiler_params=pltpu.CompilerParams(vmem_limit_bytes=58 * 1024 * 1024),
         cost_estimate=pl.CostEstimate(
@@ -181,7 +190,7 @@
     keys = rows_ref.shape[0]
     width = heads * tok_rows
     step = pl.program_id(0)
-    pieces = [slice(at, min(at + 384, keys)) for at in range(0, keys, 384)]
+    pieces = [slice(at, min(at + 576, keys)) for at in range(0, keys, 576)]
 
     def by_eights(value):
         return value.reshape(-1, 8, width)

time: 43.6 us -> 43.7 us (level)
  waiting for transfers between devices: 2.83 us -> 4.82 us
  Pallas kernels: 31.6 us -> 29.9 us
    ppermute x7, waiting for transfers between devices: 2.83 us -> 4.82 us  [move(): return lax.ppermute(value, AXES, pairs)]
    pallas_call x1, Pallas kernels: 10.8 us -> 8.79 us  [prepare(): pl.pallas_call(functools.partial(prepare_kernel, heads), out_shape=(jax.S...]
  transfers between devices with their start and end apart: 7 -> 7, of which waited for: 4 -> 4; matrix products, arithmetic and copies ran while one was open for 0% -> 0% of each run, Pallas kernels for 25% -> 20%
where the time goes in v15:
time: 43.7 us; the launch traced here: 43.5 us
  Pallas kernels  29.9 us (68%)
  starting transfers between devices  8.1 us (19%)
  waiting for transfers between devices  4.82 us (11%)
  between operations  0.67 us (2%)
    pallas_call x1, Pallas kernels, attend(): pl.pallas_call(functools.partial(attend_kernel, cfg, heads, steps), out_s...  19.3 us
    pallas_call x1, Pallas kernels, prepare(): pl.pallas_call(functools.partial(prepare_kernel, heads), out_shape=(jax.S...  8.79 us
    ppermute x7, starting transfers between devices, move(): return lax.ppermute(value, AXES, pairs)  8.1 us
    ppermute x7, waiting for transfers between devices, move(): return lax.ppermute(value, AXES, pairs)  4.82 us
    pallas_call x1, Pallas kernels, pack(): pl.pallas_call(pack_kernel, out_shape=jax.ShapeDtypeStruct((rows, 128), B...  1.83 us
  transfers between devices with their start and end apart: 7, of which 4 were waited for; matrix products, arithmetic and copies ran while one was open for 0% of the time, Pallas kernels for 20%

profile of v15, /device:TPU:0, one launch (start us, length us, event | category | flops | bytes accessed | tf_op | source)
XLA Modules:
  0.0 43.5 jit_solution(4562266815148279678)
XLA Ops:
  0.0 1.8 %pack_rows.1.rest_0_ = bf16[656,128]{1,0:T(8,128)(2,1)} custom-call(bf16[576,128]{1,0:T(8,128)(2,1)} %bitcast.2, bf16[16,576]{1,0:T(8,128)(2,1)} %cache_ref.1, f32[1,512]{1,0:T(1,128)} %bitcast.3), custom_call_target="tpu_custom_call" | custom-call | tf_op jit(solution)/shard_map/pack_rows/pallas_call | solution.py:56
  1.8 0.0 copy-start
  1.8 0.0 copy-start.1
  1.8 5.0 %collective-permute-start.2 = (bf16[656,128]{1,0:T(8,128)(2,1)}, bf16[656,128]{1,0:T(8,128)(2,1)S(1)}, u32[]{:S(2)}, u32[]{:S(2)}) collective-permute-start(bf16[656,128]{1,0:T(8,128)(2,1)} %pack_rows.1.rest_0_), channel_id=1, source_target_pairs={{0,12},{1,15},{2,14},{3,13},{4,0},{5,3},{6,2},{7,1},{8,4},{9,7},{1... | collective-permute-start | bytes 503816 | tf_op jit(solution)/shard_map/ppermute | solution.py:305
  6.9 0.0 collective-permute-start.1
  6.9 1.0 %collective-permute-start = (bf16[656,128]{1,0:T(8,128)(2,1)}, bf16[656,128]{1,0:T(8,128)(2,1)S(1)}, u32[]{:S(2)}, u32[]{:S(2)}) collective-permute-start(bf16[656,128]{1,0:T(8,128)(2,1)} %pack_rows.1.rest_0_), channel_id=1, source_target_pairs={{0,4},{1,7},{2,6},{3,5},{4,8},{5,11},{6,10},{7,9},{8,12},{9,15},{1... | collective-permute-start | bytes 503816 | tf_op jit(solution)/shard_map/ppermute | solution.py:305
  7.9 1.5 %collective-permute-start.3 = (bf16[656,128]{1,0:T(8,128)(2,1)}, bf16[656,128]{1,0:T(8,128)(2,1)S(1)}, u32[]{:S(2)}, u32[]{:S(2)}) collective-permute-start(bf16[656,128]{1,0:T(8,128)(2,1)} %pack_rows.1.rest_0_), channel_id=1, source_target_pairs={{0,2},{1,3},{2,0},{3,1},{4,6},{5,7},{6,4},{7,5},{8,10},{9,11},{10,... | collective-permute-start | bytes 503816 | tf_op jit(solution)/shard_map/ppermute | solution.py:305
  9.4 8.8 %prepare.1 = (bf16[6144,512]{1,0:T(8,128)(2,1)}, bf16[4096,512]{1,0:T(8,128)(2,1)}) custom-call(bf16[128,6144]{1,0:T(8,128)(2,1)} %q_ref.1, bf16[512,4096]{1,0:T(8,128)(2,1)} %wk_ref.1, bf16[512,4096]{1,0:T(8,128)(2,1)} %wv_ref.1), custom_call_target="tpu_custom_call" | custom-call | flops 536870912 | bytes 16777216 | tf_op jit(solution)/shard_map/prepare/pallas_call | solution.py:109
  18.2 0.0 collective-permute-done.2.rest_4_
  18.2 4.1 %collective-permute-done.1.rest_3_ = bf16[656,128]{1,0:T(8,128)(2,1)S(1)} collective-permute-done((bf16[656,128]{1,0:T(8,128)(2,1)}, bf16[656,128]{1,0:T(8,128)(2,1)S(1)}, u32[]{:S(2)}, u32[]{:S(2)}) %collective-permute-start.1) | collective-permute-done | bytes 167968 | tf_op jit(solution)/shard_map/ppermute | solution.py:305
  22.3 0.0 collective-permute-done.rest_2_
  22.3 0.0 collective-permute-start.4
  22.3 0.5 %collective-permute-start.5 = (bf16[656,128]{1,0:T(8,128)(2,1)S(1)}, bf16[656,128]{1,0:T(8,128)(2,1)S(1)}, u32[]{:S(2)}, u32[]{:S(2)}) collective-permute-start(bf16[656,128]{1,0:T(8,128)(2,1)S(1)} %collective-permute-done.1.rest_3_), channel_id=1, source_target_pairs={{0,1},{1,0},{2,3},{3,2},{4,5},{5,4},{6,7},{7,6},{8,9},{9,8},{10,11... | collective-permute-start | bytes 503816 | tf_op jit(solution)/shard_map/ppermute | solution.py:305
  22.8 0.0 collective-permute-start.6
  23.5 0.0 collective-permute-done.3.rest_1_
  23.5 0.2 collective-permute-done.4.rest_5_
  23.7 0.2 collective-permute-done.5.rest_6_
  23.9 0.3 collective-permute-done.6.rest_7_
  24.2 0.0 copy-done
  24.2 0.0 copy-done.1
  24.2 19.3 %attend.1 = bf16[128,4096]{1,0:T(8,128)(2,1)} custom-call(s32[8]{0:T(128)S(1)} %copy-done.1, s32[1]{0:T(128)S(6)} %copy.9.prefix_ref, bf16[6144,512]{1,0:T(8,128)(2,1)} %get-tuple-element.14.latent_ref, bf16[4096,512]{1,0:T(8,128)(2,1)} %get-tuple-element.15.wvt_ref, bf16[656,128]{1,0:T(8,128)(2,1)S(1)} %copy-done, ...), custom_call_target="tpu_custom_call" | custom-call | flops 12079595520 | bytes 8388608 | tf_op jit(solution)/shard_map/attend/pallas_call | solution.py:269
Async XLA Ops:
  1.8 22.4 %copy-start = (bf16[656,128]{1,0:T(8,128)(2,1)S(1)}, bf16[656,128]{1,0:T(8,128)(2,1)}, u32[]{:S(2)}) copy-start(bf16[656,128]{1,0:T(8,128)(2,1)} %pack_rows.1.rest_0_) | copy-start | bytes 503812
  1.8 22.4 %copy-start.1 = (s32[8]{0:T(128)S(1)}, s32[8]{0:T(128)}, u32[]{:S(2)}) copy-start(s32[8]{0:T(128)} %order_ref.1) | copy-start | bytes 100
  1.8 16.4 %collective-permute-start.2 = (bf16[656,128]{1,0:T(8,128)(2,1)}, bf16[656,128]{1,0:T(8,128)(2,1)S(1)}, u32[]{:S(2)}, u32[]{:S(2)}) collective-permute-start(bf16[656,128]{1,0:T(8,128)(2,1)} %pack_rows.1.rest_0_), channel_id=1, source_target_pairs={{0,12},{1,15},{2,14},{3,13},{4,0},{5,3},{6,2},{7,1},{8,4},{9,7},{1... | collective-permute-start | bytes 503816 | tf_op jit(solution)/shard_map/ppermute | solution.py:305
  6.9 15.4 %collective-permute-start.1 = (bf16[656,128]{1,0:T(8,128)(2,1)}, bf16[656,128]{1,0:T(8,128)(2,1)S(1)}, u32[]{:S(2)}, u32[]{:S(2)}) collective-permute-start(bf16[656,128]{1,0:T(8,128)(2,1)} %pack_rows.1.rest_0_), channel_id=1, source_target_pairs={{0,8},{1,11},{2,10},{3,9},{4,12},{5,15},{6,14},{7,13},{8,0},{9,3},... | collective-permute-start | bytes 503816 | tf_op jit(solution)/shard_map/ppermute | solution.py:305
  6.9 15.4 %collective-permute-start = (bf16[656,128]{1,0:T(8,128)(2,1)}, bf16[656,128]{1,0:T(8,128)(2,1)S(1)}, u32[]{:S(2)}, u32[]{:S(2)}) collective-permute-start(bf16[656,128]{1,0:T(8,128)(2,1)} %pack_rows.1.rest_0_), channel_id=1, source_target_pairs={{0,4},{1,7},{2,6},{3,5},{4,8},{5,11},{6,10},{7,9},{8,12},{9,15},{1... | collective-permute-start | bytes 503816 | tf_op jit(solution)/shard_map/ppermute | solution.py:305
  7.9 15.6 %collective-permute-start.3 = (bf16[656,128]{1,0:T(8,128)(2,1)}, bf16[656,128]{1,0:T(8,128)(2,1)S(1)}, u32[]{:S(2)}, u32[]{:S(2)}) collective-permute-start(bf16[656,128]{1,0:T(8,128)(2,1)} %pack_rows.1.rest_0_), channel_id=1, source_target_pairs={{0,2},{1,3},{2,0},{3,1},{4,6},{5,7},{6,4},{7,5},{8,10},{9,11},{10,... | collective-permute-start | bytes 503816 | tf_op jit(solution)/shard_map/ppermute | solution.py:305
  22.3 1.4 %collective-permute-start.4 = (bf16[656,128]{1,0:T(8,128)(2,1)S(1)}, bf16[656,128]{1,0:T(8,128)(2,1)S(1)}, u32[]{:S(2)}, u32[]{:S(2)}) collective-permute-start(bf16[656,128]{1,0:T(8,128)(2,1)S(1)} %collective-permute-done.rest_2_), channel_id=1, source_target_pairs={{0,1},{1,0},{2,3},{3,2},{4,5},{5,4},{6,7},{7,6},{8,9},{9,8},{10,11... | collective-permute-start | bytes 503816 | tf_op jit(solution)/shard_map/ppermute | solution.py:305
  22.3 1.6 %collective-permute-start.5 = (bf16[656,128]{1,0:T(8,128)(2,1)S(1)}, bf16[656,128]{1,0:T(8,128)(2,1)S(1)}, u32[]{:S(2)}, u32[]{:S(2)}) collective-permute-start(bf16[656,128]{1,0:T(8,128)(2,1)S(1)} %collective-permute-done.1.rest_3_), channel_id=1, source_target_pairs={{0,1},{1,0},{2,3},{3,2},{4,5},{5,4},{6,7},{7,6},{8,9},{9,8},{10,11... | collective-permute-start | bytes 503816 | tf_op jit(solution)/shard_map/ppermute | solution.py:305
  22.8 1.4 %collective-permute-start.6 = (bf16[656,128]{1,0:T(8,128)(2,1)S(1)}, bf16[656,128]{1,0:T(8,128)(2,1)S(1)}, u32[]{:S(2)}, u32[]{:S(2)}) collective-permute-start(bf16[656,128]{1,0:T(8,128)(2,1)S(1)} %collective-permute-done.2.rest_4_), channel_id=1, source_target_pairs={{0,1},{1,0},{2,3},{3,2},{4,5},{5,4},{6,7},{7,6},{8,9},{9,8},{10,11... | collective-permute-start | bytes 503816 | tf_op jit(solution)/shard_map/ppermute | solution.py:305
